TPU v7x, 256 devices: a whole 4x4x8 slice. The times are simulated.
256 devices in a mesh: dp: 4 (over y), ctx: 8 (over z), head: 8 (over x, core).
Axes of the slice: x: 4, y: 4, z: 8, core: 2. Of those that a mesh axis runs over, the one named last changes fastest.
Arguments:
- query: bfloat16 [4, 1024, 12288], P('dp', 'ctx', 'head'), may hold values from -180 to 180
- latent: bfloat16 [4, 1024, 576], P('dp', ('ctx', 'head')), may hold values from -6 to 6
- w_uk: bfloat16 [512, 8192], P(None, 'head'), may hold values from -0.25 to 0.25
- w_uv: bfloat16 [512, 8192], P(None, 'head'), may hold values from -0.25 to 0.25
- grad_out: bfloat16 [4, 1024, 8192], P('dp', 'ctx', 'head'), may hold values from -6 to 6
- block_order: int32 [16], replicated, may hold values from 0 to 15, as said below
Outputs:
- grad_query: bfloat16 [4, 1024, 12288], P('dp', 'ctx', 'head')
- grad_latent: float32 [4, 1024, 576], P('dp', ('ctx', 'head'))
- grad_w_uk: float32 [512, 8192], P(None, 'head')
- grad_w_uv: float32 [512, 8192], P(None, 'head')
Inputs may be any that keep to these rules, and one draw needn't show every extreme that they name: `block_order`: a permutation of the blocks in which storage blocks 2 r and 2 r + 1 hold blocks whose numbers add up to 15.
All inputs are finite; a program needn't handle non-finite values.
Results may differ from a plain program's by a relative error of at most 0.015.
Values may be sent and summed in bfloat16 or wider, within the bound.
No kernel may reach another device: no remote copies, remote signals or barrier semaphores. Data moves between devices by JAX's collectives and lax.ppermute only.
A program may use at most 64 MiB of HBM per device.

v0:
```python
import jax
import jax.numpy as jnp
from jax import lax
from jax.sharding import PartitionSpec as P

LAT = 512
ROPE = 64
NOPE = 128
VDIM = 128


def split_parts(wide):
    high_part = lax.optimization_barrier(wide.astype(jnp.bfloat16))
    low_part = (wide - high_part.astype(jnp.float32)).astype(jnp.bfloat16)
    return (high_part, low_part)


def contract_cols(left_wide, right):
    high_part, low_part = split_parts(left_wide)
    dims = (((1,), (1,)), ((), ()))
    first = lax.dot_general(high_part, right, dims, preferred_element_type=jnp.float32)
    return first + lax.dot_general(low_part, right, dims, preferred_element_type=jnp.float32)


def contract_rows(left, right_wide):
    high_part, low_part = split_parts(right_wide)
    dims = (((0,), (0,)), ((), ()))
    first = lax.dot_general(left, high_part, dims, preferred_element_type=jnp.float32)
    return first + lax.dot_general(left, low_part, dims, preferred_element_type=jnp.float32)


def project_rows(dkey_flat, dvalue_flat, drope, w_uk, w_uv):
    latent_part = contract_cols(dkey_flat, w_uk) + contract_cols(dvalue_flat, w_uv)
    return jnp.concatenate([latent_part, drope], axis=1)


def on_device(query, latent, w_uk, w_uv, grad_out, block_order):
    q_rows = query[0]
    d_rows = grad_out[0]
    lat = latent[0]
    rows = q_rows.shape[0]
    half = rows // 2
    heads_here = w_uk.shape[1] // NOPE
    width = NOPE + ROPE
    scale = width ** (-0.5)
    rank = lax.axis_index("ctx")
    lat_all = lax.all_gather(lat, ("ctx", "head"), axis=0, tiled=True)
    latent_c = lat_all[:, :LAT]
    keys_flat = jnp.dot(latent_c, w_uk, preferred_element_type=jnp.float32).astype(jnp.bfloat16)
    values_flat = jnp.dot(latent_c, w_uv, preferred_element_type=jnp.float32).astype(jnp.bfloat16)
    rope_all = lat_all[:, LAT:]
    seq = keys_flat.shape[0]
    keys_all = keys_flat.reshape(seq, heads_here, NOPE)
    values_all = values_flat.reshape(seq, heads_here, VDIM)
    q_heads = q_rows.reshape(rows, heads_here, width)
    d_heads = d_rows.reshape(rows, heads_here, VDIM)
    q_nope = q_heads[:, :, :NOPE]
    q_rope = q_heads[:, :, NOPE:]
    key_index = jnp.arange(seq, dtype=jnp.int32)
    key_pos = block_order[key_index // half] * half + key_index % half
    row_index = jnp.arange(rows, dtype=jnp.int32)
    own_block = block_order[2 * rank + row_index // half]
    row_pos = own_block * half + row_index % half
    allowed = (key_pos[None, :] <= row_pos[:, None])[None]
    scores = jnp.einsum("qhn,khn->hqk", q_nope, keys_all, preferred_element_type=jnp.float32)
    scores = scores + jnp.einsum(
        "qhr,kr->hqk", q_rope, rope_all, preferred_element_type=jnp.float32
    )
    scores = scores * scale
    masked = jnp.where(allowed, scores, -jnp.inf)
    top = jnp.max(masked, axis=2, keepdims=True)
    weights = jnp.where(allowed, jnp.exp(masked - top), 0.0)
    probs = weights / jnp.sum(weights, axis=2, keepdims=True)
    probs_b = probs.astype(jnp.bfloat16)
    outputs = jnp.einsum("hqk,khv->qhv", probs_b, values_all, preferred_element_type=jnp.float32)
    drows = jnp.sum(d_heads.astype(jnp.float32) * outputs, axis=2).T
    dprob = jnp.einsum("qhv,khv->hqk", d_heads, values_all, preferred_element_type=jnp.float32)
    dscore = (probs * (dprob - drows[:, :, None])).astype(jnp.bfloat16)
    dq_nope = (
        jnp.einsum("hqk,khn->qhn", dscore, keys_all, preferred_element_type=jnp.float32) * scale
    )
    dq_rope = (
        jnp.einsum("hqk,kr->qhr", dscore, rope_all, preferred_element_type=jnp.float32) * scale
    )
    dkey_all = (
        jnp.einsum("hqk,qhn->khn", dscore, q_nope, preferred_element_type=jnp.float32) * scale
    )
    drope_all = (
        jnp.einsum("hqk,qhr->kr", dscore, q_rope, preferred_element_type=jnp.float32) * scale
    )
    dvalue_all = jnp.einsum("hqk,qhv->khv", probs_b, d_heads, preferred_element_type=jnp.float32)
    grad_q = jnp.concatenate([dq_nope, dq_rope], axis=2)
    grad_query = grad_q.reshape(1, rows, heads_here * width).astype(jnp.bfloat16)
    dkey_flat = dkey_all.reshape(seq, heads_here * NOPE)
    dvalue_flat = dvalue_all.reshape(seq, heads_here * VDIM)
    grad_latent = lax.psum_scatter(
        project_rows(dkey_flat, dvalue_flat, drope_all, w_uk, w_uv),
        ("ctx", "head"),
        scatter_dimension=0,
        tiled=True,
    )
    grad_uk = contract_rows(latent_c, dkey_flat)
    grad_uv = contract_rows(latent_c, dvalue_flat)
    grad_w_uk, grad_w_uv = lax.psum((grad_uk, grad_uv), ("dp", "ctx"))
    return (grad_query, grad_latent[None], grad_w_uk, grad_w_uv)


def solution(mesh):
    return jax.shard_map(
        on_device,
        mesh=mesh,
        in_specs=(
            P("dp", "ctx", "head"),
            P("dp", ("ctx", "head"), None),
            P(None, "head"),
            P(None, "head"),
            P("dp", "ctx", "head"),
            P(),
        ),
        out_specs=(
            P("dp", "ctx", "head"),
            P("dp", ("ctx", "head"), None),
            P(None, "head"),
            P(None, "head"),
        ),
        check_vma=False,
    )
```

profile of v0, /device:TPU:32, one launch (start us, length us, event | category | flops | bytes accessed | tf_op | source)
XLA Modules:
  0.0 496.1 jit_solution(8960798203634442078)
XLA Ops:
  8.0 1.1 copy.50
  9.1 1.3 copy.47
  10.7 1.9 fusion.35
  12.7 10.1 %fusion.31 = s32[128]{0:T(128)S(1)} fusion(s32[]{:T(128)} %bitcast.11, s32[]{:T(128)} %bitcast.12, s32[]{:T(128)} %bitcast.13, s32[]{:T(128)} %bitcast.14, s32[]{:T(128)} %bitcast.15, s32[]{:T(128)} %bitcast.17, s32[]{:T(128)} %bitcast.16, s32[]{:T(128)} %bitcast.2, s32[]{:T(128)} %bitcast.3, s32[]{:T(128)} %bitcast.4, s32[]{:T(128)} %bitcast.5, s32[]{:T(128)} %bitcast.6, ...), kind=kLoop, calls=%fused_computation.98 | loop fusion | flops 6400 | bytes 580 | tf_op jit(solution)/shard_map/add | solution.py:63
  22.7 4.3 compare_select_fusion.1
  27.1 5.7 %fusion.27 = s32[1024]{0:T(1024)S(1)} fusion(pred[1024]{0:T(1024)(128)(4,1)S(1)} %compare_reduce_fusion, pred[1024]{0:T(1024)(128)(4,1)S(1)} %compare_reduce_fusion.1, pred[1024]{0:T(1024)(128)(4,1)S(1)} %compare_reduce_fusion.2, pred[1024]{0:T(1024)(128)(4,1)S(1)} %compare_reduce_fusion.3, pred[1024]{0:T(1024)(128)(4,1)S(1)} %compare_reduce_fusion.4, ...), kind=kLoop, calls=%fused_computation.71 | loop fusion | flops 17408 | bytes 17444 | tf_op jit(solution)/shard_map/add | solution.py:60
  33.0 56.0 %all-gather.3.cloned.1.call-done = bf16[1,1024,576]{2,1,0:T(8,128)(2,1)} async-done(((bf16[1,16,576]{2,1,0:T(8,128)(2,1)}), bf16[1,1024,576]{2,1,0:T(8,128)(2,1)}) %all-gather.3.cloned.1.call-update) | async-done | bytes 1179664 | tf_op jit(solution)/shard_map/all_gather | solution.py:47
  89.0 1.6 copy.46
  90.6 4.3 convolution_convert_fusion
  94.9 1.3 convolution_convert_fusion.1
  96.2 1.3 copy-done.1
  97.5 2.7 fusion.22
  100.3 5.8 %fusion.36 = (f32[8,128]{1,0:T(8,128)S(1)}, f32[8,128,1024]{1,2,0:T(8,128)}) fusion(pred[128,1024]{0,1:T(8,128)(4,1)S(1)} %broadcast_compare_fusion, f32[8,1024,128]{2,1,0:T(8,128)} %fusion.22, bf16[128,8,192]{0,2,1:T(8,128)(2,1)S(1)} %bitcast.190, bf16[1024,576]{0,1:T(8,128)(2,1)S(1)} %bitcast.196), kind=kOutput, calls=%fused_computation.103 | convolution fusion | flops 140510208 | bytes 8916992 | tf_op jit(solution)/shard_map/sub | solution.py:72
  106.1 2.7 fusion.6
  109.7 1.5 copy-done.6
  111.2 2.1 fusion.3
  117.2 2.7 fusion.15
  119.9 1.3 fusion.42
  123.0 1.3 fusion.40
  124.4 1.3 fusion.41
  125.7 1.4 add_add_fusion
  127.1 1.5 pad_maximum_fusion
  128.8 3.3 fusion.18
  132.3 2.7 add_bitcast_fusion
  134.9 2.6 add_bitcast_fusion.1
  139.5 1.5 fusion.13
  141.9 0.9 copy.60
  142.8 172.5 %all-reduce.5.cloned.1.call-done = f32[1024,576]{0,1:T(8,128)} async-done(((f32[1024,576]{0,1:T(8,128)}), f32[1024,576]{0,1:T(8,128)}) %all-reduce.5.cloned.1.call-update) | async-done | bytes 2359312
  315.3 1.1 dynamic-slice_bitcast_fusion
  317.2 167.6 %all-reduce.7.cloned.1.call-done = (f32[512,1024]{0,1:T(8,128)}, f32[512,1024]{0,1:T(8,128)}) async-done(((f32[512,1024]{0,1:T(8,128)}, f32[512,1024]{0,1:T(8,128)}), (f32[512,1024]{0,1:T(8,128)}, f32[512,1024]{0,1:T(8,128)})) %all-reduce.7.cloned.1.call-update) | async-done | bytes 4194320 | tf_op jit(solution)/shard_map/psum | solution.py:104
  484.8 3.0 copy.62
  487.8 1.8 copy.63
  (64 shorter events, 11.2 us)
Async XLA Ops:
  7.2 87.7 %copy-start = (bf16[512,1024]{1,0:T(8,128)(2,1)S(1)}, bf16[512,1024]{1,0:T(8,128)(2,1)}, u32[]{:S(2)}) copy-start(bf16[512,1024]{1,0:T(8,128)(2,1)} %param.8) | copy-start | bytes 3145732
  7.2 81.9 %all-gather.3.cloned.1.call-start = ((), (), s32[]{:S(2)}) async-start(), calls=%async_computation | async-start | bytes 1331200 | tf_op jit(solution)/shard_map/all_gather | solution.py:47
  7.9 307.4 %all-reduce.5.cloned.1.call-start = ((), (), s32[]{:S(2)}) async-start(), calls=%async_computation.1 | async-start | bytes 4718592
  9.1 99.7 %copy-start.13 = (bf16[1,128,1024]{1,2,0:T(8,128)(2,1)}, bf16[1,128,1024]{1,2,0:T(8,128)(2,1)S(1)}, u32[]{:S(2)}) copy-start(bf16[1,128,1024]{1,2,0:T(8,128)(2,1)S(1)} %copy.50) | copy-start | bytes 786436
  90.6 9.7 %copy-start.10 = (bf16[1,1024,576]{1,2,0:T(8,128)(2,1)}, bf16[1,1024,576]{1,2,0:T(8,128)(2,1)S(1)}, u32[]{:S(2)}) copy-start(bf16[1,1024,576]{1,2,0:T(8,128)(2,1)S(1)} %copy.46) | copy-start | bytes 3538948
  96.2 1.3 copy-start.1
  106.1 2.9 copy-start.16
  109.0 2.2 copy-start.6
  114.0 1.0 copy-start.14
  116.0 1.3 copy-start.11
  117.2 8.4 %copy-start.4 = (bf16[1024,1024]{0,1:T(8,128)(2,1)}, bf16[1024,1024]{0,1:T(8,128)(2,1)S(1)}, u32[]{:S(2)}) copy-start(bf16[1024,1024]{0,1:T(8,128)(2,1)S(1)} %fusion.1) | copy-start | bytes 6291460
  117.2 2.7 copy-start.15
  121.6 1.4 copy-start.3
  123.0 1.4 copy-start.8
  128.7 356.1 %all-reduce.7.cloned.1.call-start = ((), (), s32[]{:S(2)}) async-start(), calls=%async_computation.2 | async-start | bytes 8388608 | tf_op jit(solution)/shard_map/psum | solution.py:104
  128.7 3.3 copy-start.5
  128.8 3.3 copy-start.12
  128.8 3.5 copy-start.18
  132.3 2.7 copy-start.9
  137.5 0.7 copy-start.17
  139.5 1.7 copy-start.2
  484.8 3.0 copy-start.7
Sparse Core Ops, SparseCore 0:
  10.7 78.2 all-gather.2
  128.8 186.4 all-reduce.4
  319.6 165.0 all-reduce.6
where the time goes:
time: 498 us; the launch traced here: 496 us
  waiting for transfers between devices  397 us (80%)
  matrix products  37.8 us (8%)
  other arithmetic  27.3 us (5%)
  local copies, waits for them, and re-layouts  19.3 us (4%)
  between operations  14.7 us (3%)
    unnamed x4, waiting for transfers between devices  173 us
    psum x1, waiting for transfers between devices, on_device(): grad_w_uk, grad_w_uv = lax.psum((grad_uk, grad_uv), ('dp', 'ctx'))  168 us
    all_gather x1, waiting for transfers between devices, on_device(): lat_all = lax.all_gather(lat, ('ctx', 'head'), axis=0, tiled=True)  56 us
    unnamed x45, local copies, waits for them, and re-layouts  14.7 us
    add x1, other arithmetic, on_device(): row_pos = own_block * half + row_index % half  10.1 us
  transfers between devices with their start and end apart: 3, of which 3 were waited for; matrix products, arithmetic and copies ran while one was open for 8% of the time, Pallas kernels for 0%

commit v1 on v0

v1 whole, which is shorter than its diff:
```python
import functools

import jax
import jax.numpy as jnp
from jax import lax
from jax.experimental import pallas as pl
from jax.experimental.pallas import tpu as pltpu
from jax.sharding import PartitionSpec as P

LAT = 512
ROPE = 64
NOPE = 128
VDIM = 128
WIDTH = NOPE + ROPE
HALF = 64
SUB = 16
TILE = 256
BF = jnp.bfloat16
F32 = jnp.float32
VMEM = pl.BlockSpec(memory_space=pltpu.VMEM)

ROW_DO = NOPE
ROW_ROPE = ROW_DO + VDIM
ROW_LAT = ROW_ROPE + ROPE
ROW_LROPE = ROW_LAT + SUB * (LAT // 128)
ROWS_IN = ROW_LROPE + SUB
ROW_GROPE = NOPE
ROW_GL = ROW_GROPE + ROPE
ROW_GLROPE = ROW_GL + SUB * (LAT // 128)
ROWS_OUT = ROW_GLROPE + SUB


def dot_nn(a, b):
    return lax.dot_general(a, b, (((1,), (0,)), ((), ())), preferred_element_type=F32)


def dot_nt(a, b):
    return lax.dot_general(a, b, (((1,), (1,)), ((), ())), preferred_element_type=F32)


def dot_tn(a, b):
    return lax.dot_general(a, b, (((0,), (0,)), ((), ())), preferred_element_type=F32)


def pack_kernel(q_ref, d_ref, lat_ref, out_ref):
    n = out_ref.shape[0]
    for h in range(n):
        q = q_ref[:, h * WIDTH : (h + 1) * WIDTH]
        out_ref[h, 0:ROW_DO, :] = q[:, :NOPE]
        out_ref[h, ROW_DO:ROW_ROPE, :] = d_ref[:, h * VDIM : (h + 1) * VDIM]
        rope = q[:, NOPE:]
        out_ref[h, ROW_ROPE:ROW_LAT, :] = jnp.concatenate([rope[:HALF], rope[HALF:]], axis=1)
        for j in range(LAT // 128):
            out_ref[h, ROW_LAT + SUB * j : ROW_LAT + SUB * (j + 1), :] = lat_ref[
                :, 128 * j : 128 * (j + 1)
            ]
        rope_k = lat_ref[:, LAT:]
        out_ref[h, ROW_LROPE:ROWS_IN, :] = jnp.concatenate([rope_k, rope_k], axis=1)


def attention_kernel(
    order_ref, rank_ref, in_ref, lat_in_ref, wk_ref, wv_ref,
    gl_ref, gq_ref, gw_ref,
    lat_s, k_s, v_s, q_s, d_s, dk_s, dv_s, dq_s, gl_s,
):
    blocks = in_ref.shape[0]
    parts = lat_in_ref.shape[0]
    seq = lat_s.shape[0]
    scale = WIDTH ** (-0.5)
    per_half = HALF // SUB

    def place(block):
        return pl.multiple_of(order_ref[block] * HALF, HALF)

    for s in range(blocks):
        for half in range(2):
            base = place(2 * s + half)
            rows = pl.ds(base, HALF)
            lo = half * HALF
            q_s[rows, :NOPE] = in_ref[s, lo : lo + HALF, :]
            q_s[rows, NOPE:] = in_ref[s, ROW_ROPE:ROW_LAT, half * ROPE : (half + 1) * ROPE]
            d_s[rows, :] = in_ref[s, ROW_DO + lo : ROW_DO + lo + HALF, :]
            for i in range(per_half):
                p = half * per_half + i
                sub = pl.ds(pl.multiple_of(base + i * SUB, SUB), SUB)
                for j in range(LAT // 128):
                    lat_s[sub, 128 * j : 128 * (j + 1)] = lat_in_ref[p, s, SUB * j : SUB * (j + 1), :]
                k_s[sub, NOPE:] = lat_in_ref[p, s, SUB * (LAT // 128) :, :ROPE]

    w_both = jnp.concatenate([wk_ref[...], wv_ref[...]], axis=1)
    for t in range(seq // TILE):
        rows = slice(t * TILE, (t + 1) * TILE)
        both = dot_nn(lat_s[rows, :], w_both)
        k_s[rows, :NOPE] = both[:, :NOPE].astype(BF)
        v_s[rows, :] = both[:, NOPE:].astype(BF)

    dk_s[...] = jnp.zeros_like(dk_s)
    dv_s[...] = jnp.zeros_like(dv_s)
    for t in range(seq // TILE):
        rows = slice(t * TILE, (t + 1) * TILE)
        width = (t + 1) * TILE
        q = q_s[rows, :]
        d = d_s[rows, :]
        k = k_s[:width, :]
        scores = dot_nt(k, q) * scale
        key_pos = lax.broadcasted_iota(jnp.int32, (width, TILE), 0)
        row_pos = lax.broadcasted_iota(jnp.int32, (width, TILE), 1) + t * TILE
        masked = jnp.where(key_pos <= row_pos, scores, -jnp.inf)
        top = jnp.max(masked, axis=0, keepdims=True)
        weights = jnp.exp(masked - top)
        probs = weights / jnp.sum(weights, axis=0, keepdims=True)
        probs_b = probs.astype(BF)
        dprob = dot_nt(v_s[:width, :], d)
        drow = jnp.sum(probs_b.astype(F32) * dprob, axis=0, keepdims=True)
        dscore = (probs * (dprob - drow)).astype(BF)
        dq_s[rows, :] = (dot_tn(dscore, k) * scale).astype(BF)
        dk_s[:width, :] += dot_nn(dscore, q)
        dv_s[:width, :] += dot_nn(probs_b, d)

    dk = dk_s[...] * scale
    dkv = jnp.concatenate([dk[:, :NOPE], dv_s[...]], axis=1).astype(BF)
    gw = dot_tn(lat_s[...], dkv).astype(BF)
    n = gw_ref.shape[0]
    share = LAT // n
    for i in range(n):
        gw_ref[i] = gw[i * share : (i + 1) * share]
    gl_s[:, :LAT] = dot_nt(dkv, w_both).astype(BF)
    gl_s[:, LAT:] = dk[:, NOPE:].astype(BF)

    for s in range(blocks):
        for half in range(2):
            base = place(2 * s + half)
            rows = pl.ds(base, HALF)
            lo = half * HALF
            gq_ref[s, lo : lo + HALF, :] = dq_s[rows, :NOPE]
            gq_ref[s, ROW_GROPE:ROW_GL, half * ROPE : (half + 1) * ROPE] = dq_s[rows, NOPE:]
            for i in range(per_half):
                p = half * per_half + i
                sub = pl.ds(pl.multiple_of(base + i * SUB, SUB), SUB)
                for j in range(LAT // 128):
                    gl_ref[p, s, SUB * j : SUB * (j + 1), :] = gl_s[sub, 128 * j : 128 * (j + 1)]
                rope = gl_s[sub, LAT:]
                gl_ref[p, s, SUB * (LAT // 128) :, :] = jnp.concatenate([rope, rope], axis=1)


def unpack_kernel(in_ref, gq_ref, gl_ref):
    n = in_ref.shape[0]
    for h in range(n):
        rope = in_ref[h, ROW_GROPE:ROW_GL, :]
        rope = jnp.concatenate([rope[:, :ROPE], rope[:, ROPE:]], axis=0)
        gq_ref[:, h * WIDTH : (h + 1) * WIDTH] = jnp.concatenate([in_ref[h, :NOPE, :], rope], axis=1)
    for j in range(LAT // 128):
        part = in_ref[:, ROW_GL + SUB * j : ROW_GL + SUB * (j + 1), :].astype(F32)
        gl_ref[:, 128 * j : 128 * (j + 1)] = jnp.sum(part, axis=0)
    part = in_ref[:, ROW_GLROPE:ROWS_OUT, :ROPE].astype(F32)
    gl_ref[:, LAT:] = jnp.sum(part, axis=0)


def on_device(n_dp, n_ctx, n_head, query, latent, w_uk, w_uv, grad_out, block_order):
    seq = n_ctx * n_head * SUB
    rows = query.shape[1]
    rank = lax.axis_index("ctx").astype(jnp.int32).reshape(1)
    packed = pl.pallas_call(
        pack_kernel,
        out_shape=jax.ShapeDtypeStruct((n_ctx, ROWS_IN, 128), BF),
        in_specs=[VMEM] * 3,
        out_specs=VMEM,
        name="pack",
    )(query[0], grad_out[0], latent[0])
    mine = lax.all_to_all(packed, "ctx", 0, 0, tiled=True)
    lat_mine = mine[:, ROW_LAT:ROWS_IN, :]
    lat_rows = lat_mine.shape[1]
    lat_all = lax.all_to_all(
        jnp.broadcast_to(lat_mine[None], (n_head,) + lat_mine.shape), "head", 0, 0, tiled=True
    )
    full = lambda shape: pl.BlockSpec(shape, lambda i, order, rank: (0,) * len(shape))
    head_cols = pl.BlockSpec((LAT, NOPE), lambda i, order, rank: (0, rank[0]))
    gl_part, gq_part, gw_part = pl.pallas_call(
        attention_kernel,
        grid_spec=pltpu.PrefetchScalarGridSpec(
            num_scalar_prefetch=2,
            grid=(1,),
            in_specs=[full(mine.shape), full(lat_all.shape), head_cols, head_cols],
            out_specs=[
                full((n_head, n_ctx, lat_rows, 128)),
                full((n_ctx, ROW_GL, 128)),
                full((n_dp, LAT // n_dp, NOPE + VDIM)),
            ],
            scratch_shapes=[
                pltpu.VMEM((seq, LAT), BF),
                pltpu.VMEM((seq, WIDTH), BF),
                pltpu.VMEM((seq, VDIM), BF),
                pltpu.VMEM((seq, WIDTH), BF),
                pltpu.VMEM((seq, VDIM), BF),
                pltpu.VMEM((seq, WIDTH), F32),
                pltpu.VMEM((seq, VDIM), F32),
                pltpu.VMEM((seq, WIDTH), BF),
                pltpu.VMEM((seq, LAT + ROPE), BF),
            ],
        ),
        out_shape=[
            jax.ShapeDtypeStruct((n_head, n_ctx, lat_rows, 128), BF),
            jax.ShapeDtypeStruct((n_ctx, ROW_GL, 128), BF),
            jax.ShapeDtypeStruct((n_dp, LAT // n_dp, NOPE + VDIM), BF),
        ],
        compiler_params=pltpu.CompilerParams(vmem_limit_bytes=48 * 1024 * 1024),
        cost_estimate=pl.CostEstimate(
            flops=3 * 10**9, bytes_accessed=5 * 10**6, transcendentals=seq * seq
        ),
        name="attention_backward",
    )(block_order, rank, mine, lat_all, w_uk, w_uv)

    gw_sum = jnp.sum(lax.all_to_all(gw_part, "dp", 0, 0, tiled=True).astype(F32), axis=0).astype(BF)
    gw_ctx = lax.all_to_all(
        jnp.broadcast_to(gw_sum[None], (n_ctx,) + gw_sum.shape), "ctx", 0, 0, tiled=True
    )
    gw_all = lax.all_to_all(
        jnp.broadcast_to(gw_ctx[None], (n_dp,) + gw_ctx.shape), "dp", 0, 0, tiled=True
    )
    gw_all = gw_all.transpose(0, 2, 1, 3).reshape(LAT, n_ctx, NOPE + VDIM).astype(F32)
    grad_w_uk = gw_all[:, :, :NOPE].reshape(LAT, n_ctx * NOPE)
    grad_w_uv = gw_all[:, :, NOPE:].reshape(LAT, n_ctx * VDIM)

    gl_head = jnp.sum(
        lax.all_to_all(gl_part, "head", 0, 0, tiled=True).astype(F32), axis=0
    ).astype(BF)
    back = lax.all_to_all(jnp.concatenate([gq_part, gl_head], axis=1), "ctx", 0, 0, tiled=True)
    grad_query, grad_latent = pl.pallas_call(
        unpack_kernel,
        out_shape=[
            jax.ShapeDtypeStruct((rows, n_ctx * WIDTH), BF),
            jax.ShapeDtypeStruct((SUB, LAT + ROPE), F32),
        ],
        in_specs=[VMEM],
        out_specs=[VMEM, VMEM],
        name="unpack",
    )(back)
    return (grad_query[None], grad_latent[None], grad_w_uk, grad_w_uv)


def solution(mesh):
    sizes = mesh.shape
    return jax.shard_map(
        functools.partial(on_device, sizes["dp"], sizes["ctx"], sizes["head"]),
        mesh=mesh,
        in_specs=(
            P("dp", "ctx", "head"),
            P("dp", ("ctx", "head"), None),
            P(None, "head"),
            P(None, "head"),
            P("dp", "ctx", "head"),
            P(),
        ),
        out_specs=(
            P("dp", "ctx", "head"),
            P("dp", ("ctx", "head"), None),
            P(None, "head"),
            P(None, "head"),
        ),
        check_vma=False,
    )
```

time: 498 us -> 182 us (0.37)
  waiting for transfers between devices: 397 us -> 93.2 us
  blocking collectives: 0 us -> 41.9 us
  matrix products: 37.8 us -> 0 us
  other arithmetic: 27.3 us -> 1.43 us
  starting transfers between devices: 0.12 us -> 21.2 us
  between operations: 14.7 us -> 0.7 us
  Pallas kernels: 0 us -> 10.8 us
  local copies, waits for them, and re-layouts: 19.3 us -> 9.6 us
    unnamed x4 -> x0, waiting for transfers between devices: 173 us -> none
    psum x1 -> x0, waiting for transfers between devices: 168 us -> none  [on_device(): grad_w_uk, grad_w_uv = lax.psum((grad_uk, grad_uv), ('dp', 'ctx'))]
    all_to_all x0 -> x5, waiting for transfers between devices: none -> 93.2 us  [the longest x1 23.7 us: on_device(): lax.all_to_all(jnp.broadcast_to(gw_ctx[None], (n_dp,) + gw_ctx.shape), 'd...]
    all_gather x1 -> x0, waiting for transfers between devices: 56 us -> none  [on_device(): lat_all = lax.all_gather(lat, ('ctx', 'head'), axis=0, tiled=True)]
    all_to_all x0 -> x2, blocking collectives: none -> 41.9 us  [the longest x1 30.9 us: on_device(): mine = lax.all_to_all(packed, 'ctx', 0, 0, tiled=True)]
    dot_general x18 -> x0, matrix products: 32 us -> none  [the longest x2 5.95 us: contract_rows(): lax.dot_general(left, high_part, dims, preferred_element_type=jnp.float32)]
    all_to_all x0 -> x5, starting transfers between devices: none -> 21.2 us  [the longest x1 4.89 us: on_device(): lax.all_to_all(jnp.concatenate([gq_part, gl_head], axis=1), 'ctx', 0, 0,...]
    add x2 -> x0, other arithmetic: 15.8 us -> none  [the longest x1 10.1 us: on_device(): row_pos = own_block * half + row_index % half]
  transfers between devices with their start and end apart: 3 -> 5, of which waited for: 3 -> 5; matrix products, arithmetic and copies ran while one was open for 8% -> 1% of each run, Pallas kernels for 0% -> 1%
where the time goes in v1:
time: 182 us; the launch traced here: 179 us
  waiting for transfers between devices  93.2 us (51%)
  blocking collectives  41.9 us (23%)
  starting transfers between devices  21.2 us (12%)
  Pallas kernels  10.8 us (6%)
  local copies, waits for them, and re-layouts  9.6 us (5%)
    all_to_all x1, blocking collectives, on_device(): mine = lax.all_to_all(packed, 'ctx', 0, 0, tiled=True)  30.9 us
    all_to_all x1, waiting for transfers between devices, on_device(): lax.all_to_all(jnp.broadcast_to(gw_ctx[None], (n_dp,) + gw_ctx.shape), 'd...  23.7 us
    all_to_all x1, waiting for transfers between devices, on_device(): lax.all_to_all(jnp.broadcast_to(lat_mine[None], (n_head,) + lat_mine.shap...  18.8 us
    all_to_all x1, waiting for transfers between devices, on_device(): lax.all_to_all(gl_part, 'head', 0, 0, tiled=True).astype(F32)  18.6 us
    all_to_all x1, waiting for transfers between devices, on_device(): lax.all_to_all(jnp.concatenate([gq_part, gl_head], axis=1), 'ctx', 0, 0,...  16.9 us
    all_to_all x1, waiting for transfers between devices, on_device(): lax.all_to_all(jnp.broadcast_to(gw_sum[None], (n_ctx,) + gw_sum.shape), '...  15.1 us
    all_to_all x1, blocking collectives, on_device(): lax.all_to_all(gw_part, 'dp', 0, 0, tiled=True).astype(F32)  10.9 us
    pallas_call x1, Pallas kernels, on_device(): pl.pallas_call(attention_kernel, grid_spec=pltpu.PrefetchScalarGridSpec(n...  6.64 us
  transfers between devices with their start and end apart: 5, of which 5 were waited for; matrix products, arithmetic and copies ran while one was open for 1% of the time, Pallas kernels for 1%

profile of v1, /device:TPU:32, one launch (start us, length us, event | category | flops | bytes accessed | tf_op | source)
XLA Modules:
  0.0 178.8 jit_solution(10143330120613875754)
XLA Ops:
  0.6 2.2 %pack.1 = bf16[8,400,128]{2,1,0:T(8,128)(2,1)} custom-call(bf16[128,1536]{1,0:T(8,128)(2,1)} %bitcast.18, bf16[128,1024]{1,0:T(8,128)(2,1)} %bitcast.19, bf16[16,576]{1,0:T(8,128)(2,1)} %bitcast.20), custom_call_target="tpu_custom_call" | custom-call | tf_op jit(solution)/shard_map/pack/pallas_call | solution.py:163
  2.8 30.9 %all_to_all.35.in_ref = bf16[8,400,128]{2,1,0:T(8,128)(2,1)S(1)} all-to-all(bf16[8,400,128]{2,1,0:T(8,128)(2,1)} %pack.1), channel_id=1, replica_groups=mesh['dp'=4,'ctx'=8,'head'=8] {'ctx'}, dimensions={0} | all-to-all | bytes 1638400 | tf_op jit(solution)/shard_map/all_to_all | solution.py:170
  33.7 0.0 copy-start.2
  33.7 1.2 broadcast_in_dim.10
  35.0 4.3 %all-to-all-start.1 = ((bf16[8,8,80,128]{3,2,1,0:T(8,128)(2,1)}), bf16[8,8,80,128]{3,2,1,0:T(8,128)(2,1)S(1)}, u32[]{:S(2)}, u32[]{:S(2)}) async-start(bf16[8,8,80,128]{3,2,1,0:T(8,128)(2,1)} %broadcast_in_dim.10), calls=%async_computation.1 | async-start | bytes 2621440 | tf_op jit(solution)/shard_map/all_to_all | solution.py:173
  39.3 18.8 %all-to-all-done.1.lat_in_ref = bf16[8,8,80,128]{3,2,1,0:T(8,128)(2,1)S(1)} async-done(((bf16[8,8,80,128]{3,2,1,0:T(8,128)(2,1)}), bf16[8,8,80,128]{3,2,1,0:T(8,128)(2,1)S(1)}, u32[]{:S(2)}, u32[]{:S(2)}) %all-to-all-start.1) | async-done | bytes 1310752 | tf_op jit(solution)/shard_map/all_to_all | solution.py:173
  58.1 0.0 copy-done.2
  58.1 0.0 copy-start
  58.1 1.2 copy-done
  59.3 0.0 copy-start.1
  59.3 1.2 copy-done.1
  60.5 6.6 %attention_backward.1 = (bf16[8,8,80,128]{3,2,1,0:T(8,128)(2,1)}, bf16[8,192,128]{2,1,0:T(8,128)(2,1)S(1)}, bf16[4,128,256]{2,1,0:T(8,128)(2,1)S(1)}) custom-call(s32[16]{0:T(128)S(1)} %copy-done.2, s32[1]{0:T(128)} %bitcast.rank_ref, bf16[8,400,128]{2,1,0:T(8,128)(2,1)S(1)} %all_to_all.35.in_ref, bf16[8,8,80,128]{3,2,1,0:T(8,128)(2,1)S(1)} %all-to-all-done.1.lat_in_ref, ...), custom_call_target="tpu_custom_call" | custom-call | flops 3000000000 | bytes 5000000 | tf_op jit(solution)/shard_map/attention_backward/pallas_call | solution.py:178
  67.1 10.9 %all_to_all.36 = bf16[4,128,256]{2,1,0:T(8,128)(2,1)S(1)} all-to-all(bf16[4,128,256]{2,1,0:T(8,128)(2,1)S(1)} %get-tuple-element.13), channel_id=1, replica_groups=mesh['dp'=4,'ctx'=8,'head'=8] {'dp'}, dimensions={0} | all-to-all | bytes 524288 | tf_op jit(solution)/shard_map/all_to_all | solution.py:213
  78.1 3.6 %all-to-all-start.2 = ((bf16[8,8,80,128]{3,2,1,0:T(8,128)(2,1)}), bf16[8,8,80,128]{3,2,1,0:T(8,128)(2,1)S(1)}, u32[]{:S(2)}, u32[]{:S(2)}) async-start(bf16[8,8,80,128]{3,2,1,0:T(8,128)(2,1)} %get-tuple-element.10), calls=%async_computation.2 | async-start | bytes 2621440 | tf_op jit(solution)/shard_map/all_to_all | solution.py:225
  81.7 18.6 %all-to-all-done.2 = bf16[8,8,80,128]{3,2,1,0:T(8,128)(2,1)S(1)} async-done(((bf16[8,8,80,128]{3,2,1,0:T(8,128)(2,1)}), bf16[8,8,80,128]{3,2,1,0:T(8,128)(2,1)S(1)}, u32[]{:S(2)}, u32[]{:S(2)}) %all-to-all-start.2) | async-done | bytes 1310752 | tf_op jit(solution)/shard_map/all_to_all | solution.py:225
  100.3 0.8 broadcast_in_dim.13
  101.2 4.8 %all-to-all-start.5 = ((bf16[8,128,256]{2,1,0:T(8,128)(2,1)}), bf16[8,128,256]{2,1,0:T(8,128)(2,1)S(1)}, u32[]{:S(2)}, u32[]{:S(2)}) async-start(bf16[8,128,256]{2,1,0:T(8,128)(2,1)} %broadcast_in_dim.13), calls=%async_computation.5 | async-start | bytes 1048576 | tf_op jit(solution)/shard_map/all_to_all | solution.py:214
  106.0 0.2 reduce_sum.24
  106.2 0.8 pad_maximum_fusion
  107.1 15.1 %all-to-all-done.5 = bf16[8,128,256]{2,1,0:T(8,128)(2,1)S(1)} async-done(((bf16[8,128,256]{2,1,0:T(8,128)(2,1)}), bf16[8,128,256]{2,1,0:T(8,128)(2,1)S(1)}, u32[]{:S(2)}, u32[]{:S(2)}) %all-to-all-start.5) | async-done | bytes 524320 | tf_op jit(solution)/shard_map/all_to_all | solution.py:214
  122.2 4.9 %all-to-all-start.3 = ((bf16[8,272,128]{2,1,0:T(8,128)(2,1)}), bf16[8,272,128]{2,1,0:T(8,128)(2,1)S(1)}, u32[]{:S(2)}, u32[]{:S(2)}) async-start(bf16[8,272,128]{2,1,0:T(8,128)(2,1)} %pad_maximum_fusion), calls=%async_computation.3 | async-start | bytes 1114112 | tf_op jit(solution)/shard_map/all_to_all | solution.py:227
  127.1 0.3 copy.10
  127.4 16.9 %all-to-all-done.3.in_ref = bf16[8,272,128]{2,1,0:T(8,128)(2,1)S(1)} async-done(((bf16[8,272,128]{2,1,0:T(8,128)(2,1)}), bf16[8,272,128]{2,1,0:T(8,128)(2,1)S(1)}, u32[]{:S(2)}, u32[]{:S(2)}) %all-to-all-start.3) | async-done | bytes 557088 | tf_op jit(solution)/shard_map/all_to_all | solution.py:227
  144.3 0.0 copy-start.3
  144.3 1.5 broadcast_in_dim.28
  145.8 0.0 copy-done.3
  145.8 3.6 %all-to-all-start.6 = ((bf16[4,8,128,256]{3,1,2,0:T(8,128)(2,1)}), bf16[4,8,128,256]{3,1,2,0:T(8,128)(2,1)S(1)}, u32[]{:S(2)}, u32[]{:S(2)}) async-start(bf16[4,8,128,256]{3,1,2,0:T(8,128)(2,1)} %broadcast_in_dim.28), calls=%async_computation.6 | async-start | bytes 4194304 | tf_op jit(solution)/shard_map/all_to_all | solution.py:217
  149.4 2.0 %unpack.1 = (bf16[128,1536]{1,0:T(8,128)(2,1)}, f32[16,576]{1,0:T(8,128)}) custom-call(bf16[8,272,128]{2,1,0:T(8,128)(2,1)} %copy-done.3), custom_call_target="tpu_custom_call" | custom-call | tf_op jit(solution)/shard_map/unpack/pallas_call | solution.py:228
  151.4 23.7 %all-to-all-done.6 = bf16[4,8,128,256]{3,1,2,0:T(8,128)(2,1)S(1)} async-done(((bf16[4,8,128,256]{3,1,2,0:T(8,128)(2,1)}), bf16[4,8,128,256]{3,1,2,0:T(8,128)(2,1)S(1)}, u32[]{:S(2)}, u32[]{:S(2)}) %all-to-all-start.6) | async-done | bytes 2097184 | tf_op jit(solution)/shard_map/all_to_all | solution.py:217
  175.1 0.4 convert_element_type.17
  175.5 0.3 fusion
  175.8 3.0 %copy_bitcast_fusion = (f32[512,1024]{1,0:T(8,128)}, f32[512,1024]{1,0:T(8,128)}) fusion(f32[64,8,8,128]{3,2,1,0:T(8,128)S(1)} %bitcast.16, f32[64,8,8,128]{3,2,1,0:T(8,128)S(1)} %bitcast.17), kind=kLoop, calls=%fused_computation | loop fusion | bytes 8388608 | tf_op jit(solution)/shard_map/reshape | solution.py:222
  (2 shorter events, 0.1 us)
Async XLA Ops:
  33.7 24.3 %copy-start.2 = (s32[16]{0:T(128)S(1)}, s32[16]{0:T(128)}, u32[]{:S(2)}) copy-start(s32[16]{0:T(128)} %order_ref.1) | copy-start | bytes 196
  35.0 23.1 %all-to-all-start.1 = ((bf16[8,8,80,128]{3,2,1,0:T(8,128)(2,1)}), bf16[8,8,80,128]{3,2,1,0:T(8,128)(2,1)S(1)}, u32[]{:S(2)}, u32[]{:S(2)}) async-start(bf16[8,8,80,128]{3,2,1,0:T(8,128)(2,1)} %broadcast_in_dim.10), calls=%async_computation.1 | async-start | bytes 2621440 | tf_op jit(solution)/shard_map/all_to_all | solution.py:173
  58.1 1.2 copy-start
  59.3 1.2 copy-start.1
  78.1 22.3 %all-to-all-start.2 = ((bf16[8,8,80,128]{3,2,1,0:T(8,128)(2,1)}), bf16[8,8,80,128]{3,2,1,0:T(8,128)(2,1)S(1)}, u32[]{:S(2)}, u32[]{:S(2)}) async-start(bf16[8,8,80,128]{3,2,1,0:T(8,128)(2,1)} %get-tuple-element.10), calls=%async_computation.2 | async-start | bytes 2621440 | tf_op jit(solution)/shard_map/all_to_all | solution.py:225
  101.2 21.0 %all-to-all-start.5 = ((bf16[8,128,256]{2,1,0:T(8,128)(2,1)}), bf16[8,128,256]{2,1,0:T(8,128)(2,1)S(1)}, u32[]{:S(2)}, u32[]{:S(2)}) async-start(bf16[8,128,256]{2,1,0:T(8,128)(2,1)} %broadcast_in_dim.13), calls=%async_computation.5 | async-start | bytes 1048576 | tf_op jit(solution)/shard_map/all_to_all | solution.py:214
  122.2 22.1 %all-to-all-start.3 = ((bf16[8,272,128]{2,1,0:T(8,128)(2,1)}), bf16[8,272,128]{2,1,0:T(8,128)(2,1)S(1)}, u32[]{:S(2)}, u32[]{:S(2)}) async-start(bf16[8,272,128]{2,1,0:T(8,128)(2,1)} %pad_maximum_fusion), calls=%async_computation.3 | async-start | bytes 1114112 | tf_op jit(solution)/shard_map/all_to_all | solution.py:227
  144.3 1.5 copy-start.3
  145.8 29.3 %all-to-all-start.6 = ((bf16[4,8,128,256]{3,1,2,0:T(8,128)(2,1)}), bf16[4,8,128,256]{3,1,2,0:T(8,128)(2,1)S(1)}, u32[]{:S(2)}, u32[]{:S(2)}) async-start(bf16[4,8,128,256]{3,1,2,0:T(8,128)(2,1)} %broadcast_in_dim.28), calls=%async_computation.6 | async-start | bytes 4194304 | tf_op jit(solution)/shard_map/all_to_all | solution.py:217

commit v2 on v1

v2 whole, which is shorter than its diff:
```python
import functools

import jax
import jax.numpy as jnp
from jax import lax
from jax.experimental import pallas as pl
from jax.experimental.pallas import tpu as pltpu
from jax.sharding import PartitionSpec as P

LAT = 512
ROPE = 64
NOPE = 128
VDIM = 128
WIDTH = NOPE + ROPE
HALF = 64
SUB = 16
TILE = 256
BF = jnp.bfloat16
F32 = jnp.float32
VMEM = pl.BlockSpec(memory_space=pltpu.VMEM)

ROW_DO = NOPE
ROW_ROPE = ROW_DO + VDIM
ROWS_IN = ROW_ROPE + ROPE
ROW_GROPE = NOPE
ROW_GL = ROW_GROPE + ROPE
ROW_GLROPE = ROW_GL + SUB * (LAT // 128)
ROWS_OUT = ROW_GLROPE + SUB


def dot_nn(a, b):
    return lax.dot_general(a, b, (((1,), (0,)), ((), ())), preferred_element_type=F32)


def dot_nt(a, b):
    return lax.dot_general(a, b, (((1,), (1,)), ((), ())), preferred_element_type=F32)


def dot_tn(a, b):
    return lax.dot_general(a, b, (((0,), (0,)), ((), ())), preferred_element_type=F32)


def pack_kernel(rank_ref, q_ref, d_ref, wk_ref, wv_ref, out_ref, w_ref):
    n = out_ref.shape[0]
    for h in range(n):
        q = q_ref[:, h * WIDTH : (h + 1) * WIDTH]
        out_ref[h, 0:ROW_DO, :] = q[:, :NOPE]
        out_ref[h, ROW_DO:ROW_ROPE, :] = d_ref[:, h * VDIM : (h + 1) * VDIM]
        rope = q[:, NOPE:]
        out_ref[h, ROW_ROPE:ROWS_IN, :] = jnp.concatenate([rope[:HALF], rope[HALF:]], axis=1)
    w_ref[:, :NOPE] = wk_ref[...]
    w_ref[:, NOPE:] = wv_ref[...]


def attention_kernel(n_head, n_dp, order_ref, rank_ref, in_ref, w_ref, *refs):
    lat_refs, refs = refs[:n_head], refs[n_head:]
    gl_ref, gq_ref = refs[:2]
    gw_refs = refs[2 : 2 + n_dp]
    lat_s, k_s, v_s, q_s, d_s, dk_s, dv_s, dq_s, gl_s, gw_s = refs[2 + n_dp :]
    blocks = in_ref.shape[0]
    seq = lat_s.shape[0]
    scale = WIDTH ** (-0.5)
    per_half = HALF // SUB

    def place(block):
        return pl.multiple_of(order_ref[block] * HALF, HALF)

    for s in range(blocks):
        for half in range(2):
            rows = pl.ds(place(2 * s + half), HALF)
            lo = half * HALF
            q_s[rows, :NOPE] = in_ref[s, lo : lo + HALF, :]
            q_s[rows, NOPE:] = in_ref[s, ROW_ROPE:ROWS_IN, half * ROPE : (half + 1) * ROPE]
            d_s[rows, :] = in_ref[s, ROW_DO + lo : ROW_DO + lo + HALF, :]
    for shift in range(n_head):
        p = lax.rem(rank_ref[1] + n_head - shift, n_head)
        half, i = lax.div(p, per_half), lax.rem(p, per_half)
        for s in range(blocks):
            sub = pl.ds(pl.multiple_of(order_ref[2 * s + half] * HALF + i * SUB, SUB), SUB)
            lat_s[sub, :] = lat_refs[shift][s, :, :LAT]
            k_s[sub, NOPE:] = lat_refs[shift][s, :, LAT:]

    w_both = w_ref[...]
    for t in range(seq // TILE):
        rows = slice(t * TILE, (t + 1) * TILE)
        both = dot_nn(lat_s[rows, :], w_both)
        k_s[rows, :NOPE] = both[:, :NOPE].astype(BF)
        v_s[rows, :] = both[:, NOPE:].astype(BF)

    dk_s[...] = jnp.zeros_like(dk_s)
    dv_s[...] = jnp.zeros_like(dv_s)
    for t in range(seq // TILE):
        rows = slice(t * TILE, (t + 1) * TILE)
        width = (t + 1) * TILE
        q = q_s[rows, :]
        d = d_s[rows, :]
        k = k_s[:width, :]
        scores = dot_nt(k, q) * scale
        key_pos = lax.broadcasted_iota(jnp.int32, (width, TILE), 0)
        row_pos = lax.broadcasted_iota(jnp.int32, (width, TILE), 1) + t * TILE
        masked = jnp.where(key_pos <= row_pos, scores, -jnp.inf)
        top = jnp.max(masked, axis=0, keepdims=True)
        weights = jnp.exp(masked - top)
        probs = weights / jnp.sum(weights, axis=0, keepdims=True)
        probs_b = probs.astype(BF)
        dprob = dot_nt(v_s[:width, :], d)
        drow = jnp.sum(probs_b.astype(F32) * dprob, axis=0, keepdims=True)
        dscore = (probs * (dprob - drow)).astype(BF)
        dq_s[rows, :] = (dot_tn(dscore, k) * scale).astype(BF)
        dk_s[:width, :] += dot_nn(dscore, q)
        dv_s[:width, :] += dot_nn(probs_b, d)

    dk = dk_s[...] * scale
    dkv = jnp.concatenate([dk[:, :NOPE], dv_s[...]], axis=1).astype(BF)
    gw_s[...] = dot_tn(lat_s[...], dkv).astype(BF)
    share = LAT // n_dp
    for shift in range(n_dp):
        target = lax.rem(rank_ref[2] + shift, n_dp)
        gw_refs[shift][...] = gw_s[pl.ds(pl.multiple_of(target * share, share), share), :]
    gl_s[:, :LAT] = dot_nt(dkv, w_both).astype(BF)
    gl_s[:, LAT:] = dk[:, NOPE:].astype(BF)

    for s in range(blocks):
        for half in range(2):
            base = place(2 * s + half)
            rows = pl.ds(base, HALF)
            lo = half * HALF
            gq_ref[s, lo : lo + HALF, :] = dq_s[rows, :NOPE]
            gq_ref[s, ROW_GROPE:ROW_GL, half * ROPE : (half + 1) * ROPE] = dq_s[rows, NOPE:]
            for i in range(per_half):
                p = half * per_half + i
                sub = pl.ds(pl.multiple_of(base + i * SUB, SUB), SUB)
                for j in range(LAT // 128):
                    gl_ref[p, s, SUB * j : SUB * (j + 1), :] = gl_s[sub, 128 * j : 128 * (j + 1)]
                rope = gl_s[sub, LAT:]
                gl_ref[p, s, SUB * (LAT // 128) :, :] = jnp.concatenate([rope, rope], axis=1)


def unpack_kernel(in_ref, gq_ref, gl_ref):
    n = in_ref.shape[0]
    for h in range(n):
        rope = in_ref[h, ROW_GROPE:ROW_GL, :]
        rope = jnp.concatenate([rope[:, :ROPE], rope[:, ROPE:]], axis=0)
        gq_ref[:, h * WIDTH : (h + 1) * WIDTH] = jnp.concatenate([in_ref[h, :NOPE, :], rope], axis=1)
    for j in range(LAT // 128):
        part = in_ref[:, ROW_GL + SUB * j : ROW_GL + SUB * (j + 1), :].astype(F32)
        gl_ref[:, 128 * j : 128 * (j + 1)] = jnp.sum(part, axis=0)
    part = in_ref[:, ROW_GLROPE:ROWS_OUT, :ROPE].astype(F32)
    gl_ref[:, LAT:] = jnp.sum(part, axis=0)


def assemble_kernel(n_dp, rank_ref, *refs):
    part_refs, (gk_ref, gv_ref) = refs[:n_dp], refs[n_dp:]
    n_ctx, share, _ = part_refs[0].shape
    for shift in range(n_dp):
        source = lax.rem(rank_ref[2] + n_dp - shift, n_dp)
        rows = pl.ds(pl.multiple_of(source * share, share), share)
        for h in range(n_ctx):
            part = part_refs[shift][h].astype(F32)
            gk_ref[rows, h * NOPE : (h + 1) * NOPE] = part[:, :NOPE]
            gv_ref[rows, h * VDIM : (h + 1) * VDIM] = part[:, NOPE:]


def shifted(x, axis, n, shift):
    return lax.ppermute(x, axis, [(i, (i + shift) % n) for i in range(n)])


def whole(shape):
    return pl.BlockSpec(shape, lambda i, *scalars: (0,) * len(shape))


def call(kernel, name, scalars, inputs, outs, scratch=(), in_specs=None, flops=0):
    moved = sum(x.size * x.dtype.itemsize for x in inputs) + sum(
        x.size * x.dtype.itemsize for x in outs
    )
    return pl.pallas_call(
        kernel,
        grid_spec=pltpu.PrefetchScalarGridSpec(
            num_scalar_prefetch=len(scalars),
            grid=(1,),
            in_specs=in_specs or [whole(x.shape) for x in inputs],
            out_specs=[whole(x.shape) for x in outs],
            scratch_shapes=list(scratch),
        ),
        out_shape=list(outs),
        compiler_params=pltpu.CompilerParams(vmem_limit_bytes=48 * 1024 * 1024),
        cost_estimate=pl.CostEstimate(flops=flops, bytes_accessed=moved, transcendentals=0),
        name=name,
    )(*scalars, *inputs)


def on_device(n_dp, n_ctx, n_head, query, latent, w_uk, w_uv, grad_out, block_order):
    seq = n_ctx * n_head * SUB
    rows = query.shape[1]
    shape = jax.ShapeDtypeStruct
    ranks = jnp.stack([lax.axis_index(a).astype(jnp.int32) for a in ("ctx", "head", "dp")])

    lat_mine = lax.all_to_all(
        jnp.broadcast_to(latent, (n_ctx, SUB, LAT + ROPE)), "ctx", 0, 0, tiled=True
    )
    lat_all = [lat_mine] + [shifted(lat_mine, "head", n_head, i) for i in range(1, n_head)]
    head_cols = pl.BlockSpec((LAT, NOPE), lambda i, rank: (0, rank[0]))
    packed, w_both = call(
        pack_kernel,
        "pack",
        (ranks,),
        (query[0], grad_out[0], w_uk, w_uv),
        [shape((n_ctx, ROWS_IN, 128), BF), shape((LAT, NOPE + VDIM), BF)],
        in_specs=[whole(query.shape[1:]), whole(grad_out.shape[1:]), head_cols, head_cols],
    )
    mine = lax.all_to_all(packed, "ctx", 0, 0, tiled=True)

    gl_part, gq_part, *gw_parts = call(
        functools.partial(attention_kernel, n_head, n_dp),
        "attention_backward",
        (block_order, ranks),
        (mine, w_both, *lat_all),
        [
            shape((n_head, n_ctx, SUB * (LAT // 128) + SUB, 128), BF),
            shape((n_ctx, ROW_GL, 128), BF),
        ]
        + [shape((LAT // n_dp, NOPE + VDIM), BF)] * n_dp,
        scratch=[
            pltpu.VMEM((seq, LAT), BF),
            pltpu.VMEM((seq, WIDTH), BF),
            pltpu.VMEM((seq, VDIM), BF),
            pltpu.VMEM((seq, WIDTH), BF),
            pltpu.VMEM((seq, VDIM), BF),
            pltpu.VMEM((seq, WIDTH), F32),
            pltpu.VMEM((seq, VDIM), F32),
            pltpu.VMEM((seq, WIDTH), BF),
            pltpu.VMEM((seq, LAT + ROPE), BF),
            pltpu.VMEM((LAT, NOPE + VDIM), BF),
        ],
        flops=3 * 10**9,
    )

    gw_sum = gw_parts[0].astype(F32)
    for i in range(1, n_dp):
        gw_sum = gw_sum + shifted(gw_parts[i], "dp", n_dp, i).astype(F32)
    gw_sum = gw_sum.astype(BF)
    gw_ctx = lax.all_to_all(
        jnp.broadcast_to(gw_sum[None], (n_ctx,) + gw_sum.shape), "ctx", 0, 0, tiled=True
    )
    gw_all = [gw_ctx] + [shifted(gw_ctx, "dp", n_dp, i) for i in range(1, n_dp)]
    grad_w_uk, grad_w_uv = call(
        functools.partial(assemble_kernel, n_dp),
        "assemble",
        (ranks,),
        gw_all,
        [shape((LAT, n_ctx * NOPE), F32), shape((LAT, n_ctx * VDIM), F32)],
    )

    gl_head = jnp.sum(
        lax.all_to_all(gl_part, "head", 0, 0, tiled=True).astype(F32), axis=0
    ).astype(BF)
    back = lax.all_to_all(jnp.concatenate([gq_part, gl_head], axis=1), "ctx", 0, 0, tiled=True)
    grad_query, grad_latent = pl.pallas_call(
        unpack_kernel,
        out_shape=[
            jax.ShapeDtypeStruct((rows, n_ctx * WIDTH), BF),
            jax.ShapeDtypeStruct((SUB, LAT + ROPE), F32),
        ],
        in_specs=[VMEM],
        out_specs=[VMEM, VMEM],
        name="unpack",
    )(back)
    return (grad_query[None], grad_latent[None], grad_w_uk, grad_w_uv)


def solution(mesh):
    sizes = mesh.shape
    return jax.shard_map(
        functools.partial(on_device, sizes["dp"], sizes["ctx"], sizes["head"]),
        mesh=mesh,
        in_specs=(
            P("dp", "ctx", "head"),
            P("dp", ("ctx", "head"), None),
            P(None, "head"),
            P(None, "head"),
            P("dp", "ctx", "head"),
            P(),
        ),
        out_specs=(
            P("dp", "ctx", "head"),
            P("dp", ("ctx", "head"), None),
            P(None, "head"),
            P(None, "head"),
        ),
        check_vma=False,
    )
```

time: 182 us -> 140 us (0.77)
  blocking collectives: 41.9 us -> 0 us
  starting transfers between devices: 21.2 us -> 46.4 us
  waiting for transfers between devices: 93.2 us -> 68.9 us
  Pallas kernels: 10.8 us -> 13.2 us
  local copies, waits for them, and re-layouts: 9.6 us -> 7.46 us
    ppermute x0 -> x13, waiting for transfers between devices: none -> 42.1 us  [shifted(): return lax.ppermute(x, axis, [(i, (i + shift) % n) for i in range(n)])]
    all_to_all x2 -> x0, blocking collectives: 41.9 us -> none  [the longest x1 30.9 us: on_device(): mine = lax.all_to_all(packed, 'ctx', 0, 0, tiled=True)]
    all_to_all x2, waiting for transfers between devices: 42.5 us -> 2.2 us  [the longest x1 2.19 us: on_device(): lax.all_to_all(jnp.broadcast_to(latent, (n_ctx, SUB, LAT + ROPE)), 'ctx',...]
    ppermute x0 -> x13, starting transfers between devices: none -> 17 us  [shifted(): return lax.ppermute(x, axis, [(i, (i + shift) % n) for i in range(n)])]
    all_to_all x1, waiting for transfers between devices: 16.9 us -> 0.01 us  [on_device(): lax.all_to_all(jnp.concatenate([gq_part, gl_head], axis=1), 'ctx', 0, 0,...]
    all_to_all x1, waiting for transfers between devices: 18.6 us -> 9.83 us  [on_device(): lax.all_to_all(gl_part, 'head', 0, 0, tiled=True).astype(F32)]
    all_to_all x2, starting transfers between devices: 7.91 us -> 13.7 us  [the longest x1 8.57 us: on_device(): lax.all_to_all(jnp.broadcast_to(latent, (n_ctx, SUB, LAT + ROPE)), 'ctx',...]
    reshape x1 -> x0, local copies, waits for them, and re-layouts: 3.01 us -> none  [on_device(): grad_w_uv = gw_all[:, :, NOPE:].reshape(LAT, n_ctx * VDIM)]
  transfers between devices with their start and end apart: 5 -> 18, of which waited for: 5 -> 13; matrix products, arithmetic and copies ran while one was open for 1% -> 1% of each run, Pallas kernels for 1% -> 3%
where the time goes in v2:
time: 140 us; the launch traced here: 138 us
  waiting for transfers between devices  68.9 us (49%)
  starting transfers between devices  46.4 us (33%)
  Pallas kernels  13.2 us (9%)
  local copies, waits for them, and re-layouts  7.46 us (5%)
    ppermute x13, waiting for transfers between devices, shifted(): return lax.ppermute(x, axis, [(i, (i + shift) % n) for i in range(n)])  42.1 us
    ppermute x13, starting transfers between devices, shifted(): return lax.ppermute(x, axis, [(i, (i + shift) % n) for i in range(n)])  17 us
    all_to_all x1, waiting for transfers between devices, on_device(): lax.all_to_all(jnp.broadcast_to(gw_sum[None], (n_ctx,) + gw_sum.shape), '...  14.8 us
    pallas_call x3, Pallas kernels, call(): pl.pallas_call(kernel, grid_spec=pltpu.PrefetchScalarGridSpec(num_scalar_...  11.2 us
    all_to_all x1, waiting for transfers between devices, on_device(): lax.all_to_all(gl_part, 'head', 0, 0, tiled=True).astype(F32)  9.83 us
    all_to_all x1, starting transfers between devices, on_device(): lax.all_to_all(jnp.broadcast_to(latent, (n_ctx, SUB, LAT + ROPE)), 'ctx',...  8.57 us
    all_to_all x1, starting transfers between devices, on_device(): lax.all_to_all(jnp.broadcast_to(gw_sum[None], (n_ctx,) + gw_sum.shape), '...  7.21 us
    unnamed x12, local copies, waits for them, and re-layouts  5.22 us
  transfers between devices with their start and end apart: 18, of which 13 were waited for; matrix products, arithmetic and copies ran while one was open for 1% of the time, Pallas kernels for 3%

profile of v2, /device:TPU:32, one launch (start us, length us, event | category | flops | bytes accessed | tf_op | source)
XLA Modules:
  0.0 137.8 jit_solution(6336687907539522405)
XLA Ops:
  0.6 1.4 %broadcast_in_dim.20 = bf16[8,16,576]{2,1,0:T(8,128)(2,1)} broadcast(bf16[16,576]{1,0:T(8,128)(2,1)} %bitcast.10), dimensions={1,2} | broadcast | bytes 165888 | tf_op jit(solution)/shard_map/broadcast_in_dim | solution.py:199
  2.0 8.6 %all-to-all-start.1 = ((bf16[8,16,576]{2,1,0:T(8,128)(2,1)}), bf16[8,16,576]{2,1,0:T(8,128)(2,1)S(1)}, u32[]{:S(2)}, u32[]{:S(2)}) async-start(bf16[8,16,576]{2,1,0:T(8,128)(2,1)} %broadcast_in_dim.20), calls=%async_computation.1 | async-start | bytes 327680 | tf_op jit(solution)/shard_map/all_to_all | solution.py:198
  10.7 1.2 copy-done
  11.9 1.2 copy-done.1
  13.1 1.0 copy-done.2
  14.1 0.9 copy-done.3
  15.1 1.6 %pack.1 = (bf16[8,320,128]{2,1,0:T(8,128)(2,1)}, bf16[512,256]{1,0:T(8,128)(2,1)S(1)}) custom-call(s32[3]{0:T(128)S(1)} %pad_add_fusion.rank_ref, bf16[128,1536]{1,0:T(8,128)(2,1)S(1)} %bitcast.8, bf16[128,1024]{1,0:T(8,128)(2,1)S(1)} %bitcast.9, bf16[512,1024]{1,0:T(8,128)(2,1)S(1)} %copy-done, bf16[512,1024]{1,0:T(8,128)(2,1)S(1)} %copy-done.1), custom_call_target="tpu_custom_call" | custom-call | bytes 3670016 | tf_op jit(solution)/shard_map/pack/pallas_call | solution.py:176
  16.7 2.2 %all-to-all-done.1.refs_0_ = bf16[8,16,576]{2,1,0:T(8,128)(2,1)S(1)} async-done(((bf16[8,16,576]{2,1,0:T(8,128)(2,1)}), bf16[8,16,576]{2,1,0:T(8,128)(2,1)S(1)}, u32[]{:S(2)}, u32[]{:S(2)}) %all-to-all-start.1) | async-done | bytes 147488 | tf_op jit(solution)/shard_map/all_to_all | solution.py:198
  18.9 5.1 %all-to-all-start = ((bf16[8,320,128]{2,1,0:T(8,128)(2,1)}), bf16[8,320,128]{2,1,0:T(8,128)(2,1)S(1)}, u32[]{:S(2)}, u32[]{:S(2)}) async-start(bf16[8,320,128]{2,1,0:T(8,128)(2,1)} %get-tuple-element.16), calls=%async_computation | async-start | bytes 1310720 | tf_op jit(solution)/shard_map/all_to_all | solution.py:211
  24.1 1.1 collective-permute-start.6
  25.1 1.7 %collective-permute-start.5 = (bf16[8,16,576]{2,1,0:T(8,128)(2,1)S(1)}, bf16[8,16,576]{2,1,0:T(8,128)(2,1)S(1)}, u32[]{:S(2)}, u32[]{:S(2)}) collective-permute-start(bf16[8,16,576]{2,1,0:T(8,128)(2,1)S(1)} %all-to-all-done.1.refs_0_), channel_id=1, source_target_pairs={{0,6},{1,7},{2,0},{3,1},{4,2},{5,3},{6,4},{7,5},{8,14},{9,15},{10,... | collective-permute-start | bytes 442376 | tf_op jit(solution)/shard_map/ppermute | solution.py:165
  27.5 2.7 %collective-permute-start.3 = (bf16[8,16,576]{2,1,0:T(8,128)(2,1)S(1)}, bf16[8,16,576]{2,1,0:T(8,128)(2,1)S(1)}, u32[]{:S(2)}, u32[]{:S(2)}) collective-permute-start(bf16[8,16,576]{2,1,0:T(8,128)(2,1)S(1)} %all-to-all-done.1.refs_0_), channel_id=1, source_target_pairs={{0,4},{1,5},{2,6},{3,7},{4,0},{5,1},{6,2},{7,3},{8,12},{9,13},{10,... | collective-permute-start | bytes 442376 | tf_op jit(solution)/shard_map/ppermute | solution.py:165
  30.6 3.5 %collective-permute-done.5.refs_6_ = bf16[8,16,576]{2,1,0:T(8,128)(2,1)S(1)} collective-permute-done((bf16[8,16,576]{2,1,0:T(8,128)(2,1)S(1)}, bf16[8,16,576]{2,1,0:T(8,128)(2,1)S(1)}, u32[]{:S(2)}, u32[]{:S(2)}) %collective-permute-start.5) | collective-permute-done | bytes 147488 | tf_op jit(solution)/shard_map/ppermute | solution.py:165
  34.2 4.5 %collective-permute-done.3.refs_4_ = bf16[8,16,576]{2,1,0:T(8,128)(2,1)S(1)} collective-permute-done((bf16[8,16,576]{2,1,0:T(8,128)(2,1)S(1)}, bf16[8,16,576]{2,1,0:T(8,128)(2,1)S(1)}, u32[]{:S(2)}, u32[]{:S(2)}) %collective-permute-start.3) | collective-permute-done | bytes 147488 | tf_op jit(solution)/shard_map/ppermute | solution.py:165
  38.9 6.7 %collective-permute-done.1.refs_2_ = bf16[8,16,576]{2,1,0:T(8,128)(2,1)S(1)} collective-permute-done((bf16[8,16,576]{2,1,0:T(8,128)(2,1)S(1)}, bf16[8,16,576]{2,1,0:T(8,128)(2,1)S(1)}, u32[]{:S(2)}, u32[]{:S(2)}) %collective-permute-start.1) | collective-permute-done | bytes 147488 | tf_op jit(solution)/shard_map/ppermute | solution.py:165
  45.8 6.5 %attention_backward.1 = (bf16[8,8,80,128]{3,2,1,0:T(8,128)(2,1)}, bf16[8,192,128]{2,1,0:T(8,128)(2,1)S(1)}, bf16[128,256]{1,0:T(8,128)(2,1)S(1)}, bf16[128,256]{...) custom-call(s32[16]{0:T(128)S(1)} %copy-done.4, s32[3]{0:T(128)S(1)} %pad_add_fusion.rank_ref, ...), custom_call_target="tpu_custom_call" | custom-call | flops 3000000000 | bytes 4063232 | tf_op jit(solution)/shard_map/attention_backward/pallas_call | solution.py:176
  52.3 3.6 %all-to-all-start.2 = ((bf16[8,8,80,128]{3,2,1,0:T(8,128)(2,1)}), bf16[8,8,80,128]{3,2,1,0:T(8,128)(2,1)S(1)}, u32[]{:S(2)}, u32[]{:S(2)}) async-start(bf16[8,8,80,128]{3,2,1,0:T(8,128)(2,1)} %get-tuple-element.19), calls=%async_computation.2 | async-start | bytes 2621440 | tf_op jit(solution)/shard_map/all_to_all | solution.py:255
  55.8 1.7 %collective-permute-start.7 = (bf16[128,256]{1,0:T(8,128)(2,1)S(1)}, bf16[128,256]{1,0:T(8,128)(2,1)S(1)}, u32[]{:S(2)}, u32[]{:S(2)}) collective-permute-start(bf16[128,256]{1,0:T(8,128)(2,1)S(1)} %get-tuple-element.23), channel_id=1, source_target_pairs={{0,64},{64,128},{128,192},{192,0},{1,65},{65,129},{129,193},{193,1... | collective-permute-start | bytes 196616 | tf_op jit(solution)/shard_map/ppermute | solution.py:165
  57.5 2.9 %collective-permute-start.8 = (bf16[128,256]{1,0:T(8,128)(2,1)S(1)}, bf16[128,256]{1,0:T(8,128)(2,1)S(1)}, u32[]{:S(2)}, u32[]{:S(2)}) collective-permute-start(bf16[128,256]{1,0:T(8,128)(2,1)S(1)} %get-tuple-element.24), channel_id=1, source_target_pairs={{0,128},{64,192},{128,0},{192,64},{1,129},{65,193},{129,1},{193,65... | collective-permute-start | bytes 196616 | tf_op jit(solution)/shard_map/ppermute | solution.py:165
  60.4 1.3 collective-permute-start.9
  61.8 2.4 %collective-permute-done.8 = bf16[128,256]{1,0:T(8,128)(2,1)S(1)} collective-permute-done((bf16[128,256]{1,0:T(8,128)(2,1)S(1)}, bf16[128,256]{1,0:T(8,128)(2,1)S(1)}, u32[]{:S(2)}, u32[]{:S(2)}) %collective-permute-start.8) | collective-permute-done | bytes 65568 | tf_op jit(solution)/shard_map/ppermute | solution.py:165
  64.7 9.8 %all-to-all-done.2 = bf16[8,8,80,128]{3,2,1,0:T(8,128)(2,1)S(1)} async-done(((bf16[8,8,80,128]{3,2,1,0:T(8,128)(2,1)}), bf16[8,8,80,128]{3,2,1,0:T(8,128)(2,1)S(1)}, u32[]{:S(2)}, u32[]{:S(2)}) %all-to-all-start.2) | async-done | bytes 1310752 | tf_op jit(solution)/shard_map/all_to_all | solution.py:255
  75.4 7.2 %all-to-all-start.4 = ((bf16[8,128,256]{2,1,0:T(8,128)(2,1)}), bf16[8,128,256]{2,1,0:T(8,128)(2,1)S(1)}, u32[]{:S(2)}, u32[]{:S(2)}) async-start(bf16[8,128,256]{2,1,0:T(8,128)(2,1)} %broadcast_in_dim.23), calls=%async_computation.4 | async-start | bytes 1048576 | tf_op jit(solution)/shard_map/all_to_all | solution.py:242
  82.8 0.9 pad_maximum_fusion
  83.6 14.8 %all-to-all-done.4.refs_0_ = bf16[8,128,256]{2,1,0:T(8,128)(2,1)S(1)} async-done(((bf16[8,128,256]{2,1,0:T(8,128)(2,1)}), bf16[8,128,256]{2,1,0:T(8,128)(2,1)S(1)}, u32[]{:S(2)}, u32[]{:S(2)}) %all-to-all-start.4) | async-done | bytes 524320 | tf_op jit(solution)/shard_map/all_to_all | solution.py:242
  98.4 4.9 %all-to-all-start.3 = ((bf16[8,272,128]{2,1,0:T(8,128)(2,1)}), bf16[8,272,128]{2,1,0:T(8,128)(2,1)S(1)}, u32[]{:S(2)}, u32[]{:S(2)}) async-start(bf16[8,272,128]{2,1,0:T(8,128)(2,1)} %pad_maximum_fusion), calls=%async_computation.3 | async-start | bytes 1114112 | tf_op jit(solution)/shard_map/all_to_all | solution.py:257
  103.3 3.0 %collective-permute-start.12 = (bf16[8,128,256]{2,1,0:T(8,128)(2,1)S(1)}, bf16[8,128,256]{2,1,0:T(8,128)(2,1)S(1)}, u32[]{:S(2)}, u32[]{:S(2)}) collective-permute-start(bf16[8,128,256]{2,1,0:T(8,128)(2,1)S(1)} %all-to-all-done.4.refs_0_), channel_id=1, source_target_pairs={{0,192},{64,0},{128,64},{192,128},{1,193},{65,1},{129,65},{193,129... | collective-permute-start | bytes 1572872 | tf_op jit(solution)/shard_map/ppermute | solution.py:165
  107.0 1.0 collective-permute-start.10
  107.9 20.3 %collective-permute-done.12.refs_3_ = bf16[8,128,256]{2,1,0:T(8,128)(2,1)S(1)} collective-permute-done((bf16[8,128,256]{2,1,0:T(8,128)(2,1)S(1)}, bf16[8,128,256]{2,1,0:T(8,128)(2,1)S(1)}, u32[]{:S(2)}, u32[]{:S(2)}) %collective-permute-start.12) | collective-permute-done | bytes 524320 | tf_op jit(solution)/shard_map/ppermute | solution.py:165
  128.3 3.7 %collective-permute-done.10.refs_1_ = bf16[8,128,256]{2,1,0:T(8,128)(2,1)S(1)} collective-permute-done((bf16[8,128,256]{2,1,0:T(8,128)(2,1)S(1)}, bf16[8,128,256]{2,1,0:T(8,128)(2,1)S(1)}, u32[]{:S(2)}, u32[]{:S(2)}) %collective-permute-start.10) | collective-permute-done | bytes 524320 | tf_op jit(solution)/shard_map/ppermute | solution.py:165
  132.0 3.0 %assemble.1 = (f32[512,1024]{1,0:T(8,128)}, f32[512,1024]{1,0:T(8,128)}) custom-call(s32[3]{0:T(128)S(1)} %pad_add_fusion.rank_ref, bf16[8,128,256]{2,1,0:T(8,128)(2,1)S(1)} %all-to-all-done.4.refs_0_, bf16[8,128,256]{2,1,0:T(8,128)(2,1)S(1)} %collective-permute-done.10.refs_1_, bf16[8,128,256]{2,1,0:T(8,128)(2,1)S(1)} %collective-permute-done.11.refs_2_, ...), custom_call_target="tpu_custom_call" | custom-call | bytes 6291456 | tf_op jit(solution)/shard_map/assemble/pallas_call | solution.py:176
  135.8 2.0 %unpack.1 = (bf16[128,1536]{1,0:T(8,128)(2,1)}, f32[16,576]{1,0:T(8,128)}) custom-call(bf16[8,272,128]{2,1,0:T(8,128)(2,1)} %copy-done.5), custom_call_target="tpu_custom_call" | custom-call | tf_op jit(solution)/shard_map/unpack/pallas_call | solution.py:258
  (26 shorter events, 4.7 us)
Async XLA Ops:
  2.0 16.9 %all-to-all-start.1 = ((bf16[8,16,576]{2,1,0:T(8,128)(2,1)}), bf16[8,16,576]{2,1,0:T(8,128)(2,1)S(1)}, u32[]{:S(2)}, u32[]{:S(2)}) async-start(bf16[8,16,576]{2,1,0:T(8,128)(2,1)} %broadcast_in_dim.20), calls=%async_computation.1 | async-start | bytes 327680 | tf_op jit(solution)/shard_map/all_to_all | solution.py:198
  10.7 1.2 copy-start
  11.9 1.2 copy-start.1
  13.1 1.0 copy-start.2
  14.1 0.9 copy-start.3
  16.7 29.1 %copy-start.4 = (s32[16]{0:T(128)S(1)}, s32[16]{0:T(128)}, u32[]{:S(2)}) copy-start(s32[16]{0:T(128)} %order_ref.1) | copy-start | bytes 196
  18.9 26.9 %all-to-all-start = ((bf16[8,320,128]{2,1,0:T(8,128)(2,1)}), bf16[8,320,128]{2,1,0:T(8,128)(2,1)S(1)}, u32[]{:S(2)}, u32[]{:S(2)}) async-start(bf16[8,320,128]{2,1,0:T(8,128)(2,1)} %get-tuple-element.16), calls=%async_computation | async-start | bytes 1310720 | tf_op jit(solution)/shard_map/all_to_all | solution.py:211
  24.1 6.1 %collective-permute-start.6 = (bf16[8,16,576]{2,1,0:T(8,128)(2,1)S(1)}, bf16[8,16,576]{2,1,0:T(8,128)(2,1)S(1)}, u32[]{:S(2)}, u32[]{:S(2)}) collective-permute-start(bf16[8,16,576]{2,1,0:T(8,128)(2,1)S(1)} %all-to-all-done.1.refs_0_), channel_id=1, source_target_pairs={{0,7},{1,0},{2,1},{3,2},{4,3},{5,4},{6,5},{7,6},{8,15},{9,8},{10,9... | collective-permute-start | bytes 442376 | tf_op jit(solution)/shard_map/ppermute | solution.py:165
  25.1 8.9 %collective-permute-start.5 = (bf16[8,16,576]{2,1,0:T(8,128)(2,1)S(1)}, bf16[8,16,576]{2,1,0:T(8,128)(2,1)S(1)}, u32[]{:S(2)}, u32[]{:S(2)}) collective-permute-start(bf16[8,16,576]{2,1,0:T(8,128)(2,1)S(1)} %all-to-all-done.1.refs_0_), channel_id=1, source_target_pairs={{0,6},{1,7},{2,0},{3,1},{4,2},{5,3},{6,4},{7,5},{8,14},{9,15},{10,... | collective-permute-start | bytes 442376 | tf_op jit(solution)/shard_map/ppermute | solution.py:165
  26.8 7.4 %collective-permute-start.4 = (bf16[8,16,576]{2,1,0:T(8,128)(2,1)S(1)}, bf16[8,16,576]{2,1,0:T(8,128)(2,1)S(1)}, u32[]{:S(2)}, u32[]{:S(2)}) collective-permute-start(bf16[8,16,576]{2,1,0:T(8,128)(2,1)S(1)} %all-to-all-done.1.refs_0_), channel_id=1, source_target_pairs={{0,5},{1,6},{2,7},{3,0},{4,1},{5,2},{6,3},{7,4},{8,13},{9,14},{10,... | collective-permute-start | bytes 442376 | tf_op jit(solution)/shard_map/ppermute | solution.py:165
  27.5 11.2 %collective-permute-start.3 = (bf16[8,16,576]{2,1,0:T(8,128)(2,1)S(1)}, bf16[8,16,576]{2,1,0:T(8,128)(2,1)S(1)}, u32[]{:S(2)}, u32[]{:S(2)}) collective-permute-start(bf16[8,16,576]{2,1,0:T(8,128)(2,1)S(1)} %all-to-all-done.1.refs_0_), channel_id=1, source_target_pairs={{0,4},{1,5},{2,6},{3,7},{4,0},{5,1},{6,2},{7,3},{8,12},{9,13},{10,... | collective-permute-start | bytes 442376 | tf_op jit(solution)/shard_map/ppermute | solution.py:165
  30.2 8.7 %collective-permute-start.2 = (bf16[8,16,576]{2,1,0:T(8,128)(2,1)S(1)}, bf16[8,16,576]{2,1,0:T(8,128)(2,1)S(1)}, u32[]{:S(2)}, u32[]{:S(2)}) collective-permute-start(bf16[8,16,576]{2,1,0:T(8,128)(2,1)S(1)} %all-to-all-done.1.refs_0_), channel_id=1, source_target_pairs={{0,3},{1,4},{2,5},{3,6},{4,7},{5,0},{6,1},{7,2},{8,11},{9,12},{10,... | collective-permute-start | bytes 442376 | tf_op jit(solution)/shard_map/ppermute | solution.py:165
  30.2 15.5 %collective-permute-start.1 = (bf16[8,16,576]{2,1,0:T(8,128)(2,1)S(1)}, bf16[8,16,576]{2,1,0:T(8,128)(2,1)S(1)}, u32[]{:S(2)}, u32[]{:S(2)}) collective-permute-start(bf16[8,16,576]{2,1,0:T(8,128)(2,1)S(1)} %all-to-all-done.1.refs_0_), channel_id=1, source_target_pairs={{0,2},{1,3},{2,4},{3,5},{4,6},{5,7},{6,0},{7,1},{8,10},{9,11},{10,... | collective-permute-start | bytes 442376 | tf_op jit(solution)/shard_map/ppermute | solution.py:165
  34.0 11.7 %collective-permute-start = (bf16[8,16,576]{2,1,0:T(8,128)(2,1)S(1)}, bf16[8,16,576]{2,1,0:T(8,128)(2,1)S(1)}, u32[]{:S(2)}, u32[]{:S(2)}) collective-permute-start(bf16[8,16,576]{2,1,0:T(8,128)(2,1)S(1)} %all-to-all-done.1.refs_0_), channel_id=1, source_target_pairs={{0,1},{1,2},{2,3},{3,4},{4,5},{5,6},{6,7},{7,0},{8,9},{9,10},{10,1... | collective-permute-start | bytes 442376 | tf_op jit(solution)/shard_map/ppermute | solution.py:165
  52.3 22.3 %all-to-all-start.2 = ((bf16[8,8,80,128]{3,2,1,0:T(8,128)(2,1)}), bf16[8,8,80,128]{3,2,1,0:T(8,128)(2,1)S(1)}, u32[]{:S(2)}, u32[]{:S(2)}) async-start(bf16[8,8,80,128]{3,2,1,0:T(8,128)(2,1)} %get-tuple-element.19), calls=%async_computation.2 | async-start | bytes 2621440 | tf_op jit(solution)/shard_map/all_to_all | solution.py:255
  55.8 5.9 %collective-permute-start.7 = (bf16[128,256]{1,0:T(8,128)(2,1)S(1)}, bf16[128,256]{1,0:T(8,128)(2,1)S(1)}, u32[]{:S(2)}, u32[]{:S(2)}) collective-permute-start(bf16[128,256]{1,0:T(8,128)(2,1)S(1)} %get-tuple-element.23), channel_id=1, source_target_pairs={{0,64},{64,128},{128,192},{192,0},{1,65},{65,129},{129,193},{193,1... | collective-permute-start | bytes 196616 | tf_op jit(solution)/shard_map/ppermute | solution.py:165
  57.5 6.6 %collective-permute-start.8 = (bf16[128,256]{1,0:T(8,128)(2,1)S(1)}, bf16[128,256]{1,0:T(8,128)(2,1)S(1)}, u32[]{:S(2)}, u32[]{:S(2)}) collective-permute-start(bf16[128,256]{1,0:T(8,128)(2,1)S(1)} %get-tuple-element.24), channel_id=1, source_target_pairs={{0,128},{64,192},{128,0},{192,64},{1,129},{65,193},{129,1},{193,65... | collective-permute-start | bytes 196616 | tf_op jit(solution)/shard_map/ppermute | solution.py:165
  60.4 4.3 %collective-permute-start.9 = (bf16[128,256]{1,0:T(8,128)(2,1)S(1)}, bf16[128,256]{1,0:T(8,128)(2,1)S(1)}, u32[]{:S(2)}, u32[]{:S(2)}) collective-permute-start(bf16[128,256]{1,0:T(8,128)(2,1)S(1)} %get-tuple-element.25), channel_id=1, source_target_pairs={{0,192},{64,0},{128,64},{192,128},{1,193},{65,1},{129,65},{193,129... | collective-permute-start | bytes 196616 | tf_op jit(solution)/shard_map/ppermute | solution.py:165
  75.4 23.0 %all-to-all-start.4 = ((bf16[8,128,256]{2,1,0:T(8,128)(2,1)}), bf16[8,128,256]{2,1,0:T(8,128)(2,1)S(1)}, u32[]{:S(2)}, u32[]{:S(2)}) async-start(bf16[8,128,256]{2,1,0:T(8,128)(2,1)} %broadcast_in_dim.23), calls=%async_computation.4 | async-start | bytes 1048576 | tf_op jit(solution)/shard_map/all_to_all | solution.py:242
  98.4 36.6 %all-to-all-start.3 = ((bf16[8,272,128]{2,1,0:T(8,128)(2,1)}), bf16[8,272,128]{2,1,0:T(8,128)(2,1)S(1)}, u32[]{:S(2)}, u32[]{:S(2)}) async-start(bf16[8,272,128]{2,1,0:T(8,128)(2,1)} %pad_maximum_fusion), calls=%async_computation.3 | async-start | bytes 1114112 | tf_op jit(solution)/shard_map/all_to_all | solution.py:257
  103.3 25.0 %collective-permute-start.12 = (bf16[8,128,256]{2,1,0:T(8,128)(2,1)S(1)}, bf16[8,128,256]{2,1,0:T(8,128)(2,1)S(1)}, u32[]{:S(2)}, u32[]{:S(2)}) collective-permute-start(bf16[8,128,256]{2,1,0:T(8,128)(2,1)S(1)} %all-to-all-done.4.refs_0_), channel_id=1, source_target_pairs={{0,192},{64,0},{128,64},{192,128},{1,193},{65,1},{129,65},{193,129... | collective-permute-start | bytes 1572872 | tf_op jit(solution)/shard_map/ppermute | solution.py:165
  106.3 21.9 %collective-permute-start.11 = (bf16[8,128,256]{2,1,0:T(8,128)(2,1)S(1)}, bf16[8,128,256]{2,1,0:T(8,128)(2,1)S(1)}, u32[]{:S(2)}, u32[]{:S(2)}) collective-permute-start(bf16[8,128,256]{2,1,0:T(8,128)(2,1)S(1)} %all-to-all-done.4.refs_0_), channel_id=1, source_target_pairs={{0,128},{64,192},{128,0},{192,64},{1,129},{65,193},{129,1},{193,65... | collective-permute-start | bytes 1572872 | tf_op jit(solution)/shard_map/ppermute | solution.py:165
  107.0 25.0 %collective-permute-start.10 = (bf16[8,128,256]{2,1,0:T(8,128)(2,1)S(1)}, bf16[8,128,256]{2,1,0:T(8,128)(2,1)S(1)}, u32[]{:S(2)}, u32[]{:S(2)}) collective-permute-start(bf16[8,128,256]{2,1,0:T(8,128)(2,1)S(1)} %all-to-all-done.4.refs_0_), channel_id=1, source_target_pairs={{0,64},{64,128},{128,192},{192,0},{1,65},{65,129},{129,193},{193,1... | collective-permute-start | bytes 1572872 | tf_op jit(solution)/shard_map/ppermute | solution.py:165
  135.0 0.8 copy-start.5

commit v3 on v2

--- a/solution.py
+++ b/solution.py
@@ -136,29 +136,42 @@
                 gl_ref[p, s, SUB * (LAT // 128) :, :] = jnp.concatenate([rope, rope], axis=1)
 
 
-def unpack_kernel(in_ref, gq_ref, gl_ref):
-    n = in_ref.shape[0]
-    for h in range(n):
-        rope = in_ref[h, ROW_GROPE:ROW_GL, :]
+def combine_kernel(rank_ref, gq_ref, gl_ref, *out_refs):
+    n_head, n_ctx = gl_ref.shape[:2]
+    for shift in range(n_ctx):
+        target = lax.rem(rank_ref[0] + shift, n_ctx)
+        out_refs[shift][:ROW_GL, :] = gq_ref[target]
+        total = gl_ref[0, target].astype(F32)
+        for i in range(1, n_head):
+            total = total + gl_ref[i, target].astype(F32)
+        out_refs[shift][ROW_GL:, :] = total.astype(BF)
+
+
+def unpack_kernel(n_ctx, rank_ref, *refs):
+    part_refs, (gq_ref, gl_ref, in_s) = refs[:n_ctx], refs[n_ctx:]
+    for shift in range(n_ctx):
+        in_s[lax.rem(rank_ref[0] + n_ctx - shift, n_ctx)] = part_refs[shift][:ROW_GL, :]
+    for h in range(n_ctx):
+        rope = in_s[h, ROW_GROPE:ROW_GL, :]
         rope = jnp.concatenate([rope[:, :ROPE], rope[:, ROPE:]], axis=0)
-        gq_ref[:, h * WIDTH : (h + 1) * WIDTH] = jnp.concatenate([in_ref[h, :NOPE, :], rope], axis=1)
+        gq_ref[:, h * WIDTH : (h + 1) * WIDTH] = jnp.concatenate([in_s[h, :NOPE, :], rope], axis=1)
+    total = part_refs[0][ROW_GL:, :].astype(F32)
+    for i in range(1, n_ctx):
+        total = total + part_refs[i][ROW_GL:, :].astype(F32)
     for j in range(LAT // 128):
-        part = in_ref[:, ROW_GL + SUB * j : ROW_GL + SUB * (j + 1), :].astype(F32)
-        gl_ref[:, 128 * j : 128 * (j + 1)] = jnp.sum(part, axis=0)
-    part = in_ref[:, ROW_GLROPE:ROWS_OUT, :ROPE].astype(F32)
-    gl_ref[:, LAT:] = jnp.sum(part, axis=0)
-
-
-def assemble_kernel(n_dp, rank_ref, *refs):
-    part_refs, (gk_ref, gv_ref) = refs[:n_dp], refs[n_dp:]
-    n_ctx, share, _ = part_refs[0].shape
-    for shift in range(n_dp):
-        source = lax.rem(rank_ref[2] + n_dp - shift, n_dp)
-        rows = pl.ds(pl.multiple_of(source * share, share), share)
-        for h in range(n_ctx):
-            part = part_refs[shift][h].astype(F32)
-            gk_ref[rows, h * NOPE : (h + 1) * NOPE] = part[:, :NOPE]
-            gv_ref[rows, h * VDIM : (h + 1) * VDIM] = part[:, NOPE:]
+        gl_ref[:, 128 * j : 128 * (j + 1)] = total[SUB * j : SUB * (j + 1)]
+    gl_ref[:, LAT:] = total[SUB * (LAT // 128) :, :ROPE]
+
+
+def assemble_kernel(group, rank_ref, in_ref, gk_ref, gv_ref):
+    n_dp, n_ctx, share, _ = in_ref.shape
+    for i, shift in enumerate(group):
+        head = lax.rem(rank_ref[0] + n_ctx - shift, n_ctx)
+        cols = pl.ds(pl.multiple_of(head * NOPE, NOPE), NOPE)
+        for d in range(n_dp):
+            part = in_ref[d, i].astype(F32)
+            gk_ref[d * share : (d + 1) * share, cols] = part[:, :NOPE]
+            gv_ref[d * share : (d + 1) * share, cols] = part[:, NOPE:]
 
 
 def shifted(x, axis, n, shift):
@@ -169,7 +182,7 @@
     return pl.BlockSpec(shape, lambda i, *scalars: (0,) * len(shape))
 
 
-def call(kernel, name, scalars, inputs, outs, scratch=(), in_specs=None, flops=0):
+def call(kernel, name, scalars, inputs, outs, scratch=(), in_specs=None, flops=0, vmem=16):
     moved = sum(x.size * x.dtype.itemsize for x in inputs) + sum(
         x.size * x.dtype.itemsize for x in outs
     )
@@ -183,7 +196,7 @@
             scratch_shapes=list(scratch),
         ),
         out_shape=list(outs),
-        compiler_params=pltpu.CompilerParams(vmem_limit_bytes=48 * 1024 * 1024),
+        compiler_params=pltpu.CompilerParams(vmem_limit_bytes=vmem * 1024 * 1024),
         cost_estimate=pl.CostEstimate(flops=flops, bytes_accessed=moved, transcendentals=0),
         name=name,
     )(*scalars, *inputs)
@@ -233,38 +246,45 @@
             pltpu.VMEM((LAT, NOPE + VDIM), BF),
         ],
         flops=3 * 10**9,
+        vmem=28,
     )
 
     gw_sum = gw_parts[0].astype(F32)
     for i in range(1, n_dp):
         gw_sum = gw_sum + shifted(gw_parts[i], "dp", n_dp, i).astype(F32)
     gw_sum = gw_sum.astype(BF)
-    gw_ctx = lax.all_to_all(
-        jnp.broadcast_to(gw_sum[None], (n_ctx,) + gw_sum.shape), "ctx", 0, 0, tiled=True
-    )
-    gw_all = [gw_ctx] + [shifted(gw_ctx, "dp", n_dp, i) for i in range(1, n_dp)]
+    group = [0, 1, n_ctx - 1] + list(range(2, n_ctx - 1))
+    gw_ctx = jnp.stack([shifted(gw_sum, "ctx", n_ctx, i) if i else gw_sum for i in group])
+
+    gl_moved = lax.all_to_all(gl_part, "head", 0, 0, tiled=True)
+    gl_moved, gw_ctx = lax.optimization_barrier((gl_moved, gw_ctx))
+    gw_all = lax.all_to_all(
+        jnp.broadcast_to(gw_ctx[None], (n_dp,) + gw_ctx.shape), "dp", 0, 0, tiled=True
+    )
+    back = call(
+        combine_kernel,
+        "combine",
+        (ranks,),
+        (gq_part, gl_moved),
+        [shape((ROWS_OUT, 128), BF)] * n_ctx,
+    )
+    back = [back[0]] + [shifted(back[i], "ctx", n_ctx, i) for i in range(1, n_ctx)]
+    grad_query, grad_latent = call(
+        functools.partial(unpack_kernel, n_ctx),
+        "unpack",
+        (ranks,),
+        back,
+        [shape((rows, n_ctx * WIDTH), BF), shape((SUB, LAT + ROPE), F32)],
+        scratch=[pltpu.VMEM((n_ctx, ROW_GL, 128), BF)],
+    )
+    grad_query, grad_latent, gw_all = lax.optimization_barrier((grad_query, grad_latent, gw_all))
     grad_w_uk, grad_w_uv = call(
-        functools.partial(assemble_kernel, n_dp),
+        functools.partial(assemble_kernel, group),
         "assemble",
         (ranks,),
-        gw_all,
+        (gw_all,),
         [shape((LAT, n_ctx * NOPE), F32), shape((LAT, n_ctx * VDIM), F32)],
     )
-
-    gl_head = jnp.sum(
-        lax.all_to_all(gl_part, "head", 0, 0, tiled=True).astype(F32), axis=0
-    ).astype(BF)
-    back = lax.all_to_all(jnp.concatenate([gq_part, gl_head], axis=1), "ctx", 0, 0, tiled=True)
-    grad_query, grad_latent = pl.pallas_call(
-        unpack_kernel,
-        out_shape=[
-            jax.ShapeDtypeStruct((rows, n_ctx * WIDTH), BF),
-            jax.ShapeDtypeStruct((SUB, LAT + ROPE), F32),
-        ],
-        in_specs=[VMEM],
-        out_specs=[VMEM, VMEM],
-        name="unpack",
-    )(back)
     return (grad_query[None], grad_latent[None], grad_w_uk, grad_w_uv)
 
 

time: 140 us -> 122 us (0.87); the launches traced: 138 us -> 121 us
  waiting for transfers between devices: 68.9 us -> 31.4 us
  starting transfers between devices: 46.4 us -> 66.5 us
  local copies, waits for them, and re-layouts: 7.46 us -> 9.15 us
    ppermute x13 -> x24, starting transfers between devices: 17 us -> 45.3 us  [shifted(): return lax.ppermute(x, axis, [(i, (i + shift) % n) for i in range(n)])]
    all_to_all x3 -> x2, waiting for transfers between devices: 24.6 us -> 1.44 us  [the longest x1 1.43 us: on_device(): lax.all_to_all(jnp.broadcast_to(gw_ctx[None], (n_dp,) + gw_ctx.shape), 'd...]
    ppermute x13 -> x24, waiting for transfers between devices: 42.1 us -> 27.8 us  [shifted(): return lax.ppermute(x, axis, [(i, (i + shift) % n) for i in range(n)])]
    all_to_all x3 -> x2, starting transfers between devices: 15.7 us -> 7.58 us  [the longest x1 3.83 us: on_device(): lax.all_to_all(jnp.broadcast_to(gw_ctx[None], (n_dp,) + gw_ctx.shape), 'd...]
    pallas_call x3 -> x5, Pallas kernels: 11.2 us -> 13.5 us  [call(): pl.pallas_call(kernel, grid_spec=pltpu.PrefetchScalarGridSpec(num_scalar_...]
    pallas_call x1 -> x0, Pallas kernels: 2 us -> none  [on_device(): pl.pallas_call(unpack_kernel, out_shape=[jax.ShapeDtypeStruct((rows, n_ct...]
    unnamed x12 -> x20, local copies, waits for them, and re-layouts: 5.22 us -> 6.17 us
  transfers between devices with their start and end apart: 18 -> 28, of which waited for: 13 -> 17; matrix products, arithmetic and copies ran while one was open for 1% -> 0% of each run, Pallas kernels for 3% -> 3%
where the time goes in v3:
time: 122 us; the launch traced here: 121 us
  starting transfers between devices  66.5 us (55%)
  waiting for transfers between devices  31.4 us (26%)
  Pallas kernels  13.5 us (11%)
  local copies, waits for them, and re-layouts  9.15 us (8%)
    ppermute x24, starting transfers between devices, shifted(): return lax.ppermute(x, axis, [(i, (i + shift) % n) for i in range(n)])  45.3 us
    ppermute x24, waiting for transfers between devices, shifted(): return lax.ppermute(x, axis, [(i, (i + shift) % n) for i in range(n)])  27.8 us
    pallas_call x5, Pallas kernels, call(): pl.pallas_call(kernel, grid_spec=pltpu.PrefetchScalarGridSpec(num_scalar_...  13.5 us
    all_to_all x1, starting transfers between devices, on_device(): lax.all_to_all(jnp.broadcast_to(latent, (n_ctx, SUB, LAT + ROPE)), 'ctx',...  8.57 us
    unnamed x20, local copies, waits for them, and re-layouts  6.17 us
    all_to_all x1, starting transfers between devices, on_device(): mine = lax.all_to_all(packed, 'ctx', 0, 0, tiled=True)  5.01 us
    all_to_all x1, starting transfers between devices, on_device(): lax.all_to_all(jnp.broadcast_to(gw_ctx[None], (n_dp,) + gw_ctx.shape), 'd...  3.83 us
    all_to_all x1, starting transfers between devices, on_device(): gl_moved = lax.all_to_all(gl_part, 'head', 0, 0, tiled=True)  3.75 us
  transfers between devices with their start and end apart: 28, of which 17 were waited for; matrix products, arithmetic and copies ran while one was open for 0% of the time, Pallas kernels for 3%

profile of v3, /device:TPU:32, one launch (start us, length us, event | category | flops | bytes accessed | tf_op | source)
XLA Modules:
  0.0 121.3 jit_solution(14283812136047713164)
XLA Ops:
  2.0 8.6 %all-to-all-start.1 = ((bf16[8,16,576]{2,1,0:T(8,128)(2,1)}), bf16[8,16,576]{2,1,0:T(8,128)(2,1)S(1)}, u32[]{:S(2)}, u32[]{:S(2)}) async-start(bf16[8,16,576]{2,1,0:T(8,128)(2,1)} %broadcast_in_dim.20), calls=%async_computation.1 | async-start | bytes 327680 | tf_op jit(solution)/shard_map/all_to_all | solution.py:211
  15.1 1.6 %pack.1 = (bf16[8,320,128]{2,1,0:T(8,128)(2,1)}, bf16[512,256]{1,0:T(8,128)(2,1)S(1)}) custom-call(s32[3]{0:T(128)S(1)} %pad_add_fusion.rank_ref, bf16[128,1536]{1,0:T(8,128)(2,1)S(1)} %bitcast.24, bf16[128,1024]{1,0:T(8,128)(2,1)S(1)} %bitcast.25, bf16[512,1024]{1,0:T(8,128)(2,1)S(1)} %copy-done, bf16[512,1024]{1,0:T(8,128)(2,1)S(1)} %copy-done.1), custom_call_target="tpu_custom_call" | custom-call | bytes 3670016 | tf_op jit(solution)/shard_map/pack/pallas_call | solution.py:189
  16.7 2.2 %all-to-all-done.1.refs_0_ = bf16[8,16,576]{2,1,0:T(8,128)(2,1)S(1)} async-done(((bf16[8,16,576]{2,1,0:T(8,128)(2,1)}), bf16[8,16,576]{2,1,0:T(8,128)(2,1)S(1)}, u32[]{:S(2)}, u32[]{:S(2)}) %all-to-all-start.1) | async-done | bytes 147488 | tf_op jit(solution)/shard_map/all_to_all | solution.py:211
  18.9 5.0 %all-to-all-start = ((bf16[8,320,128]{2,1,0:T(8,128)(2,1)}), bf16[8,320,128]{2,1,0:T(8,128)(2,1)S(1)}, u32[]{:S(2)}, u32[]{:S(2)}) async-start(bf16[8,320,128]{2,1,0:T(8,128)(2,1)} %get-tuple-element.29), calls=%async_computation | async-start | bytes 1310720 | tf_op jit(solution)/shard_map/all_to_all | solution.py:224
  25.0 1.7 %collective-permute-start.5 = (bf16[8,16,576]{2,1,0:T(8,128)(2,1)S(1)}, bf16[8,16,576]{2,1,0:T(8,128)(2,1)S(1)}, u32[]{:S(2)}, u32[]{:S(2)}) collective-permute-start(bf16[8,16,576]{2,1,0:T(8,128)(2,1)S(1)} %all-to-all-done.1.refs_0_), channel_id=1, source_target_pairs={{0,6},{1,7},{2,0},{3,1},{4,2},{5,3},{6,4},{7,5},{8,14},{9,15},{10,... | collective-permute-start | bytes 442376 | tf_op jit(solution)/shard_map/ppermute | solution.py:178
  27.3 2.7 %collective-permute-start.3 = (bf16[8,16,576]{2,1,0:T(8,128)(2,1)S(1)}, bf16[8,16,576]{2,1,0:T(8,128)(2,1)S(1)}, u32[]{:S(2)}, u32[]{:S(2)}) collective-permute-start(bf16[8,16,576]{2,1,0:T(8,128)(2,1)S(1)} %all-to-all-done.1.refs_0_), channel_id=1, source_target_pairs={{0,4},{1,5},{2,6},{3,7},{4,0},{5,1},{6,2},{7,3},{8,12},{9,13},{10,... | collective-permute-start | bytes 442376 | tf_op jit(solution)/shard_map/ppermute | solution.py:178
  30.5 3.5 %collective-permute-done.5.refs_6_ = bf16[8,16,576]{2,1,0:T(8,128)(2,1)S(1)} collective-permute-done((bf16[8,16,576]{2,1,0:T(8,128)(2,1)S(1)}, bf16[8,16,576]{2,1,0:T(8,128)(2,1)S(1)}, u32[]{:S(2)}, u32[]{:S(2)}) %collective-permute-start.5) | collective-permute-done | bytes 147488 | tf_op jit(solution)/shard_map/ppermute | solution.py:178
  34.1 4.5 %collective-permute-done.3.refs_4_ = bf16[8,16,576]{2,1,0:T(8,128)(2,1)S(1)} collective-permute-done((bf16[8,16,576]{2,1,0:T(8,128)(2,1)S(1)}, bf16[8,16,576]{2,1,0:T(8,128)(2,1)S(1)}, u32[]{:S(2)}, u32[]{:S(2)}) %collective-permute-start.3) | collective-permute-done | bytes 147488 | tf_op jit(solution)/shard_map/ppermute | solution.py:178
  38.8 6.7 %collective-permute-done.1.refs_2_ = bf16[8,16,576]{2,1,0:T(8,128)(2,1)S(1)} collective-permute-done((bf16[8,16,576]{2,1,0:T(8,128)(2,1)S(1)}, bf16[8,16,576]{2,1,0:T(8,128)(2,1)S(1)}, u32[]{:S(2)}, u32[]{:S(2)}) %collective-permute-start.1) | collective-permute-done | bytes 147488 | tf_op jit(solution)/shard_map/ppermute | solution.py:178
  45.6 6.5 %attention_backward.1 = (bf16[8,8,80,128]{3,2,1,0:T(8,128)(2,1)}, bf16[8,192,128]{2,1,0:T(8,128)(2,1)S(1)}, bf16[128,256]{1,0:T(8,128)(2,1)S(1)}, bf16[128,256]{...) custom-call(s32[16]{0:T(128)S(1)} %copy-done.6, s32[3]{0:T(128)S(1)} %pad_add_fusion.rank_ref, ...), custom_call_target="tpu_custom_call" | custom-call | flops 3000000000 | bytes 4063232 | tf_op jit(solution)/shard_map/attention_backward/pallas_call | solution.py:189
  52.9 1.6 %collective-permute-start.7 = (bf16[128,256]{1,0:T(8,128)(2,1)S(1)}, bf16[128,256]{1,0:T(8,128)(2,1)S(1)}, u32[]{:S(2)}, u32[]{:S(2)}) collective-permute-start(bf16[128,256]{1,0:T(8,128)(2,1)S(1)} %get-tuple-element.34), channel_id=1, source_target_pairs={{0,64},{64,128},{128,192},{192,0},{1,65},{65,129},{129,193},{193,1... | collective-permute-start | bytes 196616 | tf_op jit(solution)/shard_map/ppermute | solution.py:178
  54.5 2.9 %collective-permute-start.8 = (bf16[128,256]{1,0:T(8,128)(2,1)S(1)}, bf16[128,256]{1,0:T(8,128)(2,1)S(1)}, u32[]{:S(2)}, u32[]{:S(2)}) collective-permute-start(bf16[128,256]{1,0:T(8,128)(2,1)S(1)} %get-tuple-element.35), channel_id=1, source_target_pairs={{0,128},{64,192},{128,0},{192,64},{1,129},{65,193},{129,1},{193,65... | collective-permute-start | bytes 196616 | tf_op jit(solution)/shard_map/ppermute | solution.py:178
  58.7 1.6 %collective-permute-done.8 = bf16[128,256]{1,0:T(8,128)(2,1)S(1)} collective-permute-done((bf16[128,256]{1,0:T(8,128)(2,1)S(1)}, bf16[128,256]{1,0:T(8,128)(2,1)S(1)}, u32[]{:S(2)}, u32[]{:S(2)}) %collective-permute-start.8) | collective-permute-done | bytes 65568 | tf_op jit(solution)/shard_map/ppermute | solution.py:178
  61.7 1.5 %collective-permute-start.10 = (bf16[128,256]{1,0:T(8,128)(2,1)S(1)}, bf16[128,256]{1,0:T(8,128)(2,1)S(1)}, u32[]{:S(2)}, u32[]{:S(2)}) collective-permute-start(bf16[128,256]{1,0:T(8,128)(2,1)S(1)} %get-tuple-element.55), channel_id=1, source_target_pairs={{0,8},{8,16},{16,24},{24,32},{32,40},{40,48},{48,56},{56,0},{1,9},... | collective-permute-start | bytes 196616 | tf_op jit(solution)/shard_map/ppermute | solution.py:178
  63.2 3.8 %all-to-all-start.2 = ((bf16[8,8,80,128]{3,2,1,0:T(8,128)(2,1)}), bf16[8,8,80,128]{3,2,1,0:T(8,128)(2,1)S(1)}, u32[]{:S(2)}, u32[]{:S(2)}) async-start(bf16[8,8,80,128]{3,2,1,0:T(8,128)(2,1)} %get-tuple-element.32), calls=%async_computation.2 | async-start | bytes 2621440 | tf_op jit(solution)/shard_map/all_to_all | solution.py:259
  67.0 2.8 %collective-permute-start.15 = (bf16[128,256]{1,0:T(8,128)(2,1)S(1)}, bf16[128,256]{1,0:T(8,128)(2,1)S(1)}, u32[]{:S(2)}, u32[]{:S(2)}) collective-permute-start(bf16[128,256]{1,0:T(8,128)(2,1)S(1)} %get-tuple-element.55), channel_id=1, source_target_pairs={{0,40},{8,48},{16,56},{24,0},{32,8},{40,16},{48,24},{56,32},{1,41}... | collective-permute-start | bytes 196616 | tf_op jit(solution)/shard_map/ppermute | solution.py:178
  69.7 3.3 %collective-permute-start.14 = (bf16[128,256]{1,0:T(8,128)(2,1)S(1)}, bf16[128,256]{1,0:T(8,128)(2,1)S(1)}, u32[]{:S(2)}, u32[]{:S(2)}) collective-permute-start(bf16[128,256]{1,0:T(8,128)(2,1)S(1)} %get-tuple-element.55), channel_id=1, source_target_pairs={{0,32},{8,40},{16,48},{24,56},{32,0},{40,8},{48,16},{56,24},{1,33}... | collective-permute-start | bytes 196616 | tf_op jit(solution)/shard_map/ppermute | solution.py:178
  73.0 2.7 %collective-permute-start.13 = (bf16[128,256]{1,0:T(8,128)(2,1)S(1)}, bf16[128,256]{1,0:T(8,128)(2,1)S(1)}, u32[]{:S(2)}, u32[]{:S(2)}) collective-permute-start(bf16[128,256]{1,0:T(8,128)(2,1)S(1)} %get-tuple-element.55), channel_id=1, source_target_pairs={{0,24},{8,32},{16,40},{24,48},{32,56},{40,0},{48,8},{56,16},{1,25}... | collective-permute-start | bytes 196616 | tf_op jit(solution)/shard_map/ppermute | solution.py:178
  75.7 2.0 %collective-permute-start.11 = (bf16[128,256]{1,0:T(8,128)(2,1)S(1)}, bf16[128,256]{1,0:T(8,128)(2,1)S(1)}, u32[]{:S(2)}, u32[]{:S(2)}) collective-permute-start(bf16[128,256]{1,0:T(8,128)(2,1)S(1)} %get-tuple-element.55), channel_id=1, source_target_pairs={{0,56},{8,0},{16,8},{24,16},{32,24},{40,32},{48,40},{56,48},{1,57}... | collective-permute-start | bytes 196616 | tf_op jit(solution)/shard_map/ppermute | solution.py:178
  77.7 2.7 %collective-permute-done.11 = bf16[128,256]{1,0:T(8,128)(2,1)S(1)} collective-permute-done((bf16[128,256]{1,0:T(8,128)(2,1)S(1)}, bf16[128,256]{1,0:T(8,128)(2,1)S(1)}, u32[]{:S(2)}, u32[]{:S(2)}) %collective-permute-start.11) | collective-permute-done | bytes 65568 | tf_op jit(solution)/shard_map/ppermute | solution.py:178
  80.4 4.9 %collective-permute-start.16 = (bf16[128,256]{1,0:T(8,128)(2,1)S(1)}, bf16[128,256]{1,0:T(8,128)(2,1)S(1)}, u32[]{:S(2)}, u32[]{:S(2)}) collective-permute-start(bf16[128,256]{1,0:T(8,128)(2,1)S(1)} %get-tuple-element.55), channel_id=1, source_target_pairs={{0,48},{8,56},{16,0},{24,8},{32,16},{40,24},{48,32},{56,40},{1,49}... | collective-permute-start | bytes 196616 | tf_op jit(solution)/shard_map/ppermute | solution.py:178
  87.2 1.6 %broadcast_in_dim.21 = bf16[4,8,128,256]{3,2,1,0:T(8,128)(2,1)} broadcast(bf16[8,128,256]{2,1,0:T(8,128)(2,1)S(1)} %bitcast_dynamic-update-slice_fusion), dimensions={1,2,3} | broadcast | bytes 2621440 | tf_op jit(solution)/shard_map/broadcast_in_dim | solution.py:262
  88.8 3.8 %all-to-all-start.3 = ((bf16[4,8,128,256]{3,2,1,0:T(8,128)(2,1)}), bf16[4,8,128,256]{3,2,1,0:T(8,128)(2,1)S(1)}, u32[]{:S(2)}, u32[]{:S(2)}) async-start(bf16[4,8,128,256]{3,2,1,0:T(8,128)(2,1)} %broadcast_in_dim.21), calls=%async_computation.3 | async-start | bytes 4194304 | tf_op jit(solution)/shard_map/all_to_all | solution.py:261
  95.1 2.7 %collective-permute-start.18 = (bf16[272,128]{1,0:T(8,128)(2,1)S(1)}, bf16[272,128]{1,0:T(8,128)(2,1)S(1)}, u32[]{:S(2)}, u32[]{:S(2)}) collective-permute-start(bf16[272,128]{1,0:T(8,128)(2,1)S(1)} %get-tuple-element.40), channel_id=1, source_target_pairs={{0,16},{8,24},{16,32},{24,40},{32,48},{40,56},{48,0},{56,8},{1,17}... | collective-permute-start | bytes 208904 | tf_op jit(solution)/shard_map/ppermute | solution.py:178
  97.8 4.0 %collective-permute-start.19 = (bf16[272,128]{1,0:T(8,128)(2,1)S(1)}, bf16[272,128]{1,0:T(8,128)(2,1)S(1)}, u32[]{:S(2)}, u32[]{:S(2)}) collective-permute-start(bf16[272,128]{1,0:T(8,128)(2,1)S(1)} %get-tuple-element.41), channel_id=1, source_target_pairs={{0,24},{8,32},{16,40},{24,48},{32,56},{40,0},{48,8},{56,16},{1,25}... | collective-permute-start | bytes 208904 | tf_op jit(solution)/shard_map/ppermute | solution.py:178
  101.8 2.4 %collective-permute-start.20 = (bf16[272,128]{1,0:T(8,128)(2,1)S(1)}, bf16[272,128]{1,0:T(8,128)(2,1)S(1)}, u32[]{:S(2)}, u32[]{:S(2)}) collective-permute-start(bf16[272,128]{1,0:T(8,128)(2,1)S(1)} %get-tuple-element.42), channel_id=1, source_target_pairs={{0,32},{8,40},{16,48},{24,56},{32,0},{40,8},{48,16},{56,24},{1,33}... | collective-permute-start | bytes 208904 | tf_op jit(solution)/shard_map/ppermute | solution.py:178
  104.2 2.2 %collective-permute-start.21 = (bf16[272,128]{1,0:T(8,128)(2,1)S(1)}, bf16[272,128]{1,0:T(8,128)(2,1)S(1)}, u32[]{:S(2)}, u32[]{:S(2)}) collective-permute-start(bf16[272,128]{1,0:T(8,128)(2,1)S(1)} %get-tuple-element.43), channel_id=1, source_target_pairs={{0,40},{8,48},{16,56},{24,0},{32,8},{40,16},{48,24},{56,32},{1,41}... | collective-permute-start | bytes 208904 | tf_op jit(solution)/shard_map/ppermute | solution.py:178
  107.3 2.9 %collective-permute-start.23 = (bf16[272,128]{1,0:T(8,128)(2,1)S(1)}, bf16[272,128]{1,0:T(8,128)(2,1)S(1)}, u32[]{:S(2)}, u32[]{:S(2)}) collective-permute-start(bf16[272,128]{1,0:T(8,128)(2,1)S(1)} %get-tuple-element.45), channel_id=1, source_target_pairs={{0,56},{8,0},{16,8},{24,16},{32,24},{40,32},{48,40},{56,48},{1,57}... | collective-permute-start | bytes 208904 | tf_op jit(solution)/shard_map/ppermute | solution.py:178
  110.2 1.9 %collective-permute-done.20.refs_4_ = bf16[272,128]{1,0:T(8,128)(2,1)S(1)} collective-permute-done((bf16[272,128]{1,0:T(8,128)(2,1)S(1)}, bf16[272,128]{1,0:T(8,128)(2,1)S(1)}, u32[]{:S(2)}, u32[]{:S(2)}) %collective-permute-start.20) | collective-permute-done | bytes 69664 | tf_op jit(solution)/shard_map/ppermute | solution.py:178
  112.0 2.3 %collective-permute-done.21.refs_5_ = bf16[272,128]{1,0:T(8,128)(2,1)S(1)} collective-permute-done((bf16[272,128]{1,0:T(8,128)(2,1)S(1)}, bf16[272,128]{1,0:T(8,128)(2,1)S(1)}, u32[]{:S(2)}, u32[]{:S(2)}) %collective-permute-start.21) | collective-permute-done | bytes 69664 | tf_op jit(solution)/shard_map/ppermute | solution.py:178
  115.3 1.5 %unpack.1 = (bf16[128,1536]{1,0:T(8,128)(2,1)}, f32[16,576]{1,0:T(8,128)}) custom-call(s32[3]{0:T(128)S(1)} %pad_add_fusion.rank_ref, bf16[272,128]{1,0:T(8,128)(2,1)S(1)} %get-tuple-element.38.refs_0_, bf16[272,128]{1,0:T(8,128)(2,1)S(1)} %collective-permute-done.17.refs_1_, bf16[272,128]{1,0:T(8,128)(2,1)S(1)} %collective-permute-done.18.refs_2_, ...), custom_call_target="tpu_custom_call" | custom-call | bytes 987136 | tf_op jit(solution)/shard_map/unpack/pallas_call | solution.py:189
  118.2 3.1 %assemble.1 = (f32[512,1024]{1,0:T(8,128)}, f32[512,1024]{1,0:T(8,128)}) custom-call(s32[3]{0:T(128)S(1)} %pad_add_fusion.rank_ref, bf16[4,8,128,256]{3,2,1,0:T(8,128)(2,1)S(1)} %all-to-all-done.3.in_ref), custom_call_target="tpu_custom_call" | custom-call | bytes 6291456 | tf_op jit(solution)/shard_map/assemble/pallas_call | solution.py:189
  (54 shorter events, 19.6 us)
Async XLA Ops:
  2.0 16.9 %all-to-all-start.1 = ((bf16[8,16,576]{2,1,0:T(8,128)(2,1)}), bf16[8,16,576]{2,1,0:T(8,128)(2,1)S(1)}, u32[]{:S(2)}, u32[]{:S(2)}) async-start(bf16[8,16,576]{2,1,0:T(8,128)(2,1)} %broadcast_in_dim.20), calls=%async_computation.1 | async-start | bytes 327680 | tf_op jit(solution)/shard_map/all_to_all | solution.py:211
  10.6 35.0 %copy-start.6 = (s32[16]{0:T(128)S(1)}, s32[16]{0:T(128)}, u32[]{:S(2)}) copy-start(s32[16]{0:T(128)} %order_ref.1) | copy-start | bytes 196
  10.7 1.2 %copy-start = (bf16[512,1024]{1,0:T(8,128)(2,1)S(1)}, bf16[512,1024]{1,0:T(8,128)(2,1)}, u32[]{:S(2)}) copy-start(bf16[512,1024]{1,0:T(8,128)(2,1)} %wk_ref.1) | copy-start | bytes 3145732
  11.9 1.2 %copy-start.1 = (bf16[512,1024]{1,0:T(8,128)(2,1)S(1)}, bf16[512,1024]{1,0:T(8,128)(2,1)}, u32[]{:S(2)}) copy-start(bf16[512,1024]{1,0:T(8,128)(2,1)} %wv_ref.1) | copy-start | bytes 3145732
  13.1 1.0 copy-start.4
  18.9 26.7 %all-to-all-start = ((bf16[8,320,128]{2,1,0:T(8,128)(2,1)}), bf16[8,320,128]{2,1,0:T(8,128)(2,1)S(1)}, u32[]{:S(2)}, u32[]{:S(2)}) async-start(bf16[8,320,128]{2,1,0:T(8,128)(2,1)} %get-tuple-element.29), calls=%async_computation | async-start | bytes 1310720 | tf_op jit(solution)/shard_map/all_to_all | solution.py:224
  23.9 6.1 %collective-permute-start.6 = (bf16[8,16,576]{2,1,0:T(8,128)(2,1)S(1)}, bf16[8,16,576]{2,1,0:T(8,128)(2,1)S(1)}, u32[]{:S(2)}, u32[]{:S(2)}) collective-permute-start(bf16[8,16,576]{2,1,0:T(8,128)(2,1)S(1)} %all-to-all-done.1.refs_0_), channel_id=1, source_target_pairs={{0,7},{1,0},{2,1},{3,2},{4,3},{5,4},{6,5},{7,6},{8,15},{9,8},{10,9... | collective-permute-start | bytes 442376 | tf_op jit(solution)/shard_map/ppermute | solution.py:178
  25.0 8.9 %collective-permute-start.5 = (bf16[8,16,576]{2,1,0:T(8,128)(2,1)S(1)}, bf16[8,16,576]{2,1,0:T(8,128)(2,1)S(1)}, u32[]{:S(2)}, u32[]{:S(2)}) collective-permute-start(bf16[8,16,576]{2,1,0:T(8,128)(2,1)S(1)} %all-to-all-done.1.refs_0_), channel_id=1, source_target_pairs={{0,6},{1,7},{2,0},{3,1},{4,2},{5,3},{6,4},{7,5},{8,14},{9,15},{10,... | collective-permute-start | bytes 442376 | tf_op jit(solution)/shard_map/ppermute | solution.py:178
  26.7 7.4 %collective-permute-start.4 = (bf16[8,16,576]{2,1,0:T(8,128)(2,1)S(1)}, bf16[8,16,576]{2,1,0:T(8,128)(2,1)S(1)}, u32[]{:S(2)}, u32[]{:S(2)}) collective-permute-start(bf16[8,16,576]{2,1,0:T(8,128)(2,1)S(1)} %all-to-all-done.1.refs_0_), channel_id=1, source_target_pairs={{0,5},{1,6},{2,7},{3,0},{4,1},{5,2},{6,3},{7,4},{8,13},{9,14},{10,... | collective-permute-start | bytes 442376 | tf_op jit(solution)/shard_map/ppermute | solution.py:178
  27.3 11.2 %collective-permute-start.3 = (bf16[8,16,576]{2,1,0:T(8,128)(2,1)S(1)}, bf16[8,16,576]{2,1,0:T(8,128)(2,1)S(1)}, u32[]{:S(2)}, u32[]{:S(2)}) collective-permute-start(bf16[8,16,576]{2,1,0:T(8,128)(2,1)S(1)} %all-to-all-done.1.refs_0_), channel_id=1, source_target_pairs={{0,4},{1,5},{2,6},{3,7},{4,0},{5,1},{6,2},{7,3},{8,12},{9,13},{10,... | collective-permute-start | bytes 442376 | tf_op jit(solution)/shard_map/ppermute | solution.py:178
  30.1 8.7 %collective-permute-start.2 = (bf16[8,16,576]{2,1,0:T(8,128)(2,1)S(1)}, bf16[8,16,576]{2,1,0:T(8,128)(2,1)S(1)}, u32[]{:S(2)}, u32[]{:S(2)}) collective-permute-start(bf16[8,16,576]{2,1,0:T(8,128)(2,1)S(1)} %all-to-all-done.1.refs_0_), channel_id=1, source_target_pairs={{0,3},{1,4},{2,5},{3,6},{4,7},{5,0},{6,1},{7,2},{8,11},{9,12},{10,... | collective-permute-start | bytes 442376 | tf_op jit(solution)/shard_map/ppermute | solution.py:178
  30.1 15.5 %collective-permute-start.1 = (bf16[8,16,576]{2,1,0:T(8,128)(2,1)S(1)}, bf16[8,16,576]{2,1,0:T(8,128)(2,1)S(1)}, u32[]{:S(2)}, u32[]{:S(2)}) collective-permute-start(bf16[8,16,576]{2,1,0:T(8,128)(2,1)S(1)} %all-to-all-done.1.refs_0_), channel_id=1, source_target_pairs={{0,2},{1,3},{2,4},{3,5},{4,6},{5,7},{6,0},{7,1},{8,10},{9,11},{10,... | collective-permute-start | bytes 442376 | tf_op jit(solution)/shard_map/ppermute | solution.py:178
  33.9 11.7 %collective-permute-start = (bf16[8,16,576]{2,1,0:T(8,128)(2,1)S(1)}, bf16[8,16,576]{2,1,0:T(8,128)(2,1)S(1)}, u32[]{:S(2)}, u32[]{:S(2)}) collective-permute-start(bf16[8,16,576]{2,1,0:T(8,128)(2,1)S(1)} %all-to-all-done.1.refs_0_), channel_id=1, source_target_pairs={{0,1},{1,2},{2,3},{3,4},{4,5},{5,6},{6,7},{7,0},{8,9},{9,10},{10,1... | collective-permute-start | bytes 442376 | tf_op jit(solution)/shard_map/ppermute | solution.py:178
  52.9 5.8 %collective-permute-start.7 = (bf16[128,256]{1,0:T(8,128)(2,1)S(1)}, bf16[128,256]{1,0:T(8,128)(2,1)S(1)}, u32[]{:S(2)}, u32[]{:S(2)}) collective-permute-start(bf16[128,256]{1,0:T(8,128)(2,1)S(1)} %get-tuple-element.34), channel_id=1, source_target_pairs={{0,64},{64,128},{128,192},{192,0},{1,65},{65,129},{129,193},{193,1... | collective-permute-start | bytes 196616 | tf_op jit(solution)/shard_map/ppermute | solution.py:178
  54.5 5.8 %collective-permute-start.8 = (bf16[128,256]{1,0:T(8,128)(2,1)S(1)}, bf16[128,256]{1,0:T(8,128)(2,1)S(1)}, u32[]{:S(2)}, u32[]{:S(2)}) collective-permute-start(bf16[128,256]{1,0:T(8,128)(2,1)S(1)} %get-tuple-element.35), channel_id=1, source_target_pairs={{0,128},{64,192},{128,0},{192,64},{1,129},{65,193},{129,1},{193,65... | collective-permute-start | bytes 196616 | tf_op jit(solution)/shard_map/ppermute | solution.py:178
  57.4 4.3 %collective-permute-start.9 = (bf16[128,256]{1,0:T(8,128)(2,1)S(1)}, bf16[128,256]{1,0:T(8,128)(2,1)S(1)}, u32[]{:S(2)}, u32[]{:S(2)}) collective-permute-start(bf16[128,256]{1,0:T(8,128)(2,1)S(1)} %get-tuple-element.36), channel_id=1, source_target_pairs={{0,192},{64,0},{128,64},{192,128},{1,193},{65,1},{129,65},{193,129... | collective-permute-start | bytes 196616 | tf_op jit(solution)/shard_map/ppermute | solution.py:178
  61.7 14.0 %collective-permute-start.10 = (bf16[128,256]{1,0:T(8,128)(2,1)S(1)}, bf16[128,256]{1,0:T(8,128)(2,1)S(1)}, u32[]{:S(2)}, u32[]{:S(2)}) collective-permute-start(bf16[128,256]{1,0:T(8,128)(2,1)S(1)} %get-tuple-element.55), channel_id=1, source_target_pairs={{0,8},{8,16},{16,24},{24,32},{32,40},{40,48},{48,56},{56,0},{1,9},... | collective-permute-start | bytes 196616 | tf_op jit(solution)/shard_map/ppermute | solution.py:178
  63.2 24.0 %all-to-all-start.2 = ((bf16[8,8,80,128]{3,2,1,0:T(8,128)(2,1)}), bf16[8,8,80,128]{3,2,1,0:T(8,128)(2,1)S(1)}, u32[]{:S(2)}, u32[]{:S(2)}) async-start(bf16[8,8,80,128]{3,2,1,0:T(8,128)(2,1)} %get-tuple-element.32), calls=%async_computation.2 | async-start | bytes 2621440 | tf_op jit(solution)/shard_map/all_to_all | solution.py:259
  67.0 19.5 %collective-permute-start.15 = (bf16[128,256]{1,0:T(8,128)(2,1)S(1)}, bf16[128,256]{1,0:T(8,128)(2,1)S(1)}, u32[]{:S(2)}, u32[]{:S(2)}) collective-permute-start(bf16[128,256]{1,0:T(8,128)(2,1)S(1)} %get-tuple-element.55), channel_id=1, source_target_pairs={{0,40},{8,48},{16,56},{24,0},{32,8},{40,16},{48,24},{56,32},{1,41}... | collective-permute-start | bytes 196616 | tf_op jit(solution)/shard_map/ppermute | solution.py:178
  69.7 16.8 %collective-permute-start.14 = (bf16[128,256]{1,0:T(8,128)(2,1)S(1)}, bf16[128,256]{1,0:T(8,128)(2,1)S(1)}, u32[]{:S(2)}, u32[]{:S(2)}) collective-permute-start(bf16[128,256]{1,0:T(8,128)(2,1)S(1)} %get-tuple-element.55), channel_id=1, source_target_pairs={{0,32},{8,40},{16,48},{24,56},{32,0},{40,8},{48,16},{56,24},{1,33}... | collective-permute-start | bytes 196616 | tf_op jit(solution)/shard_map/ppermute | solution.py:178
  73.0 13.5 %collective-permute-start.13 = (bf16[128,256]{1,0:T(8,128)(2,1)S(1)}, bf16[128,256]{1,0:T(8,128)(2,1)S(1)}, u32[]{:S(2)}, u32[]{:S(2)}) collective-permute-start(bf16[128,256]{1,0:T(8,128)(2,1)S(1)} %get-tuple-element.55), channel_id=1, source_target_pairs={{0,24},{8,32},{16,40},{24,48},{32,56},{40,0},{48,8},{56,16},{1,25}... | collective-permute-start | bytes 196616 | tf_op jit(solution)/shard_map/ppermute | solution.py:178
  75.7 10.8 %collective-permute-start.12 = (bf16[128,256]{1,0:T(8,128)(2,1)S(1)}, bf16[128,256]{1,0:T(8,128)(2,1)S(1)}, u32[]{:S(2)}, u32[]{:S(2)}) collective-permute-start(bf16[128,256]{1,0:T(8,128)(2,1)S(1)} %get-tuple-element.55), channel_id=1, source_target_pairs={{0,16},{8,24},{16,32},{24,40},{32,48},{40,56},{48,0},{56,8},{1,17}... | collective-permute-start | bytes 196616 | tf_op jit(solution)/shard_map/ppermute | solution.py:178
  75.7 4.7 %collective-permute-start.11 = (bf16[128,256]{1,0:T(8,128)(2,1)S(1)}, bf16[128,256]{1,0:T(8,128)(2,1)S(1)}, u32[]{:S(2)}, u32[]{:S(2)}) collective-permute-start(bf16[128,256]{1,0:T(8,128)(2,1)S(1)} %get-tuple-element.55), channel_id=1, source_target_pairs={{0,56},{8,0},{16,8},{24,16},{32,24},{40,32},{48,40},{56,48},{1,57}... | collective-permute-start | bytes 196616 | tf_op jit(solution)/shard_map/ppermute | solution.py:178
  80.4 6.8 %collective-permute-start.16 = (bf16[128,256]{1,0:T(8,128)(2,1)S(1)}, bf16[128,256]{1,0:T(8,128)(2,1)S(1)}, u32[]{:S(2)}, u32[]{:S(2)}) collective-permute-start(bf16[128,256]{1,0:T(8,128)(2,1)S(1)} %get-tuple-element.55), channel_id=1, source_target_pairs={{0,48},{8,56},{16,0},{24,8},{32,16},{40,24},{48,32},{56,40},{1,49}... | collective-permute-start | bytes 196616 | tf_op jit(solution)/shard_map/ppermute | solution.py:178
  88.8 29.5 %all-to-all-start.3 = ((bf16[4,8,128,256]{3,2,1,0:T(8,128)(2,1)}), bf16[4,8,128,256]{3,2,1,0:T(8,128)(2,1)S(1)}, u32[]{:S(2)}, u32[]{:S(2)}) async-start(bf16[4,8,128,256]{3,2,1,0:T(8,128)(2,1)} %broadcast_in_dim.21), calls=%async_computation.3 | async-start | bytes 4194304 | tf_op jit(solution)/shard_map/all_to_all | solution.py:261
  94.3 12.0 %collective-permute-start.17 = (bf16[272,128]{1,0:T(8,128)(2,1)S(1)}, bf16[272,128]{1,0:T(8,128)(2,1)S(1)}, u32[]{:S(2)}, u32[]{:S(2)}) collective-permute-start(bf16[272,128]{1,0:T(8,128)(2,1)S(1)} %get-tuple-element.39), channel_id=1, source_target_pairs={{0,8},{8,16},{16,24},{24,32},{32,40},{40,48},{48,56},{56,0},{1,9},... | collective-permute-start | bytes 208904 | tf_op jit(solution)/shard_map/ppermute | solution.py:178
  95.1 12.2 %collective-permute-start.18 = (bf16[272,128]{1,0:T(8,128)(2,1)S(1)}, bf16[272,128]{1,0:T(8,128)(2,1)S(1)}, u32[]{:S(2)}, u32[]{:S(2)}) collective-permute-start(bf16[272,128]{1,0:T(8,128)(2,1)S(1)} %get-tuple-element.40), channel_id=1, source_target_pairs={{0,16},{8,24},{16,32},{24,40},{32,48},{40,56},{48,0},{56,8},{1,17}... | collective-permute-start | bytes 208904 | tf_op jit(solution)/shard_map/ppermute | solution.py:178
  97.8 12.4 %collective-permute-start.19 = (bf16[272,128]{1,0:T(8,128)(2,1)S(1)}, bf16[272,128]{1,0:T(8,128)(2,1)S(1)}, u32[]{:S(2)}, u32[]{:S(2)}) collective-permute-start(bf16[272,128]{1,0:T(8,128)(2,1)S(1)} %get-tuple-element.41), channel_id=1, source_target_pairs={{0,24},{8,32},{16,40},{24,48},{32,56},{40,0},{48,8},{56,16},{1,25}... | collective-permute-start | bytes 208904 | tf_op jit(solution)/shard_map/ppermute | solution.py:178
  101.8 10.2 %collective-permute-start.20 = (bf16[272,128]{1,0:T(8,128)(2,1)S(1)}, bf16[272,128]{1,0:T(8,128)(2,1)S(1)}, u32[]{:S(2)}, u32[]{:S(2)}) collective-permute-start(bf16[272,128]{1,0:T(8,128)(2,1)S(1)} %get-tuple-element.42), channel_id=1, source_target_pairs={{0,32},{8,40},{16,48},{24,56},{32,0},{40,8},{48,16},{56,24},{1,33}... | collective-permute-start | bytes 208904 | tf_op jit(solution)/shard_map/ppermute | solution.py:178
  104.2 10.2 %collective-permute-start.21 = (bf16[272,128]{1,0:T(8,128)(2,1)S(1)}, bf16[272,128]{1,0:T(8,128)(2,1)S(1)}, u32[]{:S(2)}, u32[]{:S(2)}) collective-permute-start(bf16[272,128]{1,0:T(8,128)(2,1)S(1)} %get-tuple-element.43), channel_id=1, source_target_pairs={{0,40},{8,48},{16,56},{24,0},{32,8},{40,16},{48,24},{56,32},{1,41}... | collective-permute-start | bytes 208904 | tf_op jit(solution)/shard_map/ppermute | solution.py:178
  106.4 8.5 %collective-permute-start.22 = (bf16[272,128]{1,0:T(8,128)(2,1)S(1)}, bf16[272,128]{1,0:T(8,128)(2,1)S(1)}, u32[]{:S(2)}, u32[]{:S(2)}) collective-permute-start(bf16[272,128]{1,0:T(8,128)(2,1)S(1)} %get-tuple-element.44), channel_id=1, source_target_pairs={{0,48},{8,56},{16,0},{24,8},{32,16},{40,24},{48,32},{56,40},{1,49}... | collective-permute-start | bytes 208904 | tf_op jit(solution)/shard_map/ppermute | solution.py:178
  107.3 8.0 %collective-permute-start.23 = (bf16[272,128]{1,0:T(8,128)(2,1)S(1)}, bf16[272,128]{1,0:T(8,128)(2,1)S(1)}, u32[]{:S(2)}, u32[]{:S(2)}) collective-permute-start(bf16[272,128]{1,0:T(8,128)(2,1)S(1)} %get-tuple-element.45), channel_id=1, source_target_pairs={{0,56},{8,0},{16,8},{24,16},{32,24},{40,32},{48,40},{56,48},{1,57}... | collective-permute-start | bytes 208904 | tf_op jit(solution)/shard_map/ppermute | solution.py:178
  (3 other events, 2.7 us)

commit v4 on v2

--- a/solution.py
+++ b/solution.py
@@ -54,9 +54,8 @@
 
 def attention_kernel(n_head, n_dp, order_ref, rank_ref, in_ref, w_ref, *refs):
     lat_refs, refs = refs[:n_head], refs[n_head:]
-    gl_ref, gq_ref = refs[:2]
-    gw_refs = refs[2 : 2 + n_dp]
-    lat_s, k_s, v_s, q_s, d_s, dk_s, dv_s, dq_s, gl_s, gw_s = refs[2 + n_dp :]
+    gl_refs, gw_refs, gq_ref = refs[:2], refs[2 : 2 + n_dp], refs[2 + n_dp]
+    lat_s, k_s, v_s, q_s, d_s, dk_s, dv_s, dq_s, gl_s, gw_s = refs[3 + n_dp :]
     blocks = in_ref.shape[0]
     seq = lat_s.shape[0]
     scale = WIDTH ** (-0.5)
@@ -127,13 +126,33 @@
             lo = half * HALF
             gq_ref[s, lo : lo + HALF, :] = dq_s[rows, :NOPE]
             gq_ref[s, ROW_GROPE:ROW_GL, half * ROPE : (half + 1) * ROPE] = dq_s[rows, NOPE:]
-            for i in range(per_half):
-                p = half * per_half + i
-                sub = pl.ds(pl.multiple_of(base + i * SUB, SUB), SUB)
+    n_x = n_head // 2
+    x, core = lax.div(rank_ref[1], 2), lax.rem(rank_ref[1], 2)
+    for flip in range(2):
+        for shift in range(n_x):
+            p = lax.rem(x + shift, n_x) * 2 + lax.rem(core + flip, 2)
+            half, i = lax.div(p, per_half), lax.rem(p, per_half)
+            for s in range(blocks):
+                sub = pl.ds(pl.multiple_of(order_ref[2 * s + half] * HALF + i * SUB, SUB), SUB)
+                out_ref = gl_refs[flip].at[shift, s]
                 for j in range(LAT // 128):
-                    gl_ref[p, s, SUB * j : SUB * (j + 1), :] = gl_s[sub, 128 * j : 128 * (j + 1)]
+                    out_ref[SUB * j : SUB * (j + 1), :] = gl_s[sub, 128 * j : 128 * (j + 1)]
                 rope = gl_s[sub, LAT:]
-                gl_ref[p, s, SUB * (LAT // 128) :, :] = jnp.concatenate([rope, rope], axis=1)
+                out_ref[SUB * (LAT // 128) :, :] = jnp.concatenate([rope, rope], axis=1)
+
+
+def fold_kernel(keep_ref, moved_ref, *out_refs):
+    for shift, out_ref in enumerate(out_refs):
+        out_ref[...] = (keep_ref[shift].astype(F32) + moved_ref[shift].astype(F32)).astype(BF)
+
+
+def combine_kernel(gq_ref, *refs):
+    gl_refs, out_ref = refs[:-1], refs[-1]
+    out_ref[:, :ROW_GL, :] = gq_ref[...]
+    total = gl_refs[0][...].astype(F32)
+    for gl_ref in gl_refs[1:]:
+        total = total + gl_ref[...].astype(F32)
+    out_ref[:, ROW_GL:, :] = total.astype(BF)
 
 
 def unpack_kernel(in_ref, gq_ref, gl_ref):
@@ -150,13 +169,15 @@
 
 
 def assemble_kernel(n_dp, rank_ref, *refs):
-    part_refs, (gk_ref, gv_ref) = refs[:n_dp], refs[n_dp:]
-    n_ctx, share, _ = part_refs[0].shape
-    for shift in range(n_dp):
-        source = lax.rem(rank_ref[2] + n_dp - shift, n_dp)
+    in_refs, (gk_ref, gv_ref) = refs[:-2], refs[-2:]
+    share = in_refs[0].shape[1]
+    half = in_refs[3].shape[0]
+    for in_ref, step, first in zip(in_refs, (0, 3, 1, 2, 2), (0, 0, 0, 0, half)):
+        source = lax.rem(rank_ref[2] + step, n_dp)
         rows = pl.ds(pl.multiple_of(source * share, share), share)
-        for h in range(n_ctx):
-            part = part_refs[shift][h].astype(F32)
+        for i in range(in_ref.shape[0]):
+            h = first + i
+            part = in_ref[i].astype(F32)
             gk_ref[rows, h * NOPE : (h + 1) * NOPE] = part[:, :NOPE]
             gv_ref[rows, h * VDIM : (h + 1) * VDIM] = part[:, NOPE:]
 
@@ -169,7 +190,7 @@
     return pl.BlockSpec(shape, lambda i, *scalars: (0,) * len(shape))
 
 
-def call(kernel, name, scalars, inputs, outs, scratch=(), in_specs=None, flops=0):
+def call(kernel, name, scalars, inputs, outs, scratch=(), in_specs=None, flops=0, vmem=16):
     moved = sum(x.size * x.dtype.itemsize for x in inputs) + sum(
         x.size * x.dtype.itemsize for x in outs
     )
@@ -183,7 +204,7 @@
             scratch_shapes=list(scratch),
         ),
         out_shape=list(outs),
-        compiler_params=pltpu.CompilerParams(vmem_limit_bytes=48 * 1024 * 1024),
+        compiler_params=pltpu.CompilerParams(vmem_limit_bytes=vmem * 1024 * 1024),
         cost_estimate=pl.CostEstimate(flops=flops, bytes_accessed=moved, transcendentals=0),
         name=name,
     )(*scalars, *inputs)
@@ -210,16 +231,14 @@
     )
     mine = lax.all_to_all(packed, "ctx", 0, 0, tiled=True)
 
-    gl_part, gq_part, *gw_parts = call(
+    gl_keep, gl_send, *gw_parts, gq_part = call(
         functools.partial(attention_kernel, n_head, n_dp),
         "attention_backward",
         (block_order, ranks),
         (mine, w_both, *lat_all),
-        [
-            shape((n_head, n_ctx, SUB * (LAT // 128) + SUB, 128), BF),
-            shape((n_ctx, ROW_GL, 128), BF),
-        ]
-        + [shape((LAT // n_dp, NOPE + VDIM), BF)] * n_dp,
+        [shape((n_head // 2, n_ctx, SUB * (LAT // 128) + SUB, 128), BF)] * 2
+        + [shape((LAT // n_dp, NOPE + VDIM), BF)] * n_dp
+        + [shape((n_ctx, ROW_GL, 128), BF)],
         scratch=[
             pltpu.VMEM((seq, LAT), BF),
             pltpu.VMEM((seq, WIDTH), BF),
@@ -233,16 +252,56 @@
             pltpu.VMEM((LAT, NOPE + VDIM), BF),
         ],
         flops=3 * 10**9,
+        vmem=28,
     )
 
     gw_sum = gw_parts[0].astype(F32)
     for i in range(1, n_dp):
         gw_sum = gw_sum + shifted(gw_parts[i], "dp", n_dp, i).astype(F32)
     gw_sum = gw_sum.astype(BF)
+    flip = [(i, i ^ 1) for i in range(n_head)]
+    gl_recv = lax.ppermute(gl_send, "head", flip)
+    gw_sum, gl_recv = lax.optimization_barrier((gw_sum, gl_recv))
+    folded = call(
+        fold_kernel,
+        "fold",
+        (),
+        (gl_keep, gl_recv),
+        [shape(gl_keep.shape[1:], BF)] * (n_head // 2),
+    )
     gw_ctx = lax.all_to_all(
         jnp.broadcast_to(gw_sum[None], (n_ctx,) + gw_sum.shape), "ctx", 0, 0, tiled=True
     )
-    gw_all = [gw_ctx] + [shifted(gw_ctx, "dp", n_dp, i) for i in range(1, n_dp)]
+    gl_moved = [folded[0]] + [
+        lax.ppermute(folded[i], "head", [(j, (j + 2 * i) % n_head) for j in range(n_head)])
+        for i in range(1, n_head // 2)
+    ]
+    gw_ctx, *gl_moved = lax.optimization_barrier((gw_ctx, *gl_moved))
+    half = n_ctx // 2
+    before, after = shifted(gw_ctx, "dp", n_dp, 1), shifted(gw_ctx, "dp", n_dp, n_dp - 1)
+    gw_all = [
+        gw_ctx,
+        before,
+        after,
+        shifted(before[:half], "dp", n_dp, 1),
+        shifted(after[half:], "dp", n_dp, n_dp - 1),
+    ]
+    back = call(
+        combine_kernel,
+        "combine",
+        (),
+        (gq_part, *gl_moved),
+        [shape((n_ctx, ROWS_OUT, 128), BF)],
+    )[0]
+    back = lax.all_to_all(back, "ctx", 0, 0, tiled=True)
+    grad_query, grad_latent = call(
+        unpack_kernel,
+        "unpack",
+        (),
+        (back,),
+        [shape((rows, n_ctx * WIDTH), BF), shape((SUB, LAT + ROPE), F32)],
+    )
+    grad_query, grad_latent, *gw_all = lax.optimization_barrier((grad_query, grad_latent, *gw_all))
     grad_w_uk, grad_w_uv = call(
         functools.partial(assemble_kernel, n_dp),
         "assemble",
@@ -250,21 +309,6 @@
         gw_all,
         [shape((LAT, n_ctx * NOPE), F32), shape((LAT, n_ctx * VDIM), F32)],
     )
-
-    gl_head = jnp.sum(
-        lax.all_to_all(gl_part, "head", 0, 0, tiled=True).astype(F32), axis=0
-    ).astype(BF)
-    back = lax.all_to_all(jnp.concatenate([gq_part, gl_head], axis=1), "ctx", 0, 0, tiled=True)
-    grad_query, grad_latent = pl.pallas_call(
-        unpack_kernel,
-        out_shape=[
-            jax.ShapeDtypeStruct((rows, n_ctx * WIDTH), BF),
-            jax.ShapeDtypeStruct((SUB, LAT + ROPE), F32),
-        ],
-        in_specs=[VMEM],
-        out_specs=[VMEM, VMEM],
-        name="unpack",
-    )(back)
     return (grad_query[None], grad_latent[None], grad_w_uk, grad_w_uv)
 
 

time: 140 us -> 115 us (0.82); the launches traced: 138 us -> 115 us
  waiting for transfers between devices: 68.9 us -> 48.5 us
    all_to_all x1, waiting for transfers between devices: 14.8 us -> 5.08 us  [on_device(): lax.all_to_all(jnp.broadcast_to(gw_sum[None], (n_ctx,) + gw_sum.shape), '...]
    all_to_all x2 -> x1, waiting for transfers between devices: 9.83 us -> 0.48 us  [on_device(): back = lax.all_to_all(back, 'ctx', 0, 0, tiled=True)]
    ppermute x13 -> x14, waiting for transfers between devices: 42.1 us -> 34.1 us  [shifted(): return lax.ppermute(x, axis, [(i, (i + shift) % n) for i in range(n)])]
    ppermute x0 -> x4, waiting for transfers between devices: none -> 6.65 us  [the longest x3 6.65 us: on_device(): lax.ppermute(folded[i], 'head', [(j, (j + 2 * i) % n_head) for j in range...]
    ppermute x0 -> x4, starting transfers between devices: none -> 3.59 us  [the longest x3 3.5 us: on_device(): lax.ppermute(folded[i], 'head', [(j, (j + 2 * i) % n_head) for j in range...]
    all_to_all x2 -> x1, starting transfers between devices: 8.47 us -> 4.9 us  [on_device(): back = lax.all_to_all(back, 'ctx', 0, 0, tiled=True)]
    pallas_call x1 -> x0, Pallas kernels: 2 us -> none  [on_device(): pl.pallas_call(unpack_kernel, out_shape=[jax.ShapeDtypeStruct((rows, n_ct...]
    pallas_call x3 -> x6, Pallas kernels: 11.2 us -> 12.2 us  [call(): pl.pallas_call(kernel, grid_spec=pltpu.PrefetchScalarGridSpec(num_scalar_...]
  transfers between devices with their start and end apart: 18 -> 22, of which waited for: 13 -> 16; matrix products, arithmetic and copies ran while one was open for 1% -> 0% of each run, Pallas kernels for 3% -> 2%
where the time goes in v4:
time: 115 us
  waiting for transfers between devices  48.5 us (42%)
  starting transfers between devices  46.6 us (41%)
  Pallas kernels  12.2 us (11%)
  local copies, waits for them, and re-layouts  6.67 us (6%)
    ppermute x14, waiting for transfers between devices, shifted(): return lax.ppermute(x, axis, [(i, (i + shift) % n) for i in range(n)])  34.1 us
    ppermute x14, starting transfers between devices, shifted(): return lax.ppermute(x, axis, [(i, (i + shift) % n) for i in range(n)])  17.3 us
    pallas_call x6, Pallas kernels, call(): pl.pallas_call(kernel, grid_spec=pltpu.PrefetchScalarGridSpec(num_scalar_...  12.2 us
    all_to_all x1, starting transfers between devices, on_device(): lax.all_to_all(jnp.broadcast_to(latent, (n_ctx, SUB, LAT + ROPE)), 'ctx',...  8.57 us
    all_to_all x1, starting transfers between devices, on_device(): lax.all_to_all(jnp.broadcast_to(gw_sum[None], (n_ctx,) + gw_sum.shape), '...  7.21 us
    ppermute x3, waiting for transfers between devices, on_device(): lax.ppermute(folded[i], 'head', [(j, (j + 2 * i) % n_head) for j in range...  6.65 us
    all_to_all x1, waiting for transfers between devices, on_device(): lax.all_to_all(jnp.broadcast_to(gw_sum[None], (n_ctx,) + gw_sum.shape), '...  5.08 us
    all_to_all x1, starting transfers between devices, on_device(): mine = lax.all_to_all(packed, 'ctx', 0, 0, tiled=True)  5.01 us
  transfers between devices with their start and end apart: 22, of which 16 were waited for; matrix products, arithmetic and copies ran while one was open for 0% of the time, Pallas kernels for 2%

profile of v4, /device:TPU:32, one launch (start us, length us, event | category | flops | bytes accessed | tf_op | source)
XLA Modules:
  0.0 114.8 jit_solution(17381969627387359051)
XLA Ops:
  0.6 1.4 %broadcast_in_dim.20 = bf16[8,16,576]{2,1,0:T(8,128)(2,1)} broadcast(bf16[16,576]{1,0:T(8,128)(2,1)} %bitcast.10), dimensions={1,2} | broadcast | bytes 165888 | tf_op jit(solution)/shard_map/broadcast_in_dim | solution.py:220
  2.0 8.6 %all-to-all-start.1 = ((bf16[8,16,576]{2,1,0:T(8,128)(2,1)}), bf16[8,16,576]{2,1,0:T(8,128)(2,1)S(1)}, u32[]{:S(2)}, u32[]{:S(2)}) async-start(bf16[8,16,576]{2,1,0:T(8,128)(2,1)} %broadcast_in_dim.20), calls=%async_computation.1 | async-start | bytes 327680 | tf_op jit(solution)/shard_map/all_to_all | solution.py:219
  10.7 1.2 %copy-done = bf16[512,1024]{1,0:T(8,128)(2,1)S(1)} copy-done((bf16[512,1024]{1,0:T(8,128)(2,1)S(1)}, bf16[512,1024]{1,0:T(8,128)(2,1)}, u32[]{:S(2)}) %copy-start) | copy-done | bytes 1048600
  11.9 1.2 %copy-done.1 = bf16[512,1024]{1,0:T(8,128)(2,1)S(1)} copy-done((bf16[512,1024]{1,0:T(8,128)(2,1)S(1)}, bf16[512,1024]{1,0:T(8,128)(2,1)}, u32[]{:S(2)}) %copy-start.1) | copy-done | bytes 1048600
  13.1 1.0 copy-done.2
  14.1 0.9 copy-done.3
  15.1 1.6 %pack.1 = (bf16[8,320,128]{2,1,0:T(8,128)(2,1)}, bf16[512,256]{1,0:T(8,128)(2,1)S(1)}) custom-call(s32[3]{0:T(128)S(1)} %pad_add_fusion.rank_ref, bf16[128,1536]{1,0:T(8,128)(2,1)S(1)} %bitcast.8, bf16[128,1024]{1,0:T(8,128)(2,1)S(1)} %bitcast.9, bf16[512,1024]{1,0:T(8,128)(2,1)S(1)} %copy-done, bf16[512,1024]{1,0:T(8,128)(2,1)S(1)} %copy-done.1), custom_call_target="tpu_custom_call" | custom-call | bytes 3670016 | tf_op jit(solution)/shard_map/pack/pallas_call | solution.py:197
  16.7 2.2 %all-to-all-done.1.refs_0_ = bf16[8,16,576]{2,1,0:T(8,128)(2,1)S(1)} async-done(((bf16[8,16,576]{2,1,0:T(8,128)(2,1)}), bf16[8,16,576]{2,1,0:T(8,128)(2,1)S(1)}, u32[]{:S(2)}, u32[]{:S(2)}) %all-to-all-start.1) | async-done | bytes 147488 | tf_op jit(solution)/shard_map/all_to_all | solution.py:219
  18.9 5.0 %all-to-all-start = ((bf16[8,320,128]{2,1,0:T(8,128)(2,1)}), bf16[8,320,128]{2,1,0:T(8,128)(2,1)S(1)}, u32[]{:S(2)}, u32[]{:S(2)}) async-start(bf16[8,320,128]{2,1,0:T(8,128)(2,1)} %get-tuple-element.35), calls=%async_computation | async-start | bytes 1310720 | tf_op jit(solution)/shard_map/all_to_all | solution.py:232
  23.9 1.1 collective-permute-start.6
  25.0 1.7 %collective-permute-start.5 = (bf16[8,16,576]{2,1,0:T(8,128)(2,1)S(1)}, bf16[8,16,576]{2,1,0:T(8,128)(2,1)S(1)}, u32[]{:S(2)}, u32[]{:S(2)}) collective-permute-start(bf16[8,16,576]{2,1,0:T(8,128)(2,1)S(1)} %all-to-all-done.1.refs_0_), channel_id=1, source_target_pairs={{0,6},{1,7},{2,0},{3,1},{4,2},{5,3},{6,4},{7,5},{8,14},{9,15},{10,... | collective-permute-start | bytes 442376 | tf_op jit(solution)/shard_map/ppermute | solution.py:186
  27.3 2.7 %collective-permute-start.3 = (bf16[8,16,576]{2,1,0:T(8,128)(2,1)S(1)}, bf16[8,16,576]{2,1,0:T(8,128)(2,1)S(1)}, u32[]{:S(2)}, u32[]{:S(2)}) collective-permute-start(bf16[8,16,576]{2,1,0:T(8,128)(2,1)S(1)} %all-to-all-done.1.refs_0_), channel_id=1, source_target_pairs={{0,4},{1,5},{2,6},{3,7},{4,0},{5,1},{6,2},{7,3},{8,12},{9,13},{10,... | collective-permute-start | bytes 442376 | tf_op jit(solution)/shard_map/ppermute | solution.py:186
  30.5 3.5 %collective-permute-done.5.refs_6_ = bf16[8,16,576]{2,1,0:T(8,128)(2,1)S(1)} collective-permute-done((bf16[8,16,576]{2,1,0:T(8,128)(2,1)S(1)}, bf16[8,16,576]{2,1,0:T(8,128)(2,1)S(1)}, u32[]{:S(2)}, u32[]{:S(2)}) %collective-permute-start.5) | collective-permute-done | bytes 147488 | tf_op jit(solution)/shard_map/ppermute | solution.py:186
  34.1 4.5 %collective-permute-done.3.refs_4_ = bf16[8,16,576]{2,1,0:T(8,128)(2,1)S(1)} collective-permute-done((bf16[8,16,576]{2,1,0:T(8,128)(2,1)S(1)}, bf16[8,16,576]{2,1,0:T(8,128)(2,1)S(1)}, u32[]{:S(2)}, u32[]{:S(2)}) %collective-permute-start.3) | collective-permute-done | bytes 147488 | tf_op jit(solution)/shard_map/ppermute | solution.py:186
  38.8 6.7 %collective-permute-done.1.refs_2_ = bf16[8,16,576]{2,1,0:T(8,128)(2,1)S(1)} collective-permute-done((bf16[8,16,576]{2,1,0:T(8,128)(2,1)S(1)}, bf16[8,16,576]{2,1,0:T(8,128)(2,1)S(1)}, u32[]{:S(2)}, u32[]{:S(2)}) %collective-permute-start.1) | collective-permute-done | bytes 147488 | tf_op jit(solution)/shard_map/ppermute | solution.py:186
  45.6 5.5 %attention_backward.1 = (bf16[4,8,80,128]{3,2,1,0:T(8,128)(2,1)S(1)}, bf16[4,8,80,128]{3,2,1,0:T(8,128)(2,1)S(1)}, bf16[128,256]{1,0:T(8,128)(2,1)S(1)}, bf16[12...) custom-call(s32[16]{0:T(128)S(1)} %copy-done.4, ...), custom_call_target="tpu_custom_call" | custom-call | flops 3000000000 | bytes 4063232 | tf_op jit(solution)/shard_map/attention_backward/pallas_call | solution.py:197
  51.2 1.7 %collective-permute-start.7 = (bf16[128,256]{1,0:T(8,128)(2,1)S(1)}, bf16[128,256]{1,0:T(8,128)(2,1)S(1)}, u32[]{:S(2)}, u32[]{:S(2)}) collective-permute-start(bf16[128,256]{1,0:T(8,128)(2,1)S(1)} %get-tuple-element.39), channel_id=1, source_target_pairs={{0,64},{64,128},{128,192},{192,0},{1,65},{65,129},{129,193},{193,1... | collective-permute-start | bytes 196616 | tf_op jit(solution)/shard_map/ppermute | solution.py:186
  52.9 2.9 %collective-permute-start.8 = (bf16[128,256]{1,0:T(8,128)(2,1)S(1)}, bf16[128,256]{1,0:T(8,128)(2,1)S(1)}, u32[]{:S(2)}, u32[]{:S(2)}) collective-permute-start(bf16[128,256]{1,0:T(8,128)(2,1)S(1)} %get-tuple-element.40), channel_id=1, source_target_pairs={{0,128},{64,192},{128,0},{192,64},{1,129},{65,193},{129,1},{193,65... | collective-permute-start | bytes 196616 | tf_op jit(solution)/shard_map/ppermute | solution.py:186
  55.8 1.3 %collective-permute-start.9 = (bf16[128,256]{1,0:T(8,128)(2,1)S(1)}, bf16[128,256]{1,0:T(8,128)(2,1)S(1)}, u32[]{:S(2)}, u32[]{:S(2)}) collective-permute-start(bf16[128,256]{1,0:T(8,128)(2,1)S(1)} %get-tuple-element.41), channel_id=1, source_target_pairs={{0,192},{64,0},{128,64},{192,128},{1,193},{65,1},{129,65},{193,129... | collective-permute-start | bytes 196616 | tf_op jit(solution)/shard_map/ppermute | solution.py:186
  57.1 2.5 %collective-permute-done.8 = bf16[128,256]{1,0:T(8,128)(2,1)S(1)} collective-permute-done((bf16[128,256]{1,0:T(8,128)(2,1)S(1)}, bf16[128,256]{1,0:T(8,128)(2,1)S(1)}, u32[]{:S(2)}, u32[]{:S(2)}) %collective-permute-start.8) | collective-permute-done | bytes 65568 | tf_op jit(solution)/shard_map/ppermute | solution.py:186
  60.9 7.2 %all-to-all-start.2 = ((bf16[8,128,256]{2,1,0:T(8,128)(2,1)}), bf16[8,128,256]{2,1,0:T(8,128)(2,1)S(1)}, u32[]{:S(2)}, u32[]{:S(2)}) async-start(bf16[8,128,256]{2,1,0:T(8,128)(2,1)} %broadcast_in_dim.21), calls=%async_computation.2 | async-start | bytes 1048576 | tf_op jit(solution)/shard_map/all_to_all | solution.py:272
  68.4 2.0 %collective-permute-start.12 = (bf16[8,80,128]{2,1,0:T(8,128)(2,1)S(1)}, bf16[8,80,128]{2,1,0:T(8,128)(2,1)S(1)}, u32[]{:S(2)}, u32[]{:S(2)}) collective-permute-start(bf16[8,80,128]{2,1,0:T(8,128)(2,1)S(1)} %get-tuple-element.48), channel_id=1, source_target_pairs={{0,4},{1,5},{2,6},{3,7},{4,0},{5,1},{6,2},{7,3},{8,12},{9,13},{10,... | collective-permute-start | bytes 491528 | tf_op jit(solution)/shard_map/ppermute | solution.py:276
  70.4 1.4 %collective-permute-start.13 = (bf16[8,80,128]{2,1,0:T(8,128)(2,1)S(1)}, bf16[8,80,128]{2,1,0:T(8,128)(2,1)S(1)}, u32[]{:S(2)}, u32[]{:S(2)}) collective-permute-start(bf16[8,80,128]{2,1,0:T(8,128)(2,1)S(1)} %get-tuple-element.49), channel_id=1, source_target_pairs={{0,6},{1,7},{2,0},{3,1},{4,2},{5,3},{6,4},{7,5},{8,14},{9,15},{10,... | collective-permute-start | bytes 491528 | tf_op jit(solution)/shard_map/ppermute | solution.py:276
  71.8 6.0 %collective-permute-done.11.refs_1_ = bf16[8,80,128]{2,1,0:T(8,128)(2,1)S(1)} collective-permute-done((bf16[8,80,128]{2,1,0:T(8,128)(2,1)S(1)}, bf16[8,80,128]{2,1,0:T(8,128)(2,1)S(1)}, u32[]{:S(2)}, u32[]{:S(2)}) %collective-permute-start.11) | collective-permute-done | bytes 163872 | tf_op jit(solution)/shard_map/ppermute | solution.py:276
  78.5 5.1 %all-to-all-done.2.refs_0_ = bf16[8,128,256]{2,1,0:T(8,128)(2,1)S(1)} async-done(((bf16[8,128,256]{2,1,0:T(8,128)(2,1)}), bf16[8,128,256]{2,1,0:T(8,128)(2,1)S(1)}, u32[]{:S(2)}, u32[]{:S(2)}) %all-to-all-start.2) | async-done | bytes 524320 | tf_op jit(solution)/shard_map/all_to_all | solution.py:272
  84.5 4.9 %all-to-all-start.3 = ((bf16[8,272,128]{2,1,0:T(8,128)(2,1)}), bf16[8,272,128]{2,1,0:T(8,128)(2,1)S(1)}, u32[]{:S(2)}, u32[]{:S(2)}) async-start(bf16[8,272,128]{2,1,0:T(8,128)(2,1)} %combine.1), calls=%async_computation.3 | async-start | bytes 1114112 | tf_op jit(solution)/shard_map/all_to_all | solution.py:296
  89.4 2.1 %collective-permute-start.15 = (bf16[8,128,256]{2,1,0:T(8,128)(2,1)S(1)}, bf16[8,128,256]{2,1,0:T(8,128)(2,1)S(1)}, u32[]{:S(2)}, u32[]{:S(2)}) collective-permute-start(bf16[8,128,256]{2,1,0:T(8,128)(2,1)S(1)} %all-to-all-done.2.refs_0_), channel_id=1, source_target_pairs={{0,192},{64,0},{128,64},{192,128},{1,193},{65,1},{129,65},{193,129... | collective-permute-start | bytes 1572872 | tf_op jit(solution)/shard_map/ppermute | solution.py:186
  91.5 9.9 %collective-permute-done.15.refs_2_ = bf16[8,128,256]{2,1,0:T(8,128)(2,1)S(1)} collective-permute-done((bf16[8,128,256]{2,1,0:T(8,128)(2,1)S(1)}, bf16[8,128,256]{2,1,0:T(8,128)(2,1)S(1)}, u32[]{:S(2)}, u32[]{:S(2)}) %collective-permute-start.15) | collective-permute-done | bytes 524320 | tf_op jit(solution)/shard_map/ppermute | solution.py:186
  101.4 2.7 %collective-permute-start.17 = (bf16[4,128,256]{2,1,0:T(8,128)(2,1)S(1)}, bf16[4,128,256]{2,1,0:T(8,128)(2,1)S(1)}, u32[]{:S(2)}, u32[]{:S(2)}) collective-permute-start(bf16[4,128,256]{2,1,0:T(8,128)(2,1)S(1)} %slice.9), channel_id=1, source_target_pairs={{0,192},{64,0},{128,64},{192,128},{1,193},{65,1},{129,65},{193,129... | collective-permute-start | bytes 786440 | tf_op jit(solution)/shard_map/ppermute | solution.py:186
  105.6 2.4 %collective-permute-done.17.refs_4_ = bf16[4,128,256]{2,1,0:T(8,128)(2,1)S(1)} collective-permute-done((bf16[4,128,256]{2,1,0:T(8,128)(2,1)S(1)}, bf16[4,128,256]{2,1,0:T(8,128)(2,1)S(1)}, u32[]{:S(2)}, u32[]{:S(2)}) %collective-permute-start.17) | collective-permute-done | bytes 262176 | tf_op jit(solution)/shard_map/ppermute | solution.py:186
  108.0 3.8 %collective-permute-done.16.refs_3_ = bf16[4,128,256]{2,1,0:T(8,128)(2,1)S(1)} collective-permute-done((bf16[4,128,256]{2,1,0:T(8,128)(2,1)S(1)}, bf16[4,128,256]{2,1,0:T(8,128)(2,1)S(1)}, u32[]{:S(2)}, u32[]{:S(2)}) %collective-permute-start.16) | collective-permute-done | bytes 262176 | tf_op jit(solution)/shard_map/ppermute | solution.py:186
  111.8 3.0 %assemble.1 = (f32[512,1024]{1,0:T(8,128)}, f32[512,1024]{1,0:T(8,128)}) custom-call(s32[3]{0:T(128)S(1)} %pad_add_fusion.rank_ref, bf16[8,128,256]{2,1,0:T(8,128)(2,1)S(1)} %all-to-all-done.2.refs_0_, bf16[8,128,256]{2,1,0:T(8,128)(2,1)S(1)} %collective-permute-done.14.refs_1_, bf16[8,128,256]{2,1,0:T(8,128)(2,1)S(1)} %collective-permute-done.15.refs_2_, ...), custom_call_target="tpu_custom_call" | custom-call | bytes 6291456 | tf_op jit(solution)/shard_map/assemble/pallas_call | solution.py:197
  (34 shorter events, 6.3 us)
Async XLA Ops:
  2.0 16.9 %all-to-all-start.1 = ((bf16[8,16,576]{2,1,0:T(8,128)(2,1)}), bf16[8,16,576]{2,1,0:T(8,128)(2,1)S(1)}, u32[]{:S(2)}, u32[]{:S(2)}) async-start(bf16[8,16,576]{2,1,0:T(8,128)(2,1)} %broadcast_in_dim.20), calls=%async_computation.1 | async-start | bytes 327680 | tf_op jit(solution)/shard_map/all_to_all | solution.py:219
  10.6 35.0 %copy-start.4 = (s32[16]{0:T(128)S(1)}, s32[16]{0:T(128)}, u32[]{:S(2)}) copy-start(s32[16]{0:T(128)} %order_ref.1) | copy-start | bytes 196
  10.7 1.2 %copy-start = (bf16[512,1024]{1,0:T(8,128)(2,1)S(1)}, bf16[512,1024]{1,0:T(8,128)(2,1)}, u32[]{:S(2)}) copy-start(bf16[512,1024]{1,0:T(8,128)(2,1)} %wk_ref.1) | copy-start | bytes 3145732
  11.9 1.2 %copy-start.1 = (bf16[512,1024]{1,0:T(8,128)(2,1)S(1)}, bf16[512,1024]{1,0:T(8,128)(2,1)}, u32[]{:S(2)}) copy-start(bf16[512,1024]{1,0:T(8,128)(2,1)} %wv_ref.1) | copy-start | bytes 3145732
  13.1 1.0 copy-start.2
  14.1 0.9 copy-start.3
  18.9 26.7 %all-to-all-start = ((bf16[8,320,128]{2,1,0:T(8,128)(2,1)}), bf16[8,320,128]{2,1,0:T(8,128)(2,1)S(1)}, u32[]{:S(2)}, u32[]{:S(2)}) async-start(bf16[8,320,128]{2,1,0:T(8,128)(2,1)} %get-tuple-element.35), calls=%async_computation | async-start | bytes 1310720 | tf_op jit(solution)/shard_map/all_to_all | solution.py:232
  23.9 6.1 %collective-permute-start.6 = (bf16[8,16,576]{2,1,0:T(8,128)(2,1)S(1)}, bf16[8,16,576]{2,1,0:T(8,128)(2,1)S(1)}, u32[]{:S(2)}, u32[]{:S(2)}) collective-permute-start(bf16[8,16,576]{2,1,0:T(8,128)(2,1)S(1)} %all-to-all-done.1.refs_0_), channel_id=1, source_target_pairs={{0,7},{1,0},{2,1},{3,2},{4,3},{5,4},{6,5},{7,6},{8,15},{9,8},{10,9... | collective-permute-start | bytes 442376 | tf_op jit(solution)/shard_map/ppermute | solution.py:186
  25.0 8.9 %collective-permute-start.5 = (bf16[8,16,576]{2,1,0:T(8,128)(2,1)S(1)}, bf16[8,16,576]{2,1,0:T(8,128)(2,1)S(1)}, u32[]{:S(2)}, u32[]{:S(2)}) collective-permute-start(bf16[8,16,576]{2,1,0:T(8,128)(2,1)S(1)} %all-to-all-done.1.refs_0_), channel_id=1, source_target_pairs={{0,6},{1,7},{2,0},{3,1},{4,2},{5,3},{6,4},{7,5},{8,14},{9,15},{10,... | collective-permute-start | bytes 442376 | tf_op jit(solution)/shard_map/ppermute | solution.py:186
  26.7 7.4 %collective-permute-start.4 = (bf16[8,16,576]{2,1,0:T(8,128)(2,1)S(1)}, bf16[8,16,576]{2,1,0:T(8,128)(2,1)S(1)}, u32[]{:S(2)}, u32[]{:S(2)}) collective-permute-start(bf16[8,16,576]{2,1,0:T(8,128)(2,1)S(1)} %all-to-all-done.1.refs_0_), channel_id=1, source_target_pairs={{0,5},{1,6},{2,7},{3,0},{4,1},{5,2},{6,3},{7,4},{8,13},{9,14},{10,... | collective-permute-start | bytes 442376 | tf_op jit(solution)/shard_map/ppermute | solution.py:186
  27.3 11.2 %collective-permute-start.3 = (bf16[8,16,576]{2,1,0:T(8,128)(2,1)S(1)}, bf16[8,16,576]{2,1,0:T(8,128)(2,1)S(1)}, u32[]{:S(2)}, u32[]{:S(2)}) collective-permute-start(bf16[8,16,576]{2,1,0:T(8,128)(2,1)S(1)} %all-to-all-done.1.refs_0_), channel_id=1, source_target_pairs={{0,4},{1,5},{2,6},{3,7},{4,0},{5,1},{6,2},{7,3},{8,12},{9,13},{10,... | collective-permute-start | bytes 442376 | tf_op jit(solution)/shard_map/ppermute | solution.py:186
  30.1 8.7 %collective-permute-start.2 = (bf16[8,16,576]{2,1,0:T(8,128)(2,1)S(1)}, bf16[8,16,576]{2,1,0:T(8,128)(2,1)S(1)}, u32[]{:S(2)}, u32[]{:S(2)}) collective-permute-start(bf16[8,16,576]{2,1,0:T(8,128)(2,1)S(1)} %all-to-all-done.1.refs_0_), channel_id=1, source_target_pairs={{0,3},{1,4},{2,5},{3,6},{4,7},{5,0},{6,1},{7,2},{8,11},{9,12},{10,... | collective-permute-start | bytes 442376 | tf_op jit(solution)/shard_map/ppermute | solution.py:186
  30.1 15.5 %collective-permute-start.1 = (bf16[8,16,576]{2,1,0:T(8,128)(2,1)S(1)}, bf16[8,16,576]{2,1,0:T(8,128)(2,1)S(1)}, u32[]{:S(2)}, u32[]{:S(2)}) collective-permute-start(bf16[8,16,576]{2,1,0:T(8,128)(2,1)S(1)} %all-to-all-done.1.refs_0_), channel_id=1, source_target_pairs={{0,2},{1,3},{2,4},{3,5},{4,6},{5,7},{6,0},{7,1},{8,10},{9,11},{10,... | collective-permute-start | bytes 442376 | tf_op jit(solution)/shard_map/ppermute | solution.py:186
  33.9 11.7 %collective-permute-start = (bf16[8,16,576]{2,1,0:T(8,128)(2,1)S(1)}, bf16[8,16,576]{2,1,0:T(8,128)(2,1)S(1)}, u32[]{:S(2)}, u32[]{:S(2)}) collective-permute-start(bf16[8,16,576]{2,1,0:T(8,128)(2,1)S(1)} %all-to-all-done.1.refs_0_), channel_id=1, source_target_pairs={{0,1},{1,2},{2,3},{3,4},{4,5},{5,6},{6,7},{7,0},{8,9},{9,10},{10,1... | collective-permute-start | bytes 442376 | tf_op jit(solution)/shard_map/ppermute | solution.py:186
  51.1 9.0 %collective-permute-start.10 = (bf16[4,8,80,128]{3,2,1,0:T(8,128)(2,1)S(1)}, bf16[4,8,80,128]{3,2,1,0:T(8,128)(2,1)S(1)}, u32[]{:S(2)}, u32[]{:S(2)}) collective-permute-start(bf16[4,8,80,128]{3,2,1,0:T(8,128)(2,1)S(1)} %get-tuple-element.42), channel_id=1, source_target_pairs={{0,1},{1,0},{2,3},{3,2},{4,5},{5,4},{6,7},{7,6},{8,9},{9,8},{10,11... | collective-permute-start | bytes 1966088 | tf_op jit(solution)/shard_map/ppermute | solution.py:263
  51.2 5.9 %collective-permute-start.7 = (bf16[128,256]{1,0:T(8,128)(2,1)S(1)}, bf16[128,256]{1,0:T(8,128)(2,1)S(1)}, u32[]{:S(2)}, u32[]{:S(2)}) collective-permute-start(bf16[128,256]{1,0:T(8,128)(2,1)S(1)} %get-tuple-element.39), channel_id=1, source_target_pairs={{0,64},{64,128},{128,192},{192,0},{1,65},{65,129},{129,193},{193,1... | collective-permute-start | bytes 196616 | tf_op jit(solution)/shard_map/ppermute | solution.py:186
  52.9 6.7 %collective-permute-start.8 = (bf16[128,256]{1,0:T(8,128)(2,1)S(1)}, bf16[128,256]{1,0:T(8,128)(2,1)S(1)}, u32[]{:S(2)}, u32[]{:S(2)}) collective-permute-start(bf16[128,256]{1,0:T(8,128)(2,1)S(1)} %get-tuple-element.40), channel_id=1, source_target_pairs={{0,128},{64,192},{128,0},{192,64},{1,129},{65,193},{129,1},{193,65... | collective-permute-start | bytes 196616 | tf_op jit(solution)/shard_map/ppermute | solution.py:186
  55.8 4.3 %collective-permute-start.9 = (bf16[128,256]{1,0:T(8,128)(2,1)S(1)}, bf16[128,256]{1,0:T(8,128)(2,1)S(1)}, u32[]{:S(2)}, u32[]{:S(2)}) collective-permute-start(bf16[128,256]{1,0:T(8,128)(2,1)S(1)} %get-tuple-element.41), channel_id=1, source_target_pairs={{0,192},{64,0},{128,64},{192,128},{1,193},{65,1},{129,65},{193,129... | collective-permute-start | bytes 196616 | tf_op jit(solution)/shard_map/ppermute | solution.py:186
  60.9 22.6 %all-to-all-start.2 = ((bf16[8,128,256]{2,1,0:T(8,128)(2,1)}), bf16[8,128,256]{2,1,0:T(8,128)(2,1)S(1)}, u32[]{:S(2)}, u32[]{:S(2)}) async-start(bf16[8,128,256]{2,1,0:T(8,128)(2,1)} %broadcast_in_dim.21), calls=%async_computation.2 | async-start | bytes 1048576 | tf_op jit(solution)/shard_map/all_to_all | solution.py:272
  68.3 9.5 %collective-permute-start.11 = (bf16[8,80,128]{2,1,0:T(8,128)(2,1)S(1)}, bf16[8,80,128]{2,1,0:T(8,128)(2,1)S(1)}, u32[]{:S(2)}, u32[]{:S(2)}) collective-permute-start(bf16[8,80,128]{2,1,0:T(8,128)(2,1)S(1)} %get-tuple-element.47), channel_id=1, source_target_pairs={{0,2},{1,3},{2,4},{3,5},{4,6},{5,7},{6,0},{7,1},{8,10},{9,11},{10,... | collective-permute-start | bytes 491528 | tf_op jit(solution)/shard_map/ppermute | solution.py:276
  68.4 9.4 %collective-permute-start.12 = (bf16[8,80,128]{2,1,0:T(8,128)(2,1)S(1)}, bf16[8,80,128]{2,1,0:T(8,128)(2,1)S(1)}, u32[]{:S(2)}, u32[]{:S(2)}) collective-permute-start(bf16[8,80,128]{2,1,0:T(8,128)(2,1)S(1)} %get-tuple-element.48), channel_id=1, source_target_pairs={{0,4},{1,5},{2,6},{3,7},{4,0},{5,1},{6,2},{7,3},{8,12},{9,13},{10,... | collective-permute-start | bytes 491528 | tf_op jit(solution)/shard_map/ppermute | solution.py:276
  70.4 8.0 %collective-permute-start.13 = (bf16[8,80,128]{2,1,0:T(8,128)(2,1)S(1)}, bf16[8,80,128]{2,1,0:T(8,128)(2,1)S(1)}, u32[]{:S(2)}, u32[]{:S(2)}) collective-permute-start(bf16[8,80,128]{2,1,0:T(8,128)(2,1)S(1)} %get-tuple-element.49), channel_id=1, source_target_pairs={{0,6},{1,7},{2,0},{3,1},{4,2},{5,3},{6,4},{7,5},{8,14},{9,15},{10,... | collective-permute-start | bytes 491528 | tf_op jit(solution)/shard_map/ppermute | solution.py:276
  84.5 20.2 %all-to-all-start.3 = ((bf16[8,272,128]{2,1,0:T(8,128)(2,1)}), bf16[8,272,128]{2,1,0:T(8,128)(2,1)S(1)}, u32[]{:S(2)}, u32[]{:S(2)}) async-start(bf16[8,272,128]{2,1,0:T(8,128)(2,1)} %combine.1), calls=%async_computation.3 | async-start | bytes 1114112 | tf_op jit(solution)/shard_map/all_to_all | solution.py:296
  89.4 12.0 %collective-permute-start.15 = (bf16[8,128,256]{2,1,0:T(8,128)(2,1)S(1)}, bf16[8,128,256]{2,1,0:T(8,128)(2,1)S(1)}, u32[]{:S(2)}, u32[]{:S(2)}) collective-permute-start(bf16[8,128,256]{2,1,0:T(8,128)(2,1)S(1)} %all-to-all-done.2.refs_0_), channel_id=1, source_target_pairs={{0,192},{64,0},{128,64},{192,128},{1,193},{65,1},{129,65},{193,129... | collective-permute-start | bytes 1572872 | tf_op jit(solution)/shard_map/ppermute | solution.py:186
  91.5 12.6 %collective-permute-start.14 = (bf16[8,128,256]{2,1,0:T(8,128)(2,1)S(1)}, bf16[8,128,256]{2,1,0:T(8,128)(2,1)S(1)}, u32[]{:S(2)}, u32[]{:S(2)}) collective-permute-start(bf16[8,128,256]{2,1,0:T(8,128)(2,1)S(1)} %all-to-all-done.2.refs_0_), channel_id=1, source_target_pairs={{0,64},{64,128},{128,192},{192,0},{1,65},{65,129},{129,193},{193,1... | collective-permute-start | bytes 1572872 | tf_op jit(solution)/shard_map/ppermute | solution.py:186
  101.4 6.6 %collective-permute-start.17 = (bf16[4,128,256]{2,1,0:T(8,128)(2,1)S(1)}, bf16[4,128,256]{2,1,0:T(8,128)(2,1)S(1)}, u32[]{:S(2)}, u32[]{:S(2)}) collective-permute-start(bf16[4,128,256]{2,1,0:T(8,128)(2,1)S(1)} %slice.9), channel_id=1, source_target_pairs={{0,192},{64,0},{128,64},{192,128},{1,193},{65,1},{129,65},{193,129... | collective-permute-start | bytes 786440 | tf_op jit(solution)/shard_map/ppermute | solution.py:186
  104.1 7.7 %collective-permute-start.16 = (bf16[4,128,256]{2,1,0:T(8,128)(2,1)S(1)}, bf16[4,128,256]{2,1,0:T(8,128)(2,1)S(1)}, u32[]{:S(2)}, u32[]{:S(2)}) collective-permute-start(bf16[4,128,256]{2,1,0:T(8,128)(2,1)S(1)} %slice.8), channel_id=1, source_target_pairs={{0,64},{64,128},{128,192},{192,0},{1,65},{65,129},{129,193},{193,1... | collective-permute-start | bytes 786440 | tf_op jit(solution)/shard_map/ppermute | solution.py:186

commit v5 on v4

--- a/solution.py
+++ b/solution.py
@@ -17,7 +17,7 @@
 TILE = 256
 BF = jnp.bfloat16
 F32 = jnp.float32
-VMEM = pl.BlockSpec(memory_space=pltpu.VMEM)
+ANY = pl.BlockSpec(memory_space=pl.ANY)
 
 ROW_DO = NOPE
 ROW_ROPE = ROW_DO + VDIM
@@ -60,6 +60,8 @@
     seq = lat_s.shape[0]
     scale = WIDTH ** (-0.5)
     per_half = HALF // SUB
+    n_x = n_head // 2
+    x, core = lax.div(rank_ref[1], 2), lax.rem(rank_ref[1], 2)
 
     def place(block):
         return pl.multiple_of(order_ref[block] * HALF, HALF)
@@ -72,7 +74,8 @@
             q_s[rows, NOPE:] = in_ref[s, ROW_ROPE:ROWS_IN, half * ROPE : (half + 1) * ROPE]
             d_s[rows, :] = in_ref[s, ROW_DO + lo : ROW_DO + lo + HALF, :]
     for shift in range(n_head):
-        p = lax.rem(rank_ref[1] + n_head - shift, n_head)
+        other, back = divmod(shift, n_x)
+        p = lax.rem(x + n_x - back, n_x) * 2 + lax.rem(core + other, 2)
         half, i = lax.div(p, per_half), lax.rem(p, per_half)
         for s in range(blocks):
             sub = pl.ds(pl.multiple_of(order_ref[2 * s + half] * HALF + i * SUB, SUB), SUB)
@@ -126,8 +129,6 @@
             lo = half * HALF
             gq_ref[s, lo : lo + HALF, :] = dq_s[rows, :NOPE]
             gq_ref[s, ROW_GROPE:ROW_GL, half * ROPE : (half + 1) * ROPE] = dq_s[rows, NOPE:]
-    n_x = n_head // 2
-    x, core = lax.div(rank_ref[1], 2), lax.rem(rank_ref[1], 2)
     for flip in range(2):
         for shift in range(n_x):
             p = lax.rem(x + shift, n_x) * 2 + lax.rem(core + flip, 2)
@@ -168,18 +169,44 @@
     gl_ref[:, LAT:] = jnp.sum(part, axis=0)
 
 
-def assemble_kernel(n_dp, rank_ref, *refs):
-    in_refs, (gk_ref, gv_ref) = refs[:-2], refs[-2:]
+def assemble_kernel(steps, n_dp, rank_ref, *refs):
+    n_in = sum(len(group) for group in steps.values())
+    in_refs = list(refs[:n_in])
+    gk_ref, gv_ref, gk_s, gv_s, sems = refs[-5:]
     share = in_refs[0].shape[1]
-    half = in_refs[3].shape[0]
-    for in_ref, step, first in zip(in_refs, (0, 3, 1, 2, 2), (0, 0, 0, 0, half)):
-        source = lax.rem(rank_ref[2] + step, n_dp)
+    copies = []
+    for k, (step, group) in enumerate(steps.items()):
+        h = 0
+        for in_ref in [in_refs[i] for i in group]:
+            for i in range(in_ref.shape[0]):
+                part = in_ref[i].astype(F32)
+                gk_s[k, :, h * NOPE : (h + 1) * NOPE] = part[:, :NOPE]
+                gv_s[k, :, h * VDIM : (h + 1) * VDIM] = part[:, NOPE:]
+                h += 1
+        source = lax.rem(rank_ref[2] + n_dp - step, n_dp)
         rows = pl.ds(pl.multiple_of(source * share, share), share)
-        for i in range(in_ref.shape[0]):
-            h = first + i
-            part = in_ref[i].astype(F32)
-            gk_ref[rows, h * NOPE : (h + 1) * NOPE] = part[:, :NOPE]
-            gv_ref[rows, h * VDIM : (h + 1) * VDIM] = part[:, NOPE:]
+        copies.append(pltpu.make_async_copy(gk_s.at[k], gk_ref.at[rows], sems.at[k, 0]))
+        copies.append(pltpu.make_async_copy(gv_s.at[k], gv_ref.at[rows], sems.at[k, 1]))
+        copies[-2].start()
+        copies[-1].start()
+    for copy in copies:
+        copy.wait()
+
+
+def assemble(name, steps, n_dp, ranks, parts, outs, filled=()):
+    n, rows = len(steps), parts[0].shape[1]
+    return call(
+        functools.partial(assemble_kernel, steps, n_dp),
+        name,
+        (ranks,),
+        (*parts, *filled),
+        outs,
+        scratch=[pltpu.VMEM((n, rows, outs[i].shape[1]), F32) for i in range(2)]
+        + [pltpu.SemaphoreType.DMA((n, 2))],
+        in_specs=[whole(part.shape) for part in parts] + [ANY] * len(filled),
+        out_specs=[ANY, ANY],
+        aliases={1 + len(parts) + i: i for i in range(len(filled))},
+    )
 
 
 def shifted(x, axis, n, shift):
@@ -190,7 +217,10 @@
     return pl.BlockSpec(shape, lambda i, *scalars: (0,) * len(shape))
 
 
-def call(kernel, name, scalars, inputs, outs, scratch=(), in_specs=None, flops=0, vmem=16):
+def call(
+    kernel, name, scalars, inputs, outs, scratch=(), in_specs=None, flops=0, vmem=16,
+    out_specs=None, aliases=None,
+):
     moved = sum(x.size * x.dtype.itemsize for x in inputs) + sum(
         x.size * x.dtype.itemsize for x in outs
     )
@@ -200,10 +230,11 @@
             num_scalar_prefetch=len(scalars),
             grid=(1,),
             in_specs=in_specs or [whole(x.shape) for x in inputs],
-            out_specs=[whole(x.shape) for x in outs],
+            out_specs=out_specs or [whole(x.shape) for x in outs],
             scratch_shapes=list(scratch),
         ),
         out_shape=list(outs),
+        input_output_aliases=aliases or {},
         compiler_params=pltpu.CompilerParams(vmem_limit_bytes=vmem * 1024 * 1024),
         cost_estimate=pl.CostEstimate(flops=flops, bytes_accessed=moved, transcendentals=0),
         name=name,
@@ -219,7 +250,9 @@
     lat_mine = lax.all_to_all(
         jnp.broadcast_to(latent, (n_ctx, SUB, LAT + ROPE)), "ctx", 0, 0, tiled=True
     )
-    lat_all = [lat_mine] + [shifted(lat_mine, "head", n_head, i) for i in range(1, n_head)]
+    flip = [(i, i ^ 1) for i in range(n_head)]
+    lat_all = [lat_mine] + [shifted(lat_mine, "head", n_head, 2 * i) for i in range(1, n_head // 2)]
+    lat_all += [lax.ppermute(part, "head", flip) for part in lat_all]
     head_cols = pl.BlockSpec((LAT, NOPE), lambda i, rank: (0, rank[0]))
     packed, w_both = call(
         pack_kernel,
@@ -259,7 +292,6 @@
     for i in range(1, n_dp):
         gw_sum = gw_sum + shifted(gw_parts[i], "dp", n_dp, i).astype(F32)
     gw_sum = gw_sum.astype(BF)
-    flip = [(i, i ^ 1) for i in range(n_head)]
     gl_recv = lax.ppermute(gl_send, "head", flip)
     gw_sum, gl_recv = lax.optimization_barrier((gw_sum, gl_recv))
     folded = call(
@@ -279,10 +311,7 @@
     gw_ctx, *gl_moved = lax.optimization_barrier((gw_ctx, *gl_moved))
     half = n_ctx // 2
     before, after = shifted(gw_ctx, "dp", n_dp, 1), shifted(gw_ctx, "dp", n_dp, n_dp - 1)
-    gw_all = [
-        gw_ctx,
-        before,
-        after,
+    opposite = [
         shifted(before[:half], "dp", n_dp, 1),
         shifted(after[half:], "dp", n_dp, n_dp - 1),
     ]
@@ -301,13 +330,15 @@
         (back,),
         [shape((rows, n_ctx * WIDTH), BF), shape((SUB, LAT + ROPE), F32)],
     )
-    grad_query, grad_latent, *gw_all = lax.optimization_barrier((grad_query, grad_latent, *gw_all))
-    grad_w_uk, grad_w_uv = call(
-        functools.partial(assemble_kernel, n_dp),
-        "assemble",
-        (ranks,),
-        gw_all,
-        [shape((LAT, n_ctx * NOPE), F32), shape((LAT, n_ctx * VDIM), F32)],
+    outs = [shape((LAT, n_ctx * NOPE), F32), shape((LAT, n_ctx * VDIM), F32)]
+    filled = assemble(
+        "assemble_near", {0: [0], 1: [1], 3: [2]}, n_dp, ranks, [gw_ctx, before, after], outs
+    )
+    grad_query, grad_latent, *opposite = lax.optimization_barrier(
+        (grad_query, grad_latent, *opposite)
+    )
+    grad_w_uk, grad_w_uv = assemble(
+        "assemble_far", {2: [0, 1]}, n_dp, ranks, opposite, outs, filled
     )
     return (grad_query[None], grad_latent[None], grad_w_uk, grad_w_uv)
 

time: 115 us -> 109 us (0.948)
  waiting for transfers between devices: 48.5 us -> 43.3 us
  starting transfers between devices: 46.6 us -> 44.3 us
    ppermute x14 -> x10, waiting for transfers between devices: 34.1 us -> 25.3 us  [shifted(): return lax.ppermute(x, axis, [(i, (i + shift) % n) for i in range(n)])]
    all_to_all x1, waiting for transfers between devices: 0.01 us -> 4.58 us  [on_device(): mine = lax.all_to_all(packed, 'ctx', 0, 0, tiled=True)]
    all_to_all x1, starting transfers between devices: 7.21 us -> 4.85 us  [on_device(): lax.all_to_all(jnp.broadcast_to(gw_sum[None], (n_ctx,) + gw_sum.shape), '...]
    ppermute x3, starting transfers between devices: 3.5 us -> 5.73 us  [on_device(): lax.ppermute(folded[i], 'head', [(j, (j + 2 * i) % n_head) for j in range...]
    ppermute x14 -> x10, starting transfers between devices: 17.3 us -> 15.1 us  [shifted(): return lax.ppermute(x, axis, [(i, (i + shift) % n) for i in range(n)])]
    ppermute x3, waiting for transfers between devices: 6.65 us -> 5.07 us  [on_device(): lax.ppermute(folded[i], 'head', [(j, (j + 2 * i) % n_head) for j in range...]
    ppermute x0 -> x4, waiting for transfers between devices: none -> 1.38 us  [on_device(): lat_all += [lax.ppermute(part, 'head', flip) for part in lat_all]]
    pallas_call x6 -> x7, Pallas kernels: 12.2 us -> 13.2 us  [call(): pl.pallas_call(kernel, grid_spec=pltpu.PrefetchScalarGridSpec(num_scalar_...]
  transfers between devices with their start and end apart: 22 -> 22, of which waited for: 16 -> 14; matrix products, arithmetic and copies ran while one was open for 0% -> 0% of each run, Pallas kernels for 2% -> 5%
where the time goes in v5:
time: 109 us; the launch traced here: 108 us
  starting transfers between devices  44.3 us (41%)
  waiting for transfers between devices  43.3 us (40%)
  Pallas kernels  13.2 us (12%)
  local copies, waits for them, and re-layouts  6.67 us (6%)
    ppermute x10, waiting for transfers between devices, shifted(): return lax.ppermute(x, axis, [(i, (i + shift) % n) for i in range(n)])  25.3 us
    ppermute x10, starting transfers between devices, shifted(): return lax.ppermute(x, axis, [(i, (i + shift) % n) for i in range(n)])  15.1 us
    pallas_call x7, Pallas kernels, call(): pl.pallas_call(kernel, grid_spec=pltpu.PrefetchScalarGridSpec(num_scalar_...  13.2 us
    all_to_all x1, starting transfers between devices, on_device(): lax.all_to_all(jnp.broadcast_to(latent, (n_ctx, SUB, LAT + ROPE)), 'ctx',...  8.57 us
    ppermute x3, starting transfers between devices, on_device(): lax.ppermute(folded[i], 'head', [(j, (j + 2 * i) % n_head) for j in range...  5.73 us
    ppermute x3, waiting for transfers between devices, on_device(): lax.ppermute(folded[i], 'head', [(j, (j + 2 * i) % n_head) for j in range...  5.07 us
    all_to_all x1, starting transfers between devices, on_device(): mine = lax.all_to_all(packed, 'ctx', 0, 0, tiled=True)  5.01 us
    all_to_all x1, starting transfers between devices, on_device(): back = lax.all_to_all(back, 'ctx', 0, 0, tiled=True)  4.89 us
  transfers between devices with their start and end apart: 22, of which 14 were waited for; matrix products, arithmetic and copies ran while one was open for 0% of the time, Pallas kernels for 5%

profile of v5, /device:TPU:32, one launch (start us, length us, event | category | flops | bytes accessed | tf_op | source)
XLA Modules:
  0.0 108.4 jit_solution(15972344407412717111)
XLA Ops:
  0.6 1.4 %broadcast_in_dim.20 = bf16[8,16,576]{2,1,0:T(8,128)(2,1)} broadcast(bf16[16,576]{1,0:T(8,128)(2,1)} %bitcast.10), dimensions={1,2} | broadcast | bytes 165888 | tf_op jit(solution)/shard_map/broadcast_in_dim | solution.py:251
  2.0 8.6 %all-to-all-start.1 = ((bf16[8,16,576]{2,1,0:T(8,128)(2,1)}), bf16[8,16,576]{2,1,0:T(8,128)(2,1)S(1)}, u32[]{:S(2)}, u32[]{:S(2)}) async-start(bf16[8,16,576]{2,1,0:T(8,128)(2,1)} %broadcast_in_dim.20), calls=%async_computation.1 | async-start | bytes 327680 | tf_op jit(solution)/shard_map/all_to_all | solution.py:250
  10.7 1.2 %copy-done = bf16[512,1024]{1,0:T(8,128)(2,1)S(1)} copy-done((bf16[512,1024]{1,0:T(8,128)(2,1)S(1)}, bf16[512,1024]{1,0:T(8,128)(2,1)}, u32[]{:S(2)}) %copy-start) | copy-done | bytes 1048600
  11.9 1.2 %copy-done.1 = bf16[512,1024]{1,0:T(8,128)(2,1)S(1)} copy-done((bf16[512,1024]{1,0:T(8,128)(2,1)S(1)}, bf16[512,1024]{1,0:T(8,128)(2,1)}, u32[]{:S(2)}) %copy-start.1) | copy-done | bytes 1048600
  15.1 1.6 %pack.1 = (bf16[8,320,128]{2,1,0:T(8,128)(2,1)}, bf16[512,256]{1,0:T(8,128)(2,1)S(1)}) custom-call(s32[3]{0:T(128)S(1)} %pad_add_fusion.rank_ref, bf16[128,1536]{1,0:T(8,128)(2,1)S(1)} %bitcast.8, bf16[128,1024]{1,0:T(8,128)(2,1)S(1)} %bitcast.9, bf16[512,1024]{1,0:T(8,128)(2,1)S(1)} %copy-done, bf16[512,1024]{1,0:T(8,128)(2,1)S(1)} %copy-done.1), custom_call_target="tpu_custom_call" | custom-call | bytes 3670016 | tf_op jit(solution)/shard_map/pack/pallas_call | solution.py:227
  16.7 2.2 %all-to-all-done.1.refs_0_ = bf16[8,16,576]{2,1,0:T(8,128)(2,1)S(1)} async-done(((bf16[8,16,576]{2,1,0:T(8,128)(2,1)}), bf16[8,16,576]{2,1,0:T(8,128)(2,1)S(1)}, u32[]{:S(2)}, u32[]{:S(2)}) %all-to-all-start.1) | async-done | bytes 147488 | tf_op jit(solution)/shard_map/all_to_all | solution.py:250
  18.9 5.0 %all-to-all-start = ((bf16[8,320,128]{2,1,0:T(8,128)(2,1)}), bf16[8,320,128]{2,1,0:T(8,128)(2,1)S(1)}, u32[]{:S(2)}, u32[]{:S(2)}) async-start(bf16[8,320,128]{2,1,0:T(8,128)(2,1)} %get-tuple-element.34), calls=%async_computation | async-start | bytes 1310720 | tf_op jit(solution)/shard_map/all_to_all | solution.py:265
  23.9 2.8 %collective-permute-start.2 = (bf16[8,16,576]{2,1,0:T(8,128)(2,1)S(1)}, bf16[8,16,576]{2,1,0:T(8,128)(2,1)S(1)}, u32[]{:S(2)}, u32[]{:S(2)}) collective-permute-start(bf16[8,16,576]{2,1,0:T(8,128)(2,1)S(1)} %all-to-all-done.1.refs_0_), channel_id=1, source_target_pairs={{0,6},{1,7},{2,0},{3,1},{4,2},{5,3},{6,4},{7,5},{8,14},{9,15},{10,... | collective-permute-start | bytes 442376 | tf_op jit(solution)/shard_map/ppermute | solution.py:213
  28.4 4.2 %collective-permute-done.2.refs_3_ = bf16[8,16,576]{2,1,0:T(8,128)(2,1)S(1)} collective-permute-done((bf16[8,16,576]{2,1,0:T(8,128)(2,1)S(1)}, bf16[8,16,576]{2,1,0:T(8,128)(2,1)S(1)}, u32[]{:S(2)}, u32[]{:S(2)}) %collective-permute-start.2) | collective-permute-done | bytes 147488 | tf_op jit(solution)/shard_map/ppermute | solution.py:213
  32.6 2.0 %collective-permute-done.1.refs_2_ = bf16[8,16,576]{2,1,0:T(8,128)(2,1)S(1)} collective-permute-done((bf16[8,16,576]{2,1,0:T(8,128)(2,1)S(1)}, bf16[8,16,576]{2,1,0:T(8,128)(2,1)S(1)}, u32[]{:S(2)}, u32[]{:S(2)}) %collective-permute-start.1) | collective-permute-done | bytes 147488 | tf_op jit(solution)/shard_map/ppermute | solution.py:213
  34.6 1.7 %collective-permute-done.refs_1_ = bf16[8,16,576]{2,1,0:T(8,128)(2,1)S(1)} collective-permute-done((bf16[8,16,576]{2,1,0:T(8,128)(2,1)S(1)}, bf16[8,16,576]{2,1,0:T(8,128)(2,1)S(1)}, u32[]{:S(2)}, u32[]{:S(2)}) %collective-permute-start) | collective-permute-done | bytes 147488 | tf_op jit(solution)/shard_map/ppermute | solution.py:213
  36.3 1.4 %collective-permute-done.4.refs_5_ = bf16[8,16,576]{2,1,0:T(8,128)(2,1)S(1)} collective-permute-done((bf16[8,16,576]{2,1,0:T(8,128)(2,1)S(1)}, bf16[8,16,576]{2,1,0:T(8,128)(2,1)S(1)}, u32[]{:S(2)}, u32[]{:S(2)}) %collective-permute-start.4) | collective-permute-done | bytes 147488 | tf_op jit(solution)/shard_map/ppermute | solution.py:255
  37.6 4.6 %all-to-all-done.in_ref = bf16[8,320,128]{2,1,0:T(8,128)(2,1)S(1)} async-done(((bf16[8,320,128]{2,1,0:T(8,128)(2,1)}), bf16[8,320,128]{2,1,0:T(8,128)(2,1)S(1)}, u32[]{:S(2)}, u32[]{:S(2)}) %all-to-all-start) | async-done | bytes 655392 | tf_op jit(solution)/shard_map/all_to_all | solution.py:265
  42.2 5.6 %attention_backward.1 = (bf16[4,8,80,128]{3,2,1,0:T(8,128)(2,1)S(1)}, bf16[4,8,80,128]{3,2,1,0:T(8,128)(2,1)S(1)}, bf16[128,256]{1,0:T(8,128)(2,1)S(1)}, bf16[12...) custom-call(s32[16]{0:T(128)S(1)} %copy-done.4, ...), custom_call_target="tpu_custom_call" | custom-call | flops 3000000000 | bytes 4063232 | tf_op jit(solution)/shard_map/attention_backward/pallas_call | solution.py:227
  47.9 1.7 %collective-permute-start.7 = (bf16[128,256]{1,0:T(8,128)(2,1)S(1)}, bf16[128,256]{1,0:T(8,128)(2,1)S(1)}, u32[]{:S(2)}, u32[]{:S(2)}) collective-permute-start(bf16[128,256]{1,0:T(8,128)(2,1)S(1)} %get-tuple-element.38), channel_id=1, source_target_pairs={{0,64},{64,128},{128,192},{192,0},{1,65},{65,129},{129,193},{193,1... | collective-permute-start | bytes 196616 | tf_op jit(solution)/shard_map/ppermute | solution.py:213
  49.6 2.9 %collective-permute-start.8 = (bf16[128,256]{1,0:T(8,128)(2,1)S(1)}, bf16[128,256]{1,0:T(8,128)(2,1)S(1)}, u32[]{:S(2)}, u32[]{:S(2)}) collective-permute-start(bf16[128,256]{1,0:T(8,128)(2,1)S(1)} %get-tuple-element.39), channel_id=1, source_target_pairs={{0,128},{64,192},{128,0},{192,64},{1,129},{65,193},{129,1},{193,65... | collective-permute-start | bytes 196616 | tf_op jit(solution)/shard_map/ppermute | solution.py:213
  52.5 1.3 %collective-permute-start.9 = (bf16[128,256]{1,0:T(8,128)(2,1)S(1)}, bf16[128,256]{1,0:T(8,128)(2,1)S(1)}, u32[]{:S(2)}, u32[]{:S(2)}) collective-permute-start(bf16[128,256]{1,0:T(8,128)(2,1)S(1)} %get-tuple-element.40), channel_id=1, source_target_pairs={{0,192},{64,0},{128,64},{192,128},{1,193},{65,1},{129,65},{193,129... | collective-permute-start | bytes 196616 | tf_op jit(solution)/shard_map/ppermute | solution.py:213
  53.8 2.5 %collective-permute-done.8 = bf16[128,256]{1,0:T(8,128)(2,1)S(1)} collective-permute-done((bf16[128,256]{1,0:T(8,128)(2,1)S(1)}, bf16[128,256]{1,0:T(8,128)(2,1)S(1)}, u32[]{:S(2)}, u32[]{:S(2)}) %collective-permute-start.8) | collective-permute-done | bytes 65568 | tf_op jit(solution)/shard_map/ppermute | solution.py:213
  57.6 4.9 %all-to-all-start.2 = ((bf16[8,128,256]{2,1,0:T(8,128)(2,1)}), bf16[8,128,256]{2,1,0:T(8,128)(2,1)S(1)}, u32[]{:S(2)}, u32[]{:S(2)}) async-start(bf16[8,128,256]{2,1,0:T(8,128)(2,1)} %broadcast_in_dim.21), calls=%async_computation.2 | async-start | bytes 1048576 | tf_op jit(solution)/shard_map/all_to_all | solution.py:304
  62.6 1.6 %collective-permute-start.11 = (bf16[8,80,128]{2,1,0:T(8,128)(2,1)S(1)}, bf16[8,80,128]{2,1,0:T(8,128)(2,1)S(1)}, u32[]{:S(2)}, u32[]{:S(2)}) collective-permute-start(bf16[8,80,128]{2,1,0:T(8,128)(2,1)S(1)} %get-tuple-element.46), channel_id=1, source_target_pairs={{0,2},{1,3},{2,4},{3,5},{4,6},{5,7},{6,0},{7,1},{8,10},{9,11},{10,... | collective-permute-start | bytes 491528 | tf_op jit(solution)/shard_map/ppermute | solution.py:308
  64.2 2.7 %collective-permute-start.12 = (bf16[8,80,128]{2,1,0:T(8,128)(2,1)S(1)}, bf16[8,80,128]{2,1,0:T(8,128)(2,1)S(1)}, u32[]{:S(2)}, u32[]{:S(2)}) collective-permute-start(bf16[8,80,128]{2,1,0:T(8,128)(2,1)S(1)} %get-tuple-element.47), channel_id=1, source_target_pairs={{0,4},{1,5},{2,6},{3,7},{4,0},{5,1},{6,2},{7,3},{8,12},{9,13},{10,... | collective-permute-start | bytes 491528 | tf_op jit(solution)/shard_map/ppermute | solution.py:308
  66.9 1.4 %collective-permute-start.13 = (bf16[8,80,128]{2,1,0:T(8,128)(2,1)S(1)}, bf16[8,80,128]{2,1,0:T(8,128)(2,1)S(1)}, u32[]{:S(2)}, u32[]{:S(2)}) collective-permute-start(bf16[8,80,128]{2,1,0:T(8,128)(2,1)S(1)} %get-tuple-element.48), channel_id=1, source_target_pairs={{0,6},{1,7},{2,0},{3,1},{4,2},{5,3},{6,4},{7,5},{8,14},{9,15},{10,... | collective-permute-start | bytes 491528 | tf_op jit(solution)/shard_map/ppermute | solution.py:308
  68.4 2.3 %collective-permute-done.11.refs_1_ = bf16[8,80,128]{2,1,0:T(8,128)(2,1)S(1)} collective-permute-done((bf16[8,80,128]{2,1,0:T(8,128)(2,1)S(1)}, bf16[8,80,128]{2,1,0:T(8,128)(2,1)S(1)}, u32[]{:S(2)}, u32[]{:S(2)}) %collective-permute-start.11) | collective-permute-done | bytes 163872 | tf_op jit(solution)/shard_map/ppermute | solution.py:308
  70.7 2.8 %collective-permute-done.12.refs_2_ = bf16[8,80,128]{2,1,0:T(8,128)(2,1)S(1)} collective-permute-done((bf16[8,80,128]{2,1,0:T(8,128)(2,1)S(1)}, bf16[8,80,128]{2,1,0:T(8,128)(2,1)S(1)}, u32[]{:S(2)}, u32[]{:S(2)}) %collective-permute-start.12) | collective-permute-done | bytes 163872 | tf_op jit(solution)/shard_map/ppermute | solution.py:308
  73.4 4.7 %all-to-all-done.2.refs_0_ = bf16[8,128,256]{2,1,0:T(8,128)(2,1)S(1)} async-done(((bf16[8,128,256]{2,1,0:T(8,128)(2,1)}), bf16[8,128,256]{2,1,0:T(8,128)(2,1)S(1)}, u32[]{:S(2)}, u32[]{:S(2)}) %all-to-all-start.2) | async-done | bytes 524320 | tf_op jit(solution)/shard_map/all_to_all | solution.py:304
  79.1 4.9 %all-to-all-start.3 = ((bf16[8,272,128]{2,1,0:T(8,128)(2,1)}), bf16[8,272,128]{2,1,0:T(8,128)(2,1)S(1)}, u32[]{:S(2)}, u32[]{:S(2)}) async-start(bf16[8,272,128]{2,1,0:T(8,128)(2,1)} %combine.1), calls=%async_computation.3 | async-start | bytes 1114112 | tf_op jit(solution)/shard_map/all_to_all | solution.py:325
  84.0 2.1 %collective-permute-start.16 = (bf16[8,128,256]{2,1,0:T(8,128)(2,1)S(1)}, bf16[8,128,256]{2,1,0:T(8,128)(2,1)S(1)}, u32[]{:S(2)}, u32[]{:S(2)}) collective-permute-start(bf16[8,128,256]{2,1,0:T(8,128)(2,1)S(1)} %all-to-all-done.2.refs_0_), channel_id=1, source_target_pairs={{0,192},{64,0},{128,64},{192,128},{1,193},{65,1},{129,65},{193,129... | collective-permute-start | bytes 1572872 | tf_op jit(solution)/shard_map/ppermute | solution.py:213
  86.1 10.2 %collective-permute-done.16.refs_2_ = bf16[8,128,256]{2,1,0:T(8,128)(2,1)S(1)} collective-permute-done((bf16[8,128,256]{2,1,0:T(8,128)(2,1)S(1)}, bf16[8,128,256]{2,1,0:T(8,128)(2,1)S(1)}, u32[]{:S(2)}, u32[]{:S(2)}) %collective-permute-start.16) | collective-permute-done | bytes 524320 | tf_op jit(solution)/shard_map/ppermute | solution.py:213
  96.3 2.6 %collective-permute-start.17 = (bf16[4,128,256]{2,1,0:T(8,128)(2,1)S(1)}, bf16[4,128,256]{2,1,0:T(8,128)(2,1)S(1)}, u32[]{:S(2)}, u32[]{:S(2)}) collective-permute-start(bf16[4,128,256]{2,1,0:T(8,128)(2,1)S(1)} %slice.9), channel_id=1, source_target_pairs={{0,192},{64,0},{128,64},{192,128},{1,193},{65,1},{129,65},{193,129... | collective-permute-start | bytes 786440 | tf_op jit(solution)/shard_map/ppermute | solution.py:213
  99.1 2.3 %assemble_near.1 = (f32[512,1024]{1,0:T(8,128)}, f32[512,1024]{1,0:T(8,128)}) custom-call(s32[3]{0:T(128)S(1)} %pad_add_fusion.rank_ref, bf16[8,128,256]{2,1,0:T(8,128)(2,1)S(1)} %all-to-all-done.2.refs_0_, bf16[8,128,256]{2,1,0:T(8,128)(2,1)S(1)} %collective-permute-done.14.refs_1_, bf16[8,128,256]{2,1,0:T(8,128)(2,1)S(1)} %collective-permute-done.16.refs_2_), custom_call_target="tpu_custom_call" | custom-call | bytes 5767168 | tf_op jit(solution)/shard_map/assemble_near/pallas_call | solution.py:227
  102.8 3.8 %collective-permute-done.15.refs_0_ = bf16[4,128,256]{2,1,0:T(8,128)(2,1)S(1)} collective-permute-done((bf16[4,128,256]{2,1,0:T(8,128)(2,1)S(1)}, bf16[4,128,256]{2,1,0:T(8,128)(2,1)S(1)}, u32[]{:S(2)}, u32[]{:S(2)}) %collective-permute-start.15) | collective-permute-done | bytes 262176 | tf_op jit(solution)/shard_map/ppermute | solution.py:213
  106.6 1.6 %assemble_far.1 = (f32[512,1024]{1,0:T(8,128)}, f32[512,1024]{1,0:T(8,128)}) custom-call(s32[3]{0:T(128)S(1)} %pad_add_fusion.rank_ref, bf16[4,128,256]{2,1,0:T(8,128)(2,1)S(1)} %collective-permute-done.15.refs_0_, bf16[4,128,256]{2,1,0:T(8,128)(2,1)S(1)} %collective-permute-done.17.refs_1_, ...), custom_call_target="tpu_custom_call", output_to_operand_aliasing={{0}: (3, {}), {1}: (4, {})} | custom-call | bytes 8912896 | tf_op jit(solution)/shard_map/assemble_far/pallas_call | solution.py:227
  (35 shorter events, 7.8 us)
Async XLA Ops:
  2.0 16.9 %all-to-all-start.1 = ((bf16[8,16,576]{2,1,0:T(8,128)(2,1)}), bf16[8,16,576]{2,1,0:T(8,128)(2,1)S(1)}, u32[]{:S(2)}, u32[]{:S(2)}) async-start(bf16[8,16,576]{2,1,0:T(8,128)(2,1)} %broadcast_in_dim.20), calls=%async_computation.1 | async-start | bytes 327680 | tf_op jit(solution)/shard_map/all_to_all | solution.py:250
  10.6 31.6 %copy-start.4 = (s32[16]{0:T(128)S(1)}, s32[16]{0:T(128)}, u32[]{:S(2)}) copy-start(s32[16]{0:T(128)} %order_ref.1) | copy-start | bytes 196
  10.7 1.2 %copy-start = (bf16[512,1024]{1,0:T(8,128)(2,1)S(1)}, bf16[512,1024]{1,0:T(8,128)(2,1)}, u32[]{:S(2)}) copy-start(bf16[512,1024]{1,0:T(8,128)(2,1)} %wk_ref.1) | copy-start | bytes 3145732
  11.9 1.2 %copy-start.1 = (bf16[512,1024]{1,0:T(8,128)(2,1)S(1)}, bf16[512,1024]{1,0:T(8,128)(2,1)}, u32[]{:S(2)}) copy-start(bf16[512,1024]{1,0:T(8,128)(2,1)} %wv_ref.1) | copy-start | bytes 3145732
  13.1 1.0 copy-start.2
  14.1 0.9 copy-start.3
  18.9 23.3 %all-to-all-start = ((bf16[8,320,128]{2,1,0:T(8,128)(2,1)}), bf16[8,320,128]{2,1,0:T(8,128)(2,1)S(1)}, u32[]{:S(2)}, u32[]{:S(2)}) async-start(bf16[8,320,128]{2,1,0:T(8,128)(2,1)} %get-tuple-element.34), calls=%async_computation | async-start | bytes 1310720 | tf_op jit(solution)/shard_map/all_to_all | solution.py:265
  23.9 8.6 %collective-permute-start.2 = (bf16[8,16,576]{2,1,0:T(8,128)(2,1)S(1)}, bf16[8,16,576]{2,1,0:T(8,128)(2,1)S(1)}, u32[]{:S(2)}, u32[]{:S(2)}) collective-permute-start(bf16[8,16,576]{2,1,0:T(8,128)(2,1)S(1)} %all-to-all-done.1.refs_0_), channel_id=1, source_target_pairs={{0,6},{1,7},{2,0},{3,1},{4,2},{5,3},{6,4},{7,5},{8,14},{9,15},{10,... | collective-permute-start | bytes 442376 | tf_op jit(solution)/shard_map/ppermute | solution.py:213
  26.7 7.9 %collective-permute-start.1 = (bf16[8,16,576]{2,1,0:T(8,128)(2,1)S(1)}, bf16[8,16,576]{2,1,0:T(8,128)(2,1)S(1)}, u32[]{:S(2)}, u32[]{:S(2)}) collective-permute-start(bf16[8,16,576]{2,1,0:T(8,128)(2,1)S(1)} %all-to-all-done.1.refs_0_), channel_id=1, source_target_pairs={{0,4},{1,5},{2,6},{3,7},{4,0},{5,1},{6,2},{7,3},{8,12},{9,13},{10,... | collective-permute-start | bytes 442376 | tf_op jit(solution)/shard_map/ppermute | solution.py:213
  27.5 8.8 %collective-permute-start = (bf16[8,16,576]{2,1,0:T(8,128)(2,1)S(1)}, bf16[8,16,576]{2,1,0:T(8,128)(2,1)S(1)}, u32[]{:S(2)}, u32[]{:S(2)}) collective-permute-start(bf16[8,16,576]{2,1,0:T(8,128)(2,1)S(1)} %all-to-all-done.1.refs_0_), channel_id=1, source_target_pairs={{0,2},{1,3},{2,4},{3,5},{4,6},{5,7},{6,0},{7,1},{8,10},{9,11},{10,... | collective-permute-start | bytes 442376 | tf_op jit(solution)/shard_map/ppermute | solution.py:213
  28.4 7.9 %collective-permute-start.3 = (bf16[8,16,576]{2,1,0:T(8,128)(2,1)S(1)}, bf16[8,16,576]{2,1,0:T(8,128)(2,1)S(1)}, u32[]{:S(2)}, u32[]{:S(2)}) collective-permute-start(bf16[8,16,576]{2,1,0:T(8,128)(2,1)S(1)} %all-to-all-done.1.refs_0_), channel_id=1, source_target_pairs={{0,1},{1,0},{2,3},{3,2},{4,5},{5,4},{6,7},{7,6},{8,9},{9,8},{10,11... | collective-permute-start | bytes 442376 | tf_op jit(solution)/shard_map/ppermute | solution.py:255
  32.6 3.7 %collective-permute-start.6 = (bf16[8,16,576]{2,1,0:T(8,128)(2,1)S(1)}, bf16[8,16,576]{2,1,0:T(8,128)(2,1)S(1)}, u32[]{:S(2)}, u32[]{:S(2)}) collective-permute-start(bf16[8,16,576]{2,1,0:T(8,128)(2,1)S(1)} %collective-permute-done.2.refs_3_), channel_id=1, source_target_pairs={{0,1},{1,0},{2,3},{3,2},{4,5},{5,4},{6,7},{7,6},{8,9},{9,8},{10,11... | collective-permute-start | bytes 442376 | tf_op jit(solution)/shard_map/ppermute | solution.py:255
  34.6 1.7 %collective-permute-start.5 = (bf16[8,16,576]{2,1,0:T(8,128)(2,1)S(1)}, bf16[8,16,576]{2,1,0:T(8,128)(2,1)S(1)}, u32[]{:S(2)}, u32[]{:S(2)}) collective-permute-start(bf16[8,16,576]{2,1,0:T(8,128)(2,1)S(1)} %collective-permute-done.1.refs_2_), channel_id=1, source_target_pairs={{0,1},{1,0},{2,3},{3,2},{4,5},{5,4},{6,7},{7,6},{8,9},{9,8},{10,11... | collective-permute-start | bytes 442376 | tf_op jit(solution)/shard_map/ppermute | solution.py:255
  36.2 1.4 %collective-permute-start.4 = (bf16[8,16,576]{2,1,0:T(8,128)(2,1)S(1)}, bf16[8,16,576]{2,1,0:T(8,128)(2,1)S(1)}, u32[]{:S(2)}, u32[]{:S(2)}) collective-permute-start(bf16[8,16,576]{2,1,0:T(8,128)(2,1)S(1)} %collective-permute-done.refs_1_), channel_id=1, source_target_pairs={{0,1},{1,0},{2,3},{3,2},{4,5},{5,4},{6,7},{7,6},{8,9},{9,8},{10,11... | collective-permute-start | bytes 442376 | tf_op jit(solution)/shard_map/ppermute | solution.py:255
  47.8 9.0 %collective-permute-start.10 = (bf16[4,8,80,128]{3,2,1,0:T(8,128)(2,1)S(1)}, bf16[4,8,80,128]{3,2,1,0:T(8,128)(2,1)S(1)}, u32[]{:S(2)}, u32[]{:S(2)}) collective-permute-start(bf16[4,8,80,128]{3,2,1,0:T(8,128)(2,1)S(1)} %get-tuple-element.41), channel_id=1, source_target_pairs={{0,1},{1,0},{2,3},{3,2},{4,5},{5,4},{6,7},{7,6},{8,9},{9,8},{10,11... | collective-permute-start | bytes 1966088 | tf_op jit(solution)/shard_map/ppermute | solution.py:295
  47.9 5.9 %collective-permute-start.7 = (bf16[128,256]{1,0:T(8,128)(2,1)S(1)}, bf16[128,256]{1,0:T(8,128)(2,1)S(1)}, u32[]{:S(2)}, u32[]{:S(2)}) collective-permute-start(bf16[128,256]{1,0:T(8,128)(2,1)S(1)} %get-tuple-element.38), channel_id=1, source_target_pairs={{0,64},{64,128},{128,192},{192,0},{1,65},{65,129},{129,193},{193,1... | collective-permute-start | bytes 196616 | tf_op jit(solution)/shard_map/ppermute | solution.py:213
  49.6 6.7 %collective-permute-start.8 = (bf16[128,256]{1,0:T(8,128)(2,1)S(1)}, bf16[128,256]{1,0:T(8,128)(2,1)S(1)}, u32[]{:S(2)}, u32[]{:S(2)}) collective-permute-start(bf16[128,256]{1,0:T(8,128)(2,1)S(1)} %get-tuple-element.39), channel_id=1, source_target_pairs={{0,128},{64,192},{128,0},{192,64},{1,129},{65,193},{129,1},{193,65... | collective-permute-start | bytes 196616 | tf_op jit(solution)/shard_map/ppermute | solution.py:213
  52.5 4.3 %collective-permute-start.9 = (bf16[128,256]{1,0:T(8,128)(2,1)S(1)}, bf16[128,256]{1,0:T(8,128)(2,1)S(1)}, u32[]{:S(2)}, u32[]{:S(2)}) collective-permute-start(bf16[128,256]{1,0:T(8,128)(2,1)S(1)} %get-tuple-element.40), channel_id=1, source_target_pairs={{0,192},{64,0},{128,64},{192,128},{1,193},{65,1},{129,65},{193,129... | collective-permute-start | bytes 196616 | tf_op jit(solution)/shard_map/ppermute | solution.py:213
  57.6 20.6 %all-to-all-start.2 = ((bf16[8,128,256]{2,1,0:T(8,128)(2,1)}), bf16[8,128,256]{2,1,0:T(8,128)(2,1)S(1)}, u32[]{:S(2)}, u32[]{:S(2)}) async-start(bf16[8,128,256]{2,1,0:T(8,128)(2,1)} %broadcast_in_dim.21), calls=%async_computation.2 | async-start | bytes 1048576 | tf_op jit(solution)/shard_map/all_to_all | solution.py:304
  62.6 8.0 %collective-permute-start.11 = (bf16[8,80,128]{2,1,0:T(8,128)(2,1)S(1)}, bf16[8,80,128]{2,1,0:T(8,128)(2,1)S(1)}, u32[]{:S(2)}, u32[]{:S(2)}) collective-permute-start(bf16[8,80,128]{2,1,0:T(8,128)(2,1)S(1)} %get-tuple-element.46), channel_id=1, source_target_pairs={{0,2},{1,3},{2,4},{3,5},{4,6},{5,7},{6,0},{7,1},{8,10},{9,11},{10,... | collective-permute-start | bytes 491528 | tf_op jit(solution)/shard_map/ppermute | solution.py:308
  64.2 9.2 %collective-permute-start.12 = (bf16[8,80,128]{2,1,0:T(8,128)(2,1)S(1)}, bf16[8,80,128]{2,1,0:T(8,128)(2,1)S(1)}, u32[]{:S(2)}, u32[]{:S(2)}) collective-permute-start(bf16[8,80,128]{2,1,0:T(8,128)(2,1)S(1)} %get-tuple-element.47), channel_id=1, source_target_pairs={{0,4},{1,5},{2,6},{3,7},{4,0},{5,1},{6,2},{7,3},{8,12},{9,13},{10,... | collective-permute-start | bytes 491528 | tf_op jit(solution)/shard_map/ppermute | solution.py:308
  66.9 6.5 %collective-permute-start.13 = (bf16[8,80,128]{2,1,0:T(8,128)(2,1)S(1)}, bf16[8,80,128]{2,1,0:T(8,128)(2,1)S(1)}, u32[]{:S(2)}, u32[]{:S(2)}) collective-permute-start(bf16[8,80,128]{2,1,0:T(8,128)(2,1)S(1)} %get-tuple-element.48), channel_id=1, source_target_pairs={{0,6},{1,7},{2,0},{3,1},{4,2},{5,3},{6,4},{7,5},{8,14},{9,15},{10,... | collective-permute-start | bytes 491528 | tf_op jit(solution)/shard_map/ppermute | solution.py:308
  79.1 22.3 %all-to-all-start.3 = ((bf16[8,272,128]{2,1,0:T(8,128)(2,1)}), bf16[8,272,128]{2,1,0:T(8,128)(2,1)S(1)}, u32[]{:S(2)}, u32[]{:S(2)}) async-start(bf16[8,272,128]{2,1,0:T(8,128)(2,1)} %combine.1), calls=%async_computation.3 | async-start | bytes 1114112 | tf_op jit(solution)/shard_map/all_to_all | solution.py:325
  84.0 12.3 %collective-permute-start.16 = (bf16[8,128,256]{2,1,0:T(8,128)(2,1)S(1)}, bf16[8,128,256]{2,1,0:T(8,128)(2,1)S(1)}, u32[]{:S(2)}, u32[]{:S(2)}) collective-permute-start(bf16[8,128,256]{2,1,0:T(8,128)(2,1)S(1)} %all-to-all-done.2.refs_0_), channel_id=1, source_target_pairs={{0,192},{64,0},{128,64},{192,128},{1,193},{65,1},{129,65},{193,129... | collective-permute-start | bytes 1572872 | tf_op jit(solution)/shard_map/ppermute | solution.py:213
  86.1 12.9 %collective-permute-start.14 = (bf16[8,128,256]{2,1,0:T(8,128)(2,1)S(1)}, bf16[8,128,256]{2,1,0:T(8,128)(2,1)S(1)}, u32[]{:S(2)}, u32[]{:S(2)}) collective-permute-start(bf16[8,128,256]{2,1,0:T(8,128)(2,1)S(1)} %all-to-all-done.2.refs_0_), channel_id=1, source_target_pairs={{0,64},{64,128},{128,192},{192,0},{1,65},{65,129},{129,193},{193,1... | collective-permute-start | bytes 1572872 | tf_op jit(solution)/shard_map/ppermute | solution.py:213
  96.3 6.5 %collective-permute-start.17 = (bf16[4,128,256]{2,1,0:T(8,128)(2,1)S(1)}, bf16[4,128,256]{2,1,0:T(8,128)(2,1)S(1)}, u32[]{:S(2)}, u32[]{:S(2)}) collective-permute-start(bf16[4,128,256]{2,1,0:T(8,128)(2,1)S(1)} %slice.9), channel_id=1, source_target_pairs={{0,192},{64,0},{128,64},{192,128},{1,193},{65,1},{129,65},{193,129... | collective-permute-start | bytes 786440 | tf_op jit(solution)/shard_map/ppermute | solution.py:213
  99.0 7.7 %collective-permute-start.15 = (bf16[4,128,256]{2,1,0:T(8,128)(2,1)S(1)}, bf16[4,128,256]{2,1,0:T(8,128)(2,1)S(1)}, u32[]{:S(2)}, u32[]{:S(2)}) collective-permute-start(bf16[4,128,256]{2,1,0:T(8,128)(2,1)S(1)} %slice.8), channel_id=1, source_target_pairs={{0,64},{64,128},{128,192},{192,0},{1,65},{65,129},{129,193},{193,1... | collective-permute-start | bytes 786440 | tf_op jit(solution)/shard_map/ppermute | solution.py:213

commit v6 on v5

--- a/solution.py
+++ b/solution.py
@@ -308,7 +308,6 @@
         lax.ppermute(folded[i], "head", [(j, (j + 2 * i) % n_head) for j in range(n_head)])
         for i in range(1, n_head // 2)
     ]
-    gw_ctx, *gl_moved = lax.optimization_barrier((gw_ctx, *gl_moved))
     half = n_ctx // 2
     before, after = shifted(gw_ctx, "dp", n_dp, 1), shifted(gw_ctx, "dp", n_dp, n_dp - 1)
     opposite = [

time: 109 us -> 108 us (level)
  transfers between devices with their start and end apart: 22 -> 22, of which waited for: 14 -> 14; matrix products, arithmetic and copies ran while one was open for 0% -> 0% of each run, Pallas kernels for 5% -> 6%
where the time goes in v6:
time: 108 us; the launch traced here: 107 us
  starting transfers between devices  44.3 us (41%)
  waiting for transfers between devices  42.4 us (39%)
  Pallas kernels  13.2 us (12%)
  local copies, waits for them, and re-layouts  6.67 us (6%)
    ppermute x10, waiting for transfers between devices, shifted(): return lax.ppermute(x, axis, [(i, (i + shift) % n) for i in range(n)])  24.4 us
    ppermute x10, starting transfers between devices, shifted(): return lax.ppermute(x, axis, [(i, (i + shift) % n) for i in range(n)])  15.1 us
    pallas_call x7, Pallas kernels, call(): pl.pallas_call(kernel, grid_spec=pltpu.PrefetchScalarGridSpec(num_scalar_...  13.2 us
    all_to_all x1, starting transfers between devices, on_device(): lax.all_to_all(jnp.broadcast_to(latent, (n_ctx, SUB, LAT + ROPE)), 'ctx',...  8.57 us
    ppermute x3, starting transfers between devices, on_device(): lax.ppermute(folded[i], 'head', [(j, (j + 2 * i) % n_head) for j in range...  5.73 us
    ppermute x3, waiting for transfers between devices, on_device(): lax.ppermute(folded[i], 'head', [(j, (j + 2 * i) % n_head) for j in range...  5.07 us
    all_to_all x1, starting transfers between devices, on_device(): mine = lax.all_to_all(packed, 'ctx', 0, 0, tiled=True)  5.01 us
    all_to_all x1, starting transfers between devices, on_device(): back = lax.all_to_all(back, 'ctx', 0, 0, tiled=True)  4.89 us
  transfers between devices with their start and end apart: 22, of which 14 were waited for; matrix products, arithmetic and copies ran while one was open for 0% of the time, Pallas kernels for 6%

profile of v6, /device:TPU:32, one launch (start us, length us, event | category | flops | bytes accessed | tf_op | source)
XLA Modules:
  0.0 107.5 jit_solution(2235941044608277109)
XLA Ops:
  0.6 1.4 %broadcast_in_dim.20 = bf16[8,16,576]{2,1,0:T(8,128)(2,1)} broadcast(bf16[16,576]{1,0:T(8,128)(2,1)} %bitcast.10), dimensions={1,2} | broadcast | bytes 165888 | tf_op jit(solution)/shard_map/broadcast_in_dim | solution.py:251
  2.0 8.6 %all-to-all-start.1 = ((bf16[8,16,576]{2,1,0:T(8,128)(2,1)}), bf16[8,16,576]{2,1,0:T(8,128)(2,1)S(1)}, u32[]{:S(2)}, u32[]{:S(2)}) async-start(bf16[8,16,576]{2,1,0:T(8,128)(2,1)} %broadcast_in_dim.20), calls=%async_computation.1 | async-start | bytes 327680 | tf_op jit(solution)/shard_map/all_to_all | solution.py:250
  10.7 1.2 %copy-done = bf16[512,1024]{1,0:T(8,128)(2,1)S(1)} copy-done((bf16[512,1024]{1,0:T(8,128)(2,1)S(1)}, bf16[512,1024]{1,0:T(8,128)(2,1)}, u32[]{:S(2)}) %copy-start) | copy-done | bytes 1048600
  11.9 1.2 %copy-done.1 = bf16[512,1024]{1,0:T(8,128)(2,1)S(1)} copy-done((bf16[512,1024]{1,0:T(8,128)(2,1)S(1)}, bf16[512,1024]{1,0:T(8,128)(2,1)}, u32[]{:S(2)}) %copy-start.1) | copy-done | bytes 1048600
  15.1 1.6 %pack.1 = (bf16[8,320,128]{2,1,0:T(8,128)(2,1)}, bf16[512,256]{1,0:T(8,128)(2,1)S(1)}) custom-call(s32[3]{0:T(128)S(1)} %pad_add_fusion.rank_ref, bf16[128,1536]{1,0:T(8,128)(2,1)S(1)} %bitcast.8, bf16[128,1024]{1,0:T(8,128)(2,1)S(1)} %bitcast.9, bf16[512,1024]{1,0:T(8,128)(2,1)S(1)} %copy-done, bf16[512,1024]{1,0:T(8,128)(2,1)S(1)} %copy-done.1), custom_call_target="tpu_custom_call" | custom-call | bytes 3670016 | tf_op jit(solution)/shard_map/pack/pallas_call | solution.py:227
  16.7 2.2 %all-to-all-done.1.refs_0_ = bf16[8,16,576]{2,1,0:T(8,128)(2,1)S(1)} async-done(((bf16[8,16,576]{2,1,0:T(8,128)(2,1)}), bf16[8,16,576]{2,1,0:T(8,128)(2,1)S(1)}, u32[]{:S(2)}, u32[]{:S(2)}) %all-to-all-start.1) | async-done | bytes 147488 | tf_op jit(solution)/shard_map/all_to_all | solution.py:250
  18.9 5.0 %all-to-all-start = ((bf16[8,320,128]{2,1,0:T(8,128)(2,1)}), bf16[8,320,128]{2,1,0:T(8,128)(2,1)S(1)}, u32[]{:S(2)}, u32[]{:S(2)}) async-start(bf16[8,320,128]{2,1,0:T(8,128)(2,1)} %get-tuple-element.29), calls=%async_computation | async-start | bytes 1310720 | tf_op jit(solution)/shard_map/all_to_all | solution.py:265
  23.9 2.8 %collective-permute-start.2 = (bf16[8,16,576]{2,1,0:T(8,128)(2,1)S(1)}, bf16[8,16,576]{2,1,0:T(8,128)(2,1)S(1)}, u32[]{:S(2)}, u32[]{:S(2)}) collective-permute-start(bf16[8,16,576]{2,1,0:T(8,128)(2,1)S(1)} %all-to-all-done.1.refs_0_), channel_id=1, source_target_pairs={{0,6},{1,7},{2,0},{3,1},{4,2},{5,3},{6,4},{7,5},{8,14},{9,15},{10,... | collective-permute-start | bytes 442376 | tf_op jit(solution)/shard_map/ppermute | solution.py:213
  28.4 4.2 %collective-permute-done.2.refs_3_ = bf16[8,16,576]{2,1,0:T(8,128)(2,1)S(1)} collective-permute-done((bf16[8,16,576]{2,1,0:T(8,128)(2,1)S(1)}, bf16[8,16,576]{2,1,0:T(8,128)(2,1)S(1)}, u32[]{:S(2)}, u32[]{:S(2)}) %collective-permute-start.2) | collective-permute-done | bytes 147488 | tf_op jit(solution)/shard_map/ppermute | solution.py:213
  32.6 2.0 %collective-permute-done.1.refs_2_ = bf16[8,16,576]{2,1,0:T(8,128)(2,1)S(1)} collective-permute-done((bf16[8,16,576]{2,1,0:T(8,128)(2,1)S(1)}, bf16[8,16,576]{2,1,0:T(8,128)(2,1)S(1)}, u32[]{:S(2)}, u32[]{:S(2)}) %collective-permute-start.1) | collective-permute-done | bytes 147488 | tf_op jit(solution)/shard_map/ppermute | solution.py:213
  34.6 1.7 %collective-permute-done.refs_1_ = bf16[8,16,576]{2,1,0:T(8,128)(2,1)S(1)} collective-permute-done((bf16[8,16,576]{2,1,0:T(8,128)(2,1)S(1)}, bf16[8,16,576]{2,1,0:T(8,128)(2,1)S(1)}, u32[]{:S(2)}, u32[]{:S(2)}) %collective-permute-start) | collective-permute-done | bytes 147488 | tf_op jit(solution)/shard_map/ppermute | solution.py:213
  36.3 1.4 %collective-permute-done.4.refs_5_ = bf16[8,16,576]{2,1,0:T(8,128)(2,1)S(1)} collective-permute-done((bf16[8,16,576]{2,1,0:T(8,128)(2,1)S(1)}, bf16[8,16,576]{2,1,0:T(8,128)(2,1)S(1)}, u32[]{:S(2)}, u32[]{:S(2)}) %collective-permute-start.4) | collective-permute-done | bytes 147488 | tf_op jit(solution)/shard_map/ppermute | solution.py:255
  37.6 4.6 %all-to-all-done.in_ref = bf16[8,320,128]{2,1,0:T(8,128)(2,1)S(1)} async-done(((bf16[8,320,128]{2,1,0:T(8,128)(2,1)}), bf16[8,320,128]{2,1,0:T(8,128)(2,1)S(1)}, u32[]{:S(2)}, u32[]{:S(2)}) %all-to-all-start) | async-done | bytes 655392 | tf_op jit(solution)/shard_map/all_to_all | solution.py:265
  42.2 5.6 %attention_backward.1 = (bf16[4,8,80,128]{3,2,1,0:T(8,128)(2,1)S(1)}, bf16[4,8,80,128]{3,2,1,0:T(8,128)(2,1)S(1)}, bf16[128,256]{1,0:T(8,128)(2,1)S(1)}, bf16[12...) custom-call(s32[16]{0:T(128)S(1)} %copy-done.4, ...), custom_call_target="tpu_custom_call" | custom-call | flops 3000000000 | bytes 4063232 | tf_op jit(solution)/shard_map/attention_backward/pallas_call | solution.py:227
  47.9 1.7 %collective-permute-start.7 = (bf16[128,256]{1,0:T(8,128)(2,1)S(1)}, bf16[128,256]{1,0:T(8,128)(2,1)S(1)}, u32[]{:S(2)}, u32[]{:S(2)}) collective-permute-start(bf16[128,256]{1,0:T(8,128)(2,1)S(1)} %get-tuple-element.34), channel_id=1, source_target_pairs={{0,64},{64,128},{128,192},{192,0},{1,65},{65,129},{129,193},{193,1... | collective-permute-start | bytes 196616 | tf_op jit(solution)/shard_map/ppermute | solution.py:213
  49.6 2.9 %collective-permute-start.8 = (bf16[128,256]{1,0:T(8,128)(2,1)S(1)}, bf16[128,256]{1,0:T(8,128)(2,1)S(1)}, u32[]{:S(2)}, u32[]{:S(2)}) collective-permute-start(bf16[128,256]{1,0:T(8,128)(2,1)S(1)} %get-tuple-element.35), channel_id=1, source_target_pairs={{0,128},{64,192},{128,0},{192,64},{1,129},{65,193},{129,1},{193,65... | collective-permute-start | bytes 196616 | tf_op jit(solution)/shard_map/ppermute | solution.py:213
  52.5 1.3 %collective-permute-start.9 = (bf16[128,256]{1,0:T(8,128)(2,1)S(1)}, bf16[128,256]{1,0:T(8,128)(2,1)S(1)}, u32[]{:S(2)}, u32[]{:S(2)}) collective-permute-start(bf16[128,256]{1,0:T(8,128)(2,1)S(1)} %get-tuple-element.36), channel_id=1, source_target_pairs={{0,192},{64,0},{128,64},{192,128},{1,193},{65,1},{129,65},{193,129... | collective-permute-start | bytes 196616 | tf_op jit(solution)/shard_map/ppermute | solution.py:213
  53.8 2.5 %collective-permute-done.8 = bf16[128,256]{1,0:T(8,128)(2,1)S(1)} collective-permute-done((bf16[128,256]{1,0:T(8,128)(2,1)S(1)}, bf16[128,256]{1,0:T(8,128)(2,1)S(1)}, u32[]{:S(2)}, u32[]{:S(2)}) %collective-permute-start.8) | collective-permute-done | bytes 65568 | tf_op jit(solution)/shard_map/ppermute | solution.py:213
  57.6 4.9 %all-to-all-start.3 = ((bf16[8,128,256]{2,1,0:T(8,128)(2,1)}), bf16[8,128,256]{2,1,0:T(8,128)(2,1)S(1)}, u32[]{:S(2)}, u32[]{:S(2)}) async-start(bf16[8,128,256]{2,1,0:T(8,128)(2,1)} %broadcast_in_dim.21), calls=%async_computation.3 | async-start | bytes 1048576 | tf_op jit(solution)/shard_map/all_to_all | solution.py:304
  62.6 1.6 %collective-permute-start.11 = (bf16[8,80,128]{2,1,0:T(8,128)(2,1)S(1)}, bf16[8,80,128]{2,1,0:T(8,128)(2,1)S(1)}, u32[]{:S(2)}, u32[]{:S(2)}) collective-permute-start(bf16[8,80,128]{2,1,0:T(8,128)(2,1)S(1)} %get-tuple-element.40), channel_id=1, source_target_pairs={{0,2},{1,3},{2,4},{3,5},{4,6},{5,7},{6,0},{7,1},{8,10},{9,11},{10,... | collective-permute-start | bytes 491528 | tf_op jit(solution)/shard_map/ppermute | solution.py:308
  64.2 2.7 %collective-permute-start.12 = (bf16[8,80,128]{2,1,0:T(8,128)(2,1)S(1)}, bf16[8,80,128]{2,1,0:T(8,128)(2,1)S(1)}, u32[]{:S(2)}, u32[]{:S(2)}) collective-permute-start(bf16[8,80,128]{2,1,0:T(8,128)(2,1)S(1)} %get-tuple-element.41), channel_id=1, source_target_pairs={{0,4},{1,5},{2,6},{3,7},{4,0},{5,1},{6,2},{7,3},{8,12},{9,13},{10,... | collective-permute-start | bytes 491528 | tf_op jit(solution)/shard_map/ppermute | solution.py:308
  66.9 1.4 %collective-permute-start.13 = (bf16[8,80,128]{2,1,0:T(8,128)(2,1)S(1)}, bf16[8,80,128]{2,1,0:T(8,128)(2,1)S(1)}, u32[]{:S(2)}, u32[]{:S(2)}) collective-permute-start(bf16[8,80,128]{2,1,0:T(8,128)(2,1)S(1)} %get-tuple-element.42), channel_id=1, source_target_pairs={{0,6},{1,7},{2,0},{3,1},{4,2},{5,3},{6,4},{7,5},{8,14},{9,15},{10,... | collective-permute-start | bytes 491528 | tf_op jit(solution)/shard_map/ppermute | solution.py:308
  68.4 2.3 %collective-permute-done.11.refs_1_ = bf16[8,80,128]{2,1,0:T(8,128)(2,1)S(1)} collective-permute-done((bf16[8,80,128]{2,1,0:T(8,128)(2,1)S(1)}, bf16[8,80,128]{2,1,0:T(8,128)(2,1)S(1)}, u32[]{:S(2)}, u32[]{:S(2)}) %collective-permute-start.11) | collective-permute-done | bytes 163872 | tf_op jit(solution)/shard_map/ppermute | solution.py:308
  70.7 2.8 %collective-permute-done.12.refs_2_ = bf16[8,80,128]{2,1,0:T(8,128)(2,1)S(1)} collective-permute-done((bf16[8,80,128]{2,1,0:T(8,128)(2,1)S(1)}, bf16[8,80,128]{2,1,0:T(8,128)(2,1)S(1)}, u32[]{:S(2)}, u32[]{:S(2)}) %collective-permute-start.12) | collective-permute-done | bytes 163872 | tf_op jit(solution)/shard_map/ppermute | solution.py:308
  74.3 3.8 %all-to-all-done.3.refs_0_ = bf16[8,128,256]{2,1,0:T(8,128)(2,1)S(1)} async-done(((bf16[8,128,256]{2,1,0:T(8,128)(2,1)}), bf16[8,128,256]{2,1,0:T(8,128)(2,1)S(1)}, u32[]{:S(2)}, u32[]{:S(2)}) %all-to-all-start.3) | async-done | bytes 524320 | tf_op jit(solution)/shard_map/all_to_all | solution.py:304
  78.2 4.9 %all-to-all-start.2 = ((bf16[8,272,128]{2,1,0:T(8,128)(2,1)}), bf16[8,272,128]{2,1,0:T(8,128)(2,1)S(1)}, u32[]{:S(2)}, u32[]{:S(2)}) async-start(bf16[8,272,128]{2,1,0:T(8,128)(2,1)} %combine.1), calls=%async_computation.2 | async-start | bytes 1114112 | tf_op jit(solution)/shard_map/all_to_all | solution.py:324
  83.1 2.1 %collective-permute-start.16 = (bf16[8,128,256]{2,1,0:T(8,128)(2,1)S(1)}, bf16[8,128,256]{2,1,0:T(8,128)(2,1)S(1)}, u32[]{:S(2)}, u32[]{:S(2)}) collective-permute-start(bf16[8,128,256]{2,1,0:T(8,128)(2,1)S(1)} %all-to-all-done.3.refs_0_), channel_id=1, source_target_pairs={{0,192},{64,0},{128,64},{192,128},{1,193},{65,1},{129,65},{193,129... | collective-permute-start | bytes 1572872 | tf_op jit(solution)/shard_map/ppermute | solution.py:213
  85.2 10.2 %collective-permute-done.16.refs_2_ = bf16[8,128,256]{2,1,0:T(8,128)(2,1)S(1)} collective-permute-done((bf16[8,128,256]{2,1,0:T(8,128)(2,1)S(1)}, bf16[8,128,256]{2,1,0:T(8,128)(2,1)S(1)}, u32[]{:S(2)}, u32[]{:S(2)}) %collective-permute-start.16) | collective-permute-done | bytes 524320 | tf_op jit(solution)/shard_map/ppermute | solution.py:213
  95.4 2.6 %collective-permute-start.17 = (bf16[4,128,256]{2,1,0:T(8,128)(2,1)S(1)}, bf16[4,128,256]{2,1,0:T(8,128)(2,1)S(1)}, u32[]{:S(2)}, u32[]{:S(2)}) collective-permute-start(bf16[4,128,256]{2,1,0:T(8,128)(2,1)S(1)} %slice.9), channel_id=1, source_target_pairs={{0,192},{64,0},{128,64},{192,128},{1,193},{65,1},{129,65},{193,129... | collective-permute-start | bytes 786440 | tf_op jit(solution)/shard_map/ppermute | solution.py:213
  100.0 2.3 %assemble_near.1 = (f32[512,1024]{1,0:T(8,128)}, f32[512,1024]{1,0:T(8,128)}) custom-call(s32[3]{0:T(128)S(1)} %pad_add_fusion.rank_ref, bf16[8,128,256]{2,1,0:T(8,128)(2,1)S(1)} %all-to-all-done.3.refs_0_, bf16[8,128,256]{2,1,0:T(8,128)(2,1)S(1)} %collective-permute-done.14.refs_1_, bf16[8,128,256]{2,1,0:T(8,128)(2,1)S(1)} %collective-permute-done.16.refs_2_), custom_call_target="tpu_custom_call" | custom-call | bytes 5767168 | tf_op jit(solution)/shard_map/assemble_near/pallas_call | solution.py:227
  102.4 3.4 %collective-permute-done.15.refs_0_ = bf16[4,128,256]{2,1,0:T(8,128)(2,1)S(1)} collective-permute-done((bf16[4,128,256]{2,1,0:T(8,128)(2,1)S(1)}, bf16[4,128,256]{2,1,0:T(8,128)(2,1)S(1)}, u32[]{:S(2)}, u32[]{:S(2)}) %collective-permute-start.15) | collective-permute-done | bytes 262176 | tf_op jit(solution)/shard_map/ppermute | solution.py:213
  105.7 1.6 %assemble_far.1 = (f32[512,1024]{1,0:T(8,128)}, f32[512,1024]{1,0:T(8,128)}) custom-call(s32[3]{0:T(128)S(1)} %pad_add_fusion.rank_ref, bf16[4,128,256]{2,1,0:T(8,128)(2,1)S(1)} %collective-permute-done.15.refs_0_, bf16[4,128,256]{2,1,0:T(8,128)(2,1)S(1)} %collective-permute-done.17.refs_1_, ...), custom_call_target="tpu_custom_call", output_to_operand_aliasing={{0}: (3, {}), {1}: (4, {})} | custom-call | bytes 8912896 | tf_op jit(solution)/shard_map/assemble_far/pallas_call | solution.py:227
  (35 shorter events, 8.2 us)
Async XLA Ops:
  2.0 16.9 %all-to-all-start.1 = ((bf16[8,16,576]{2,1,0:T(8,128)(2,1)}), bf16[8,16,576]{2,1,0:T(8,128)(2,1)S(1)}, u32[]{:S(2)}, u32[]{:S(2)}) async-start(bf16[8,16,576]{2,1,0:T(8,128)(2,1)} %broadcast_in_dim.20), calls=%async_computation.1 | async-start | bytes 327680 | tf_op jit(solution)/shard_map/all_to_all | solution.py:250
  10.6 31.6 %copy-start.4 = (s32[16]{0:T(128)S(1)}, s32[16]{0:T(128)}, u32[]{:S(2)}) copy-start(s32[16]{0:T(128)} %order_ref.1) | copy-start | bytes 196
  10.7 1.2 %copy-start = (bf16[512,1024]{1,0:T(8,128)(2,1)S(1)}, bf16[512,1024]{1,0:T(8,128)(2,1)}, u32[]{:S(2)}) copy-start(bf16[512,1024]{1,0:T(8,128)(2,1)} %wk_ref.1) | copy-start | bytes 3145732
  11.9 1.2 %copy-start.1 = (bf16[512,1024]{1,0:T(8,128)(2,1)S(1)}, bf16[512,1024]{1,0:T(8,128)(2,1)}, u32[]{:S(2)}) copy-start(bf16[512,1024]{1,0:T(8,128)(2,1)} %wv_ref.1) | copy-start | bytes 3145732
  13.1 1.0 copy-start.2
  14.1 0.9 copy-start.3
  18.9 23.3 %all-to-all-start = ((bf16[8,320,128]{2,1,0:T(8,128)(2,1)}), bf16[8,320,128]{2,1,0:T(8,128)(2,1)S(1)}, u32[]{:S(2)}, u32[]{:S(2)}) async-start(bf16[8,320,128]{2,1,0:T(8,128)(2,1)} %get-tuple-element.29), calls=%async_computation | async-start | bytes 1310720 | tf_op jit(solution)/shard_map/all_to_all | solution.py:265
  23.9 8.6 %collective-permute-start.2 = (bf16[8,16,576]{2,1,0:T(8,128)(2,1)S(1)}, bf16[8,16,576]{2,1,0:T(8,128)(2,1)S(1)}, u32[]{:S(2)}, u32[]{:S(2)}) collective-permute-start(bf16[8,16,576]{2,1,0:T(8,128)(2,1)S(1)} %all-to-all-done.1.refs_0_), channel_id=1, source_target_pairs={{0,6},{1,7},{2,0},{3,1},{4,2},{5,3},{6,4},{7,5},{8,14},{9,15},{10,... | collective-permute-start | bytes 442376 | tf_op jit(solution)/shard_map/ppermute | solution.py:213
  26.7 7.9 %collective-permute-start.1 = (bf16[8,16,576]{2,1,0:T(8,128)(2,1)S(1)}, bf16[8,16,576]{2,1,0:T(8,128)(2,1)S(1)}, u32[]{:S(2)}, u32[]{:S(2)}) collective-permute-start(bf16[8,16,576]{2,1,0:T(8,128)(2,1)S(1)} %all-to-all-done.1.refs_0_), channel_id=1, source_target_pairs={{0,4},{1,5},{2,6},{3,7},{4,0},{5,1},{6,2},{7,3},{8,12},{9,13},{10,... | collective-permute-start | bytes 442376 | tf_op jit(solution)/shard_map/ppermute | solution.py:213
  27.5 8.8 %collective-permute-start = (bf16[8,16,576]{2,1,0:T(8,128)(2,1)S(1)}, bf16[8,16,576]{2,1,0:T(8,128)(2,1)S(1)}, u32[]{:S(2)}, u32[]{:S(2)}) collective-permute-start(bf16[8,16,576]{2,1,0:T(8,128)(2,1)S(1)} %all-to-all-done.1.refs_0_), channel_id=1, source_target_pairs={{0,2},{1,3},{2,4},{3,5},{4,6},{5,7},{6,0},{7,1},{8,10},{9,11},{10,... | collective-permute-start | bytes 442376 | tf_op jit(solution)/shard_map/ppermute | solution.py:213
  28.4 7.9 %collective-permute-start.3 = (bf16[8,16,576]{2,1,0:T(8,128)(2,1)S(1)}, bf16[8,16,576]{2,1,0:T(8,128)(2,1)S(1)}, u32[]{:S(2)}, u32[]{:S(2)}) collective-permute-start(bf16[8,16,576]{2,1,0:T(8,128)(2,1)S(1)} %all-to-all-done.1.refs_0_), channel_id=1, source_target_pairs={{0,1},{1,0},{2,3},{3,2},{4,5},{5,4},{6,7},{7,6},{8,9},{9,8},{10,11... | collective-permute-start | bytes 442376 | tf_op jit(solution)/shard_map/ppermute | solution.py:255
  32.6 3.7 %collective-permute-start.6 = (bf16[8,16,576]{2,1,0:T(8,128)(2,1)S(1)}, bf16[8,16,576]{2,1,0:T(8,128)(2,1)S(1)}, u32[]{:S(2)}, u32[]{:S(2)}) collective-permute-start(bf16[8,16,576]{2,1,0:T(8,128)(2,1)S(1)} %collective-permute-done.2.refs_3_), channel_id=1, source_target_pairs={{0,1},{1,0},{2,3},{3,2},{4,5},{5,4},{6,7},{7,6},{8,9},{9,8},{10,11... | collective-permute-start | bytes 442376 | tf_op jit(solution)/shard_map/ppermute | solution.py:255
  34.6 1.7 %collective-permute-start.5 = (bf16[8,16,576]{2,1,0:T(8,128)(2,1)S(1)}, bf16[8,16,576]{2,1,0:T(8,128)(2,1)S(1)}, u32[]{:S(2)}, u32[]{:S(2)}) collective-permute-start(bf16[8,16,576]{2,1,0:T(8,128)(2,1)S(1)} %collective-permute-done.1.refs_2_), channel_id=1, source_target_pairs={{0,1},{1,0},{2,3},{3,2},{4,5},{5,4},{6,7},{7,6},{8,9},{9,8},{10,11... | collective-permute-start | bytes 442376 | tf_op jit(solution)/shard_map/ppermute | solution.py:255
  36.2 1.4 %collective-permute-start.4 = (bf16[8,16,576]{2,1,0:T(8,128)(2,1)S(1)}, bf16[8,16,576]{2,1,0:T(8,128)(2,1)S(1)}, u32[]{:S(2)}, u32[]{:S(2)}) collective-permute-start(bf16[8,16,576]{2,1,0:T(8,128)(2,1)S(1)} %collective-permute-done.refs_1_), channel_id=1, source_target_pairs={{0,1},{1,0},{2,3},{3,2},{4,5},{5,4},{6,7},{7,6},{8,9},{9,8},{10,11... | collective-permute-start | bytes 442376 | tf_op jit(solution)/shard_map/ppermute | solution.py:255
  47.8 9.0 %collective-permute-start.10 = (bf16[4,8,80,128]{3,2,1,0:T(8,128)(2,1)S(1)}, bf16[4,8,80,128]{3,2,1,0:T(8,128)(2,1)S(1)}, u32[]{:S(2)}, u32[]{:S(2)}) collective-permute-start(bf16[4,8,80,128]{3,2,1,0:T(8,128)(2,1)S(1)} %get-tuple-element.37), channel_id=1, source_target_pairs={{0,1},{1,0},{2,3},{3,2},{4,5},{5,4},{6,7},{7,6},{8,9},{9,8},{10,11... | collective-permute-start | bytes 1966088 | tf_op jit(solution)/shard_map/ppermute | solution.py:295
  47.9 5.9 %collective-permute-start.7 = (bf16[128,256]{1,0:T(8,128)(2,1)S(1)}, bf16[128,256]{1,0:T(8,128)(2,1)S(1)}, u32[]{:S(2)}, u32[]{:S(2)}) collective-permute-start(bf16[128,256]{1,0:T(8,128)(2,1)S(1)} %get-tuple-element.34), channel_id=1, source_target_pairs={{0,64},{64,128},{128,192},{192,0},{1,65},{65,129},{129,193},{193,1... | collective-permute-start | bytes 196616 | tf_op jit(solution)/shard_map/ppermute | solution.py:213
  49.6 6.7 %collective-permute-start.8 = (bf16[128,256]{1,0:T(8,128)(2,1)S(1)}, bf16[128,256]{1,0:T(8,128)(2,1)S(1)}, u32[]{:S(2)}, u32[]{:S(2)}) collective-permute-start(bf16[128,256]{1,0:T(8,128)(2,1)S(1)} %get-tuple-element.35), channel_id=1, source_target_pairs={{0,128},{64,192},{128,0},{192,64},{1,129},{65,193},{129,1},{193,65... | collective-permute-start | bytes 196616 | tf_op jit(solution)/shard_map/ppermute | solution.py:213
  52.5 4.3 %collective-permute-start.9 = (bf16[128,256]{1,0:T(8,128)(2,1)S(1)}, bf16[128,256]{1,0:T(8,128)(2,1)S(1)}, u32[]{:S(2)}, u32[]{:S(2)}) collective-permute-start(bf16[128,256]{1,0:T(8,128)(2,1)S(1)} %get-tuple-element.36), channel_id=1, source_target_pairs={{0,192},{64,0},{128,64},{192,128},{1,193},{65,1},{129,65},{193,129... | collective-permute-start | bytes 196616 | tf_op jit(solution)/shard_map/ppermute | solution.py:213
  57.6 20.6 %all-to-all-start.3 = ((bf16[8,128,256]{2,1,0:T(8,128)(2,1)}), bf16[8,128,256]{2,1,0:T(8,128)(2,1)S(1)}, u32[]{:S(2)}, u32[]{:S(2)}) async-start(bf16[8,128,256]{2,1,0:T(8,128)(2,1)} %broadcast_in_dim.21), calls=%async_computation.3 | async-start | bytes 1048576 | tf_op jit(solution)/shard_map/all_to_all | solution.py:304
  62.6 8.0 %collective-permute-start.11 = (bf16[8,80,128]{2,1,0:T(8,128)(2,1)S(1)}, bf16[8,80,128]{2,1,0:T(8,128)(2,1)S(1)}, u32[]{:S(2)}, u32[]{:S(2)}) collective-permute-start(bf16[8,80,128]{2,1,0:T(8,128)(2,1)S(1)} %get-tuple-element.40), channel_id=1, source_target_pairs={{0,2},{1,3},{2,4},{3,5},{4,6},{5,7},{6,0},{7,1},{8,10},{9,11},{10,... | collective-permute-start | bytes 491528 | tf_op jit(solution)/shard_map/ppermute | solution.py:308
  64.2 9.2 %collective-permute-start.12 = (bf16[8,80,128]{2,1,0:T(8,128)(2,1)S(1)}, bf16[8,80,128]{2,1,0:T(8,128)(2,1)S(1)}, u32[]{:S(2)}, u32[]{:S(2)}) collective-permute-start(bf16[8,80,128]{2,1,0:T(8,128)(2,1)S(1)} %get-tuple-element.41), channel_id=1, source_target_pairs={{0,4},{1,5},{2,6},{3,7},{4,0},{5,1},{6,2},{7,3},{8,12},{9,13},{10,... | collective-permute-start | bytes 491528 | tf_op jit(solution)/shard_map/ppermute | solution.py:308
  66.9 6.5 %collective-permute-start.13 = (bf16[8,80,128]{2,1,0:T(8,128)(2,1)S(1)}, bf16[8,80,128]{2,1,0:T(8,128)(2,1)S(1)}, u32[]{:S(2)}, u32[]{:S(2)}) collective-permute-start(bf16[8,80,128]{2,1,0:T(8,128)(2,1)S(1)} %get-tuple-element.42), channel_id=1, source_target_pairs={{0,6},{1,7},{2,0},{3,1},{4,2},{5,3},{6,4},{7,5},{8,14},{9,15},{10,... | collective-permute-start | bytes 491528 | tf_op jit(solution)/shard_map/ppermute | solution.py:308
  78.2 20.9 %all-to-all-start.2 = ((bf16[8,272,128]{2,1,0:T(8,128)(2,1)}), bf16[8,272,128]{2,1,0:T(8,128)(2,1)S(1)}, u32[]{:S(2)}, u32[]{:S(2)}) async-start(bf16[8,272,128]{2,1,0:T(8,128)(2,1)} %combine.1), calls=%async_computation.2 | async-start | bytes 1114112 | tf_op jit(solution)/shard_map/all_to_all | solution.py:324
  83.1 12.3 %collective-permute-start.16 = (bf16[8,128,256]{2,1,0:T(8,128)(2,1)S(1)}, bf16[8,128,256]{2,1,0:T(8,128)(2,1)S(1)}, u32[]{:S(2)}, u32[]{:S(2)}) collective-permute-start(bf16[8,128,256]{2,1,0:T(8,128)(2,1)S(1)} %all-to-all-done.3.refs_0_), channel_id=1, source_target_pairs={{0,192},{64,0},{128,64},{192,128},{1,193},{65,1},{129,65},{193,129... | collective-permute-start | bytes 1572872 | tf_op jit(solution)/shard_map/ppermute | solution.py:213
  85.2 12.9 %collective-permute-start.14 = (bf16[8,128,256]{2,1,0:T(8,128)(2,1)S(1)}, bf16[8,128,256]{2,1,0:T(8,128)(2,1)S(1)}, u32[]{:S(2)}, u32[]{:S(2)}) collective-permute-start(bf16[8,128,256]{2,1,0:T(8,128)(2,1)S(1)} %all-to-all-done.3.refs_0_), channel_id=1, source_target_pairs={{0,64},{64,128},{128,192},{192,0},{1,65},{65,129},{129,193},{193,1... | collective-permute-start | bytes 1572872 | tf_op jit(solution)/shard_map/ppermute | solution.py:213
  95.4 6.9 %collective-permute-start.17 = (bf16[4,128,256]{2,1,0:T(8,128)(2,1)S(1)}, bf16[4,128,256]{2,1,0:T(8,128)(2,1)S(1)}, u32[]{:S(2)}, u32[]{:S(2)}) collective-permute-start(bf16[4,128,256]{2,1,0:T(8,128)(2,1)S(1)} %slice.9), channel_id=1, source_target_pairs={{0,192},{64,0},{128,64},{192,128},{1,193},{65,1},{129,65},{193,129... | collective-permute-start | bytes 786440 | tf_op jit(solution)/shard_map/ppermute | solution.py:213
  98.1 7.7 %collective-permute-start.15 = (bf16[4,128,256]{2,1,0:T(8,128)(2,1)S(1)}, bf16[4,128,256]{2,1,0:T(8,128)(2,1)S(1)}, u32[]{:S(2)}, u32[]{:S(2)}) collective-permute-start(bf16[4,128,256]{2,1,0:T(8,128)(2,1)S(1)} %slice.8), channel_id=1, source_target_pairs={{0,64},{64,128},{128,192},{192,0},{1,65},{65,129},{129,193},{193,1... | collective-permute-start | bytes 786440 | tf_op jit(solution)/shard_map/ppermute | solution.py:213
